TPU v7x, 32 devices: a whole 2x2x4 slice. The times are simulated.
32 devices in a mesh: px: 4 (over z), py: 8 (over y, x, core).
Axes of the slice: x: 2, y: 2, z: 4, core: 2. Of those that a mesh axis runs over, the one named last changes fastest.
Arguments:
- field_in: bfloat16 [32, 8, 512, 512], P(None, 'py', 'px'), may hold values from -6 to 6
- cotangent: bfloat16 [32, 8, 512, 512], P(None, 'py', 'px'), may hold values from -6 to 6
- spectrum_saved: float32 [32, 8, 32, 32, 2], P(None, None, 'px', 'py'), may hold values from -6 to 6
- weight_store: float32 [2048, 2, 32, 32], P(('px', 'py')), may hold values from -4.2 to 4.2
- block_slot: int32 [32, 32], P('py', 'px'), may hold values from 0 to 511, as said below
- kx_modes: int32 [32], replicated, may hold values from 0 to 511, as said below
- ky_modes: int32 [32], replicated, may hold values from 0 to 511, as said below
- pointwise: bfloat16 [32, 32], replicated, may hold values from -0.25 to 0.25
- bias_vector: float32 [32], replicated, may hold values from -3 to 3
Outputs:
- field_grad: float32 [32, 8, 512, 512], P(None, 'py', 'px')
- store_grad: float32 [2048, 2, 32, 32], P(('px', 'py'))
Inputs may be any that keep to these rules, and one draw needn't show every extreme that they name: `kx_modes`: 32 distinct wave numbers k, each with k < 32 or k > 480. `ky_modes`: 32 distinct wave numbers k, each with k < 32 or k > 480. `block_slot`: within each px index's 8 second-dimension modes, the values over all 32 x 8 mode pairs are distinct; v // 64 is the py index of the device that stores the block and v % 64 its slot there; in each such group one py index stores 64 blocks, and the other slots hold unused blocks.
All inputs are finite; a program needn't handle non-finite values.
Results may differ from a plain program's by a relative error of at most 0.0003.
Values sent between devices are 32-bit elements; how exact they have to be, the bound alone decides.
No kernel may reach another device: no remote copies, remote signals or barrier semaphores. Data moves between devices by JAX's collectives and lax.ppermute only.
A program may use at most 128 MiB of HBM per device.

v0:
```python
import functools
import math

import jax
import jax.numpy as jnp
from jax import lax
from jax.experimental import pallas as pl
from jax.experimental.pallas import tpu as pltpu
from jax.sharding import PartitionSpec as P

precise = lax.Precision.HIGHEST


def phase_table(length, modes):
    points = lax.iota(jnp.int32, length)
    wrapped = points[:, None] * modes[None, :] % length
    angle = wrapped.astype(jnp.float32) * (2.0 * math.pi / length)
    return (jnp.cos(angle), jnp.sin(angle))


def gelu_slope(values):
    normal_cdf = 0.5 * (1.0 + lax.erf(values * 0.7071067811865476))
    density = jnp.exp(-0.5 * values * values) * 0.3989422804014327
    return normal_cdf + values * density


def channel_mix(blocks, spectrum):
    block_re = blocks[:, :, 0]
    block_im = blocks[:, :, 1]
    spec_re = spectrum[..., 0]
    spec_im = spectrum[..., 1]
    form = "baoc,czba->ozba"
    out_re = jnp.einsum(form, block_re, spec_re, precision=precise) - jnp.einsum(
        form, block_im, spec_im, precision=precise
    )
    out_im = jnp.einsum(form, block_re, spec_im, precision=precise) + jnp.einsum(
        form, block_im, spec_re, precision=precise
    )
    return jnp.stack([out_re, out_im], -1)


def channel_adjoint(blocks, spectrum):
    block_re = blocks[:, :, 0]
    block_im = blocks[:, :, 1]
    grad_re = spectrum[..., 0]
    grad_im = spectrum[..., 1]
    form = "baoc,ozba->czba"
    out_re = jnp.einsum(form, block_re, grad_re, precision=precise) + jnp.einsum(
        form, block_im, grad_im, precision=precise
    )
    out_im = jnp.einsum(form, block_re, grad_im, precision=precise) - jnp.einsum(
        form, block_im, grad_re, precision=precise
    )
    return jnp.stack([out_re, out_im], -1)


def block_gradient(spectrum_grad, spectrum):
    grad_re = spectrum_grad[..., 0]
    grad_im = spectrum_grad[..., 1]
    spec_re = spectrum[..., 0]
    spec_im = spectrum[..., 1]
    form = "ozba,czba->aboc"
    out_re = jnp.einsum(form, grad_re, spec_re, precision=precise) + jnp.einsum(
        form, grad_im, spec_im, precision=precise
    )
    out_im = jnp.einsum(form, grad_im, spec_re, precision=precise) - jnp.einsum(
        form, grad_re, spec_im, precision=precise
    )
    return jnp.stack([out_re, out_im], 2)


def invert_rows(spectrum, cos_rows, sin_rows):
    spec_re = spectrum[..., 0]
    spec_im = spectrum[..., 1]
    form = "czma,xa->czmx"
    back_re = jnp.einsum(form, spec_re, cos_rows, precision=precise) - jnp.einsum(
        form, spec_im, sin_rows, precision=precise
    )
    back_im = jnp.einsum(form, spec_re, sin_rows, precision=precise) + jnp.einsum(
        form, spec_im, cos_rows, precision=precise
    )
    joined = jnp.stack([back_re, back_im], 3)
    return joined.reshape(joined.shape[0], joined.shape[1], 2 * joined.shape[2], joined.shape[4])


def on_device(
    field_in,
    cotangent,
    spectrum_saved,
    weight_store,
    block_slot,
    kx_modes,
    ky_modes,
    pointwise,
    bias_vector,
):
    channels, planes, rows_x, width_y = field_in.shape
    full_x = rows_x * lax.axis_size("px")
    modes_y = ky_modes.shape[0]
    local_y = modes_y // lax.axis_size("px")
    capacity = weight_store.shape[0]
    factor = 1.0 / math.sqrt(full_x * width_y)
    cos_y, sin_y = phase_table(width_y, ky_modes)
    table_y = jnp.stack([cos_y, -sin_y], 2).reshape(width_y, 2 * modes_y)
    cos_x, sin_x = phase_table(full_x, kx_modes)
    store_row, slots_row = (
        lax.all_gather(weight_store, "py", axis=0, tiled=True),
        lax.all_gather(block_slot, "py", axis=0, tiled=True),
    )
    slots_flat = slots_row.reshape(-1)

    def inverse_planes(spectrum):
        joined = invert_rows(spectrum, cos_x, sin_x)
        returned = lax.all_to_all(joined, "px", split_axis=3, concat_axis=2, tiled=True)
        return factor * jnp.einsum("czkx,yk->czxy", returned, table_y, precision=precise)

    weight_full = pointwise.astype(jnp.float32)
    local_x = block_slot.shape[0]
    indices = jnp.transpose(block_slot).reshape(-1)
    blocks = jnp.take(store_row, indices, axis=0).reshape(local_y, local_x, 2, channels, channels)
    mixed = channel_mix(blocks, spectrum_saved)

    def from_modes(spectrum):
        return lax.all_to_all(spectrum, "py", split_axis=1, concat_axis=3, tiled=True)

    spectral = inverse_planes(from_modes(mixed))
    mapped = jnp.einsum("oc,czxy->ozxy", pointwise, field_in, preferred_element_type=jnp.float32)
    grad = cotangent.astype(jnp.float32) * gelu_slope(
        mapped + bias_vector.reshape(channels, 1, 1, 1) + spectral
    )
    partial_value = jnp.einsum("czxy,yk->czkx", grad, table_y, precision=precise)
    moved = lax.all_to_all(partial_value, "px", split_axis=2, concat_axis=3, tiled=True)
    pieces = moved.reshape(channels, planes, local_y, 2, full_x)
    part_re = pieces[:, :, :, 0]
    part_im = pieces[:, :, :, 1]
    form = "czmx,xk->czmk"
    real_part = jnp.einsum(form, part_re, cos_x, precision=precise) + jnp.einsum(
        form, part_im, sin_x, precision=precise
    )
    imag_part = jnp.einsum(form, part_im, cos_x, precision=precise) - jnp.einsum(
        form, part_re, sin_x, precision=precise
    )
    spectrum_grad = lax.all_to_all(
        factor * jnp.stack([real_part, imag_part], -1),
        "py",
        split_axis=3,
        concat_axis=1,
        tiled=True,
    )
    input_spectrum = channel_adjoint(blocks, spectrum_grad)
    local_grad = block_gradient(spectrum_grad, spectrum_saved)
    field_grad = jnp.einsum("oc,ozxy->czxy", weight_full, grad, precision=precise) + inverse_planes(
        from_modes(input_spectrum)
    )
    grads_all = lax.all_gather(local_grad, "py", axis=0, tiled=True)
    grads_flat = grads_all.reshape(slots_flat.shape[0], 2 * channels * channels)
    targets = lax.axis_index("py") * capacity + lax.iota(jnp.int32, capacity)
    select = (targets[:, None] == slots_flat[None, :]).astype(jnp.float32)
    store_flat = jnp.dot(select, grads_flat, precision=precise)
    store_grad = store_flat.reshape(capacity, 2, channels, channels)
    return (field_grad, store_grad)


def split(values):
    high = values.astype(jnp.bfloat16)
    return high, (values - high.astype(jnp.float32)).astype(jnp.bfloat16)


def dot(left, right):
    return jnp.dot(left, right, preferred_element_type=jnp.float32)


def dot_rows(left, right):
    return lax.dot_general(left, right, (((1,), (1,)), ((), ())), preferred_element_type=jnp.float32)


def lanes_of(shape):
    return lax.broadcasted_iota(jnp.int32, shape, len(shape) - 1)


def rows_of(shape):
    return lax.broadcasted_iota(jnp.int32, shape, len(shape) - 2)


def whole(count):
    return [pl.BlockSpec(memory_space=pltpu.VMEM)] * count


def params(mebibytes=12):
    return pltpu.CompilerParams(vmem_limit_bytes=mebibytes * 1024 * 1024)


def takes(microseconds):
    return pl.CostEstimate(flops=int(microseconds * 10**9), bytes_accessed=2**20, transcendentals=0)


def outside(count):
    return [pl.BlockSpec(memory_space=pltpu.HBM)] * count


def scalars(count):
    return [pl.BlockSpec(memory_space=pltpu.SMEM)] * count


BEND_TERMS = (
    0.7978849414899104,
    0.03633308440863974,
    -3.2594744583983906e-05,
    -5.5306316703040985e-05,
    3.964773129084329e-06,
    -1.322662760933859e-07,
    1.7562773353616594e-09,
)
DENSITY = math.sqrt(2.0 / math.pi)


def twice_gelu_slope(scaled):
    square = scaled * scaled
    total = BEND_TERMS[-1] / DENSITY ** (2 * len(BEND_TERMS) - 1)
    for power in range(len(BEND_TERMS) - 2, -1, -1):
        total = total * square + BEND_TERMS[power] / DENSITY ** (2 * power + 1)
    bell = jnp.exp2(square * (-0.5 * math.log2(math.e) / DENSITY**2))
    return (1.0 + jnp.tanh(scaled * total)) + scaled * bell


def column_of(ref, start, count, rows):
    shape = (rows, 128)
    row = rows_of(shape) % count
    out = jnp.zeros(shape, jnp.int32)
    for i in range(count):
        out = jnp.where(row == i, ref[start(i)], out)
    return out


def prepare_kernel(
    place_ref, ky_ref, kx_ref, store_ref, ti_ref, tf_ref, xi_ref, xf_ref, packed_ref, *, full_x, count_x, count_y
):
    for channel in range(store_ref.shape[1]):
        rows = pl.ds(channel * store_ref.shape[2], store_ref.shape[2])
        packed_ref[rows] = jnp.concatenate([store_ref[0, channel], store_ref[1, channel]], 1)
    modes_y, width = ky_ref.shape[0], tf_ref.shape[1]
    modes_x, rows_x = kx_ref.shape[0], xf_ref.shape[0] // 4
    local_y = modes_y // count_x
    factor = 1.0 / math.sqrt(full_x * width)
    place = place_ref[0]
    start = place * rows_x
    local_x = modes_x // count_y

    def angles(modes, points, length):
        return ((modes * points) & (length - 1)).astype(jnp.float32) * (2.0 * math.pi / length)

    def ky_at(i):
        return (place ^ (i // local_y)) * local_y + i % local_y

    def kx_at(i):
        return (place_ref[1] ^ (i // local_x)) * local_x + i % local_x

    ky = column_of(ky_ref, ky_at, modes_y, modes_y)
    ky = jnp.concatenate([ky] * (width // 128), 1)
    angle = angles(ky, lanes_of(ky.shape), width)
    waves = jnp.concatenate([jnp.cos(angle), -jnp.sin(angle)], 0)
    high, low = split(waves)
    tf_ref[...] = jnp.concatenate([high, low], 0)
    for index, scale in enumerate((DENSITY, 1.0)):
        high, low = split(scale * waves)
        ti_ref[index] = jnp.concatenate([high, high, low, jnp.zeros_like(low)], 0)
    kx = column_of(kx_ref, kx_at, modes_x, modes_x)
    angle = angles(kx, start + lanes_of((modes_x, rows_x)), full_x)
    cos, sin, zero = factor * jnp.cos(angle), factor * jnp.sin(angle), jnp.zeros_like(angle)
    rows = [[cos, sin, zero, zero], [-sin, cos, zero, zero], [zero, zero, cos, sin], [zero, zero, -sin, cos]]
    high, low = split(jnp.concatenate([jnp.concatenate(row, 1) for row in rows], 0))
    xi_ref[...] = jnp.concatenate([high, high, low], 0)
    shape = (rows_x, 4 * modes_x)
    kx = jnp.transpose(column_of(kx_ref, kx_at, modes_x, 4 * modes_x))
    angle = angles(kx, start + rows_of(shape), full_x)
    cos, sin, zero = 0.5 * factor * jnp.cos(angle), 0.5 * factor * jnp.sin(angle), jnp.zeros_like(angle)
    lane = lanes_of(shape)
    real = (lane // modes_x) % 2 == 0
    first = lane < 2 * modes_x
    from_re, from_im = jnp.where(real, cos, -sin), jnp.where(real, sin, cos)
    rows = [
        jnp.where(first, from_re, zero),
        jnp.where(first, from_im, zero),
        jnp.where(first, zero, from_re),
        jnp.where(first, zero, from_im),
    ]
    high, low = split(jnp.concatenate(rows, 0))
    xf_ref[...] = jnp.concatenate([high, low], 1)


def prepare(place, ky, kx, store, full_x, rows_x, width, count_y):
    modes_y, modes_x = ky.shape[0], kx.shape[0]
    shapes = (
        (2, 4 * 2 * modes_y, width),
        (2 * 2 * modes_y, width),
        (3 * 4 * modes_x, 4 * rows_x),
        (4 * rows_x, 8 * modes_x),
    )
    return pl.pallas_call(
        functools.partial(prepare_kernel, full_x=full_x, count_x=full_x // rows_x, count_y=count_y),
        out_shape=[jax.ShapeDtypeStruct(shape, jnp.bfloat16) for shape in shapes]
        + [jax.ShapeDtypeStruct((store.shape[1] * store.shape[2], 2 * store.shape[3]), jnp.float32)],
        in_specs=scalars(3) + whole(1),
        out_specs=whole(5),
        compiler_params=params(),
        cost_estimate=takes(2),
        name="prepare",
    )(place, ky, kx, store)


def duplicate(values):
    return jnp.concatenate([values, values], -1)


def pack_kernel(slots_hbm, spec_hbm, out_ref, slots_ref, spec_ref, sems):
    copies = [
        pltpu.make_async_copy(slots_hbm, slots_ref, sems.at[0]),
        pltpu.make_async_copy(spec_hbm, spec_ref, sems.at[1]),
    ]
    for copy in copies:
        copy.start()
    for copy in copies:
        copy.wait()
    local_x, local_y = slots_ref.shape
    modes = local_x * local_y
    groups = spec_ref.shape[0] // modes
    columns = []
    for group in range(groups // 2):
        for part in range(2):
            columns.append(spec_ref[pl.ds(group * 2 * modes + part, modes, stride=2)])
    shape = (modes, out_ref.shape[1] - groups * spec_ref.shape[1])
    row = rows_of(shape)
    numbers = jnp.zeros(shape, jnp.int32)
    for mode in range(modes):
        numbers = jnp.where(row == mode, slots_ref[mode % local_x, mode // local_x], numbers)
    out_ref[...] = jnp.concatenate(columns + [numbers.astype(jnp.float32)], 1)


def pack(slots, spectrum, lanes):
    modes = slots.size
    width = spectrum.size // modes + lanes
    return pl.pallas_call(
        pack_kernel,
        out_shape=jax.ShapeDtypeStruct((modes, width), jnp.float32),
        in_specs=outside(2),
        out_specs=whole(1)[0],
        scratch_shapes=[
            pltpu.SMEM(slots.shape, slots.dtype),
            pltpu.VMEM(spectrum.shape, spectrum.dtype),
            pltpu.SemaphoreType.DMA((2,)),
        ],
        compiler_params=params(60),
        name="pack",
    )(slots, spectrum)


def mix_kernel(place_ref, packed_ref, *refs, count, local_x):
    pieces, (kept_ref, slots_ref, out_ref, ra_ref, rb_ref, uc_ref, ud_ref) = refs[:count], refs[count:]
    planes, channels, lanes = out_ref.shape
    capacity = lanes // 2
    wide = pieces[0].shape[1] - lanes
    local_y = pieces[0].shape[0] // local_x
    for index, piece in enumerate(pieces):
        for mode in range(local_y):
            rows = pl.ds((mode * count + index) * local_x, local_x)
            slots_ref[rows] = piece[pl.ds(mode * local_x, local_x), pl.ds(wide, lanes)]
    numbers = jnp.transpose(jnp.concatenate([piece[:, pl.ds(wide, lanes)] for piece in pieces], 0))
    wanted = (place_ref[1] * capacity + rows_of(numbers.shape) % capacity).astype(jnp.float32)
    chosen = (numbers == wanted).astype(jnp.bfloat16)
    high, low = split(jnp.concatenate([piece[:, pl.ds(0, wide)] for piece in pieces], 0))
    placed = jnp.transpose(dot(chosen, high) + dot(chosen, low))
    kept_ref[...] = placed
    parts = placed.reshape(planes, 2, channels, lanes)
    first = lanes_of((channels, lanes)) < capacity
    for plane in range(planes):
        rows = pl.ds(plane * channels, channels)
        uc_ref[rows] = jnp.where(first, parts[plane, 0], parts[plane, 1])
        ud_ref[rows] = jnp.where(first, parts[plane, 1], parts[plane, 0])
    for part in range(channels):
        rows = pl.ds(part * channels, channels)
        block = packed_ref[rows]
        swapped = swap_halves(block)
        low_half = lanes_of(block.shape) < capacity
        ra_ref[rows] = jnp.where(low_half, block, swapped)
        rb_ref[rows] = jnp.where(low_half, -swapped, block)

    def step(channel, sums):
        ra = ra_ref[pl.ds(channel, channels, stride=channels)]
        rb = rb_ref[pl.ds(channel, channels, stride=channels)]
        return tuple(
            total
            + ra * uc_ref[pl.ds(plane * channels + channel, 1)]
            + rb * ud_ref[pl.ds(plane * channels + channel, 1)]
            for plane, total in enumerate(sums)
        )

    zero = jnp.zeros((channels, lanes), jnp.float32)
    sums = lax.fori_loop(0, channels, step, (zero,) * planes)
    for plane in range(planes):
        out_ref[plane] = sums[plane]


def mix(place, packed, pieces, planes, local_x):
    channels, lanes = math.isqrt(packed.shape[0]), packed.shape[1]
    count = len(pieces)
    return pl.pallas_call(
        functools.partial(mix_kernel, count=count, local_x=local_x),
        out_shape=[
            jax.ShapeDtypeStruct((2 * planes * channels, lanes), jnp.float32),
            jax.ShapeDtypeStruct((count * pieces[0].shape[0], lanes), jnp.float32),
            jax.ShapeDtypeStruct((planes, channels, lanes), jnp.float32),
        ],
        in_specs=scalars(1) + whole(1 + count),
        out_specs=whole(3),
        scratch_shapes=[pltpu.VMEM((channels * channels, lanes), jnp.float32)] * 2
        + [pltpu.VMEM((planes * channels, lanes), jnp.float32)] * 2,
        compiler_params=params(),
        cost_estimate=takes(3),
        name="mix",
    )(place, packed, *pieces)


def swap_halves(values):
    half = values.shape[-1] // 2
    return jnp.concatenate([values[..., half:], values[..., :half]], -1)


def weight_grad_kernel(place_ref, kept_ref, *refs):
    *pairs, out_ref, gs_ref = refs
    grads = [each.at[core] for each in pairs for core in range(2)]
    channels, lanes = grads[0].shape
    capacity = lanes // 2
    starts = []
    for index, grad in enumerate(grads):
        swapped = swap_halves(grad[...])
        gs_ref[index] = jnp.where(lanes_of(swapped.shape) < capacity, swapped, -swapped)
        starts.append((place_ref[1] ^ index) * 2 * channels)

    def step(channel, carry):
        total = jnp.zeros((channels, lanes), jnp.float32)
        for index, start in enumerate(starts):
            real = kept_ref[pl.ds(start, channels)]
            imag = kept_ref[pl.ds(start + channels, channels)]
            total = total + real * grads[index][pl.ds(channel, 1)] + imag * gs_ref[index, pl.ds(channel, 1)]
        out_ref[0, channel] = total[:, :capacity]
        out_ref[1, channel] = total[:, capacity:]
        return carry

    lax.fori_loop(0, channels, step, 0, unroll=4)


def weight_grad(place, kept, pairs):
    _, channels, lanes = pairs[0].shape
    return pl.pallas_call(
        weight_grad_kernel,
        out_shape=jax.ShapeDtypeStruct((2, channels, channels, lanes // 2), jnp.float32),
        in_specs=scalars(1) + whole(1 + len(pairs)),
        out_specs=whole(1)[0],
        scratch_shapes=[pltpu.VMEM((2 * len(pairs), channels, lanes), jnp.float32)],
        compiler_params=params(),
        cost_estimate=takes(2),
        name="weight_grad",
    )(place, kept, *pairs)


def fill_selection(slots_ref, chosen_ref, modes_x, capacity, flip=0):
    lanes = 2 * capacity
    shape = (modes_x, lanes)
    lane = lanes_of(shape)
    first = lane < capacity
    zero = jnp.zeros(shape, jnp.float32)
    for mode in range(slots_ref.shape[0] // modes_x):
        numbers = slots_ref[pl.ds(mode * modes_x, modes_x)]
        for owner in range(chosen_ref.shape[1] // lanes):
            wanted = ((owner ^ flip) * capacity + lane % capacity).astype(jnp.float32)
            hit = jnp.where(numbers == wanted, 1.0, 0.0)
            both = jnp.concatenate([jnp.where(first, hit, zero), jnp.where(first, zero, hit)], 0)
            chosen_ref[pl.ds(mode * 2 * modes_x, 2 * modes_x), pl.ds(owner * lanes, lanes)] = both.astype(jnp.bfloat16)


def slots_to_modes(blocks, chosen_ref, out_ref, modes_x):
    channels = blocks[0].shape[0]
    half = channels // 2
    high, low = split(jnp.concatenate(blocks, 1))
    found = dot_rows(jnp.concatenate([high, low], 0), chosen_ref[...])
    found = found[:channels] + found[channels:]
    local_y = found.shape[1] // (2 * modes_x)
    for mode in range(local_y):
        piece = found[:, mode * 2 * modes_x : (mode + 1) * 2 * modes_x]
        out_ref[pl.ds(mode, half, stride=local_y)] = jnp.concatenate([piece[:half], piece[half:]], 1)


def to_modes_kernel(slots_ref, in_ref, out_ref, chosen_ref, *, modes_x):
    owners, _, lanes = in_ref.shape
    fill_selection(slots_ref, chosen_ref, modes_x, lanes // 2)
    slots_to_modes([in_ref[owner] for owner in range(owners)], chosen_ref, out_ref, modes_x)


def to_modes(slots, values, modes_x):
    owners, channels, lanes = values.shape
    local_y = slots.shape[0] // modes_x
    return pl.pallas_call(
        functools.partial(to_modes_kernel, modes_x=modes_x),
        out_shape=jax.ShapeDtypeStruct((channels // 2 * local_y, 4 * modes_x), jnp.float32),
        in_specs=whole(2),
        out_specs=whole(1)[0],
        scratch_shapes=[pltpu.VMEM((2 * slots.shape[0], owners * lanes), jnp.bfloat16)],
        compiler_params=params(),
        cost_estimate=takes(1),
        name="to_modes",
    )(slots, values)


def adjoint_kernel(place_ref, slots_ref, *refs, modes_x, blocks, count):
    pieces, stores, refs = refs[:blocks], refs[blocks : -5], refs[-5:]
    same_ref, other_ref, out_ref, chosen_ref, sum_ref = refs
    _, channels, lanes = same_ref.shape
    half = channels // 2
    fill_selection(slots_ref, chosen_ref, modes_x, lanes // 2, place_ref[1])
    sum_ref[...] = sum(piece[...] for piece in pieces)
    local_y = sum_ref.shape[0] // half
    columns = []
    for mode in range(local_y):
        piece = sum_ref[pl.ds(mode, half, stride=local_y)]
        columns.append(jnp.concatenate([piece[:, : 2 * modes_x], piece[:, 2 * modes_x :]], 0))
    high, low = split(jnp.concatenate(columns, 1))
    found = dot(jnp.concatenate([high, low], 0), chosen_ref[...])
    found = found[:channels] + found[channels:]
    mixed = []
    for owner in range(count):
        values = found[:, owner * lanes : (owner + 1) * lanes]
        (other_ref if owner % 2 else same_ref)[owner // 2] = values
        swapped = swap_halves(values)
        real = jnp.zeros((channels, lanes), jnp.float32)
        imag = real
        for channel in range(channels):
            store, row = stores[owner], channel
            if owner >= count - 2:
                store = stores[owner + (2 if channel >= half else 0)]
                row = channel % half
            block = store[pl.ds(row * channels, channels)]
            real = real + block * values[channel : channel + 1]
            imag = imag + block * swapped[channel : channel + 1]
        other_re, other_im = swap_halves(real), swap_halves(imag)
        first = lanes_of(real.shape) < lanes // 2
        mixed.append(jnp.where(first, real + other_re, other_im - imag))
    slots_to_modes(mixed, chosen_ref, out_ref, modes_x)


def adjoint(place, slots, pieces, stores, modes_x):
    count, blocks = len(stores) - 2, len(pieces)
    lanes = stores[0].shape[1]
    channels = 2 * pieces[0].shape[0] * modes_x // slots.shape[0]
    return pl.pallas_call(
        functools.partial(adjoint_kernel, modes_x=modes_x, blocks=blocks, count=count),
        out_shape=[jax.ShapeDtypeStruct((count // 2, channels, lanes), jnp.float32)] * 2
        + [jax.ShapeDtypeStruct(pieces[0].shape, jnp.float32)],
        in_specs=scalars(1) + whole(1 + blocks + len(stores)),
        out_specs=whole(3),
        scratch_shapes=[
            pltpu.VMEM((2 * slots.shape[0], count * lanes), jnp.bfloat16),
            pltpu.VMEM(pieces[0].shape, jnp.float32),
        ],
        compiler_params=params(),
        cost_estimate=takes(3),
        name="adjoint",
    )(place, slots, *pieces, *stores)


def pair_kernel(same_ref, other_ref, *outs):
    for index, out in enumerate(outs):
        out[0] = same_ref[index]
        out[1] = other_ref[index]


def pair(same, other):
    return pl.pallas_call(
        pair_kernel,
        out_shape=[jax.ShapeDtypeStruct((2,) + same.shape[1:], same.dtype)] * same.shape[0],
        in_specs=whole(2),
        out_specs=whole(same.shape[0]),
        compiler_params=params(),
        cost_estimate=takes(0.3),
        name="pair",
    )(same, other)


def halves_kernel(first_ref, second_ref, low_ref, high_ref):
    half = low_ref.shape[0]
    low_ref[...] = first_ref[pl.ds(0, half)]
    high_ref[...] = second_ref[pl.ds(half, half)]


def halves(first, second):
    shape = (first.shape[0] // 2, first.shape[1])
    return pl.pallas_call(
        halves_kernel,
        out_shape=[jax.ShapeDtypeStruct(shape, first.dtype)] * 2,
        in_specs=whole(2),
        out_specs=whole(2),
        compiler_params=params(),
        cost_estimate=takes(0.3),
        name="halves",
    )(first, second)


def spread(small, rows, axis):
    count = small.shape[0]
    shape = (count * rows, count)
    take = (rows_of(shape) // rows == lanes_of(shape)).astype(jnp.bfloat16)
    shape = (count, count * rows)
    put = (lanes_of(shape) // rows == rows_of(shape)).astype(jnp.bfloat16)
    picked = dot(take, small) if axis else dot_rows(take, small)
    full = dot(picked.astype(jnp.bfloat16), put)
    shape = full.shape
    return jnp.where(rows_of(shape) % rows == lanes_of(shape) % rows, full, 0.0)


def pointwise_kernel(weight_ref, bias_ref, in_ref, out_ref, full_ref, shift_ref):
    channels, rows_x, width = in_ref.shape
    rows = full_ref.shape[0] // channels
    steps = rows_x // (2 * rows)

    full_ref[...] = spread(weight_ref[...], rows, 1).astype(jnp.bfloat16)
    for channel in range(channels):
        shift_ref[channel] = jnp.full(shift_ref.shape[1:], bias_ref[channel] * DENSITY, jnp.float32)

    def step(index, carry):
        values = in_ref[:, pl.ds(index * 2 * rows, 2 * rows), :].astype(jnp.float32)
        for half in range(2):
            block = values[:, half * rows : (half + 1) * rows].reshape(channels * rows, width)
            out = dot(full_ref[...], block.astype(jnp.bfloat16)).reshape(channels, rows, width)
            at = index * 2 * rows + half * rows
            out_ref[:, pl.ds(at, rows), :] = out * DENSITY + shift_ref[...]
        return carry

    lax.fori_loop(0, steps, step, 0)


def pointwise_map(weight, bias, values, rows=8):
    channels, rows_x, width = values.shape
    return pl.pallas_call(
        pointwise_kernel,
        out_shape=jax.ShapeDtypeStruct(values.shape, jnp.float32),
        in_specs=whole(1) + scalars(1) + whole(1),
        out_specs=whole(1)[0],
        scratch_shapes=[
            pltpu.VMEM((channels * rows, channels * rows), jnp.bfloat16),
            pltpu.VMEM((channels, rows, width), jnp.float32),
        ],
        compiler_params=params(),
        cost_estimate=takes(4),
        name="pointwise_map",
    )(weight, bias, values)


def pointwise_back_kernel(weight_ref, in_ref, out_ref, full_ref):
    channels, rows_x, width = in_ref.shape
    rows = full_ref.shape[0] // channels
    full_ref[...] = (0.5 * spread(weight_ref[...], rows, 0)).astype(jnp.bfloat16)

    def step(index, carry):
        block = in_ref[:, pl.ds(index * rows, rows), :].reshape(channels * rows, width)
        high, low = split(block)
        out = dot(full_ref[...], high) + dot(full_ref[...], low)
        out_ref[:, pl.ds(index * rows, rows), :] = out.reshape(channels, rows, width)
        return carry

    lax.fori_loop(0, rows_x // rows, step, 0)


def pointwise_back(weight, values, rows=8):
    channels = values.shape[0]
    return pl.pallas_call(
        pointwise_back_kernel,
        out_shape=jax.ShapeDtypeStruct(values.shape, jnp.float32),
        in_specs=whole(2),
        out_specs=whole(1)[0],
        scratch_shapes=[pltpu.VMEM((channels * rows, channels * rows), jnp.bfloat16)],
        compiler_params=params(),
        cost_estimate=takes(4),
        name="pointwise_back",
    )(weight, values)


def invert_x(pieces, xi_ref, st_ref):
    high, low = split(jnp.concatenate([piece[...] for piece in pieces], 0))
    deep = high.shape[1]
    left = jnp.concatenate([high, low], 1)
    found = dot(left, xi_ref[pl.ds(0, 2 * deep)]) + dot(high, xi_ref[pl.ds(2 * deep, deep)])
    st_ref[...] = found.reshape(st_ref.shape)


def spectral_part(index, half, st_ref, table):
    blocks, _, local_y, wide = st_ref.shape
    rows_x = wide // 4
    here = st_ref[:, index, :, pl.ds(half * 2 * rows_x, 2 * rows_x)].reshape(blocks * local_y, 2 * rows_x)
    parts = [here[:, :rows_x], here[:, rows_x:]]
    tall = jnp.transpose(jnp.concatenate(parts + parts, 0))
    high = tall.astype(jnp.bfloat16)
    first = lanes_of(tall.shape) < tall.shape[1] // 2
    mixed = jnp.where(first, tall, tall - high.astype(jnp.float32)).astype(jnp.bfloat16)
    return dot(jnp.concatenate([mixed, high], 1), table)


def slope_kernel(*refs, blocks):
    pieces, (xi_ref, ti_ref, tf_ref, xf_ref, mapped_ref, cot_ref) = refs[:blocks], refs[blocks : blocks + 6]
    (grad_ref, *sums), (st_ref, yt_ref) = refs[blocks + 6 : -2], refs[-2:]
    channels, rows_x, _ = mapped_ref.shape
    deep = tf_ref.shape[0] // 2
    modes_y = deep // 2
    local_y = modes_y // blocks
    invert_x(pieces, xi_ref, st_ref)

    def step(index, carry):
        for half in range(2):
            channel = half * (channels // 2) + index
            before = mapped_ref[channel] + spectral_part(index, half, st_ref, ti_ref[0])
            grad = cot_ref[channel].astype(jnp.float32) * twice_gelu_slope(before)
            grad_ref[channel] = grad
            high, low = split(grad)
            both = dot_rows(tf_ref[...], high)
            found = both[:deep] + both[deep:] + dot_rows(tf_ref[pl.ds(0, deep)], low)
            for block in range(blocks):
                for part in range(2):
                    at = part * modes_y + block * local_y
                    columns = pl.ds((2 * half + part) * rows_x, rows_x)
                    yt_ref[block, index, :, columns] = found[at : at + local_y]
        return carry

    lax.fori_loop(0, channels // 2, step, 0, unroll=2)
    high, low = split(yt_ref[...].reshape(-1, yt_ref.shape[-1]))
    lanes = xf_ref.shape[1] // 2
    both = dot(high, xf_ref[...])
    total = both[:, :lanes] + both[:, lanes:] + dot(low, xf_ref[:, :lanes])
    rows = total.shape[0] // blocks
    for block in range(blocks):
        sums[block][...] = total[block * rows : (block + 1) * rows]


def slope_step(pieces, tables, mapped, cotangent):
    ti, tf, xi, xf = tables
    blocks = len(pieces)
    channels, rows_x, _ = mapped.shape
    half = channels // 2
    local_y = pieces[0].shape[0] // half
    grad, *sums = pl.pallas_call(
        functools.partial(slope_kernel, blocks=blocks),
        out_shape=[jax.ShapeDtypeStruct(mapped.shape, jnp.float32)]
        + [jax.ShapeDtypeStruct(pieces[0].shape, jnp.float32)] * blocks,
        in_specs=whole(blocks + 6),
        out_specs=whole(1 + blocks),
        scratch_shapes=[pltpu.VMEM((blocks, half, local_y, 4 * rows_x), jnp.float32)] * 2,
        compiler_params=params(),
        cost_estimate=takes(13),
        name="slope_step",
    )(*pieces, xi, ti, tf, xf, mapped, cotangent)
    return grad, sums


def finish_kernel(*refs, blocks, group):
    pieces, (xi_ref, ti_ref, part_ref, out_ref, st_ref, sum_ref, sems) = refs[:blocks], refs[blocks:]
    channels = part_ref.shape[0]
    invert_x(pieces, xi_ref, st_ref)

    def copies(index):
        for half in range(2):
            rows = pl.ds(half * (channels // 2) + index * group, group)
            yield pltpu.make_async_copy(sum_ref.at[rows], out_ref.at[rows], sems.at[half, index])

    def step(index, carry):
        for half in range(2):
            for member in range(group):
                place = index * group + member
                channel = half * (channels // 2) + place
                sum_ref[channel] = part_ref[channel] + spectral_part(place, half, st_ref, ti_ref[1])
        for copy in copies(index):
            copy.start()
        return carry

    def settle(index, carry):
        for copy in copies(index):
            copy.wait()
        return carry

    steps = channels // (2 * group)
    lax.fori_loop(0, steps, step, 0)
    lax.fori_loop(0, steps, settle, 0)


def finish(pieces, tables, part, group=2):
    ti, _, xi, _ = tables
    blocks = len(pieces)
    channels, rows_x, _ = part.shape
    half = channels // 2
    local_y = pieces[0].shape[0] // half
    return pl.pallas_call(
        functools.partial(finish_kernel, blocks=blocks, group=group),
        out_shape=jax.ShapeDtypeStruct(part.shape, jnp.float32),
        in_specs=whole(blocks + 3),
        out_specs=outside(1)[0],
        scratch_shapes=[
            pltpu.VMEM((blocks, half, local_y, 4 * rows_x), jnp.float32),
            pltpu.VMEM(part.shape, jnp.float32),
            pltpu.SemaphoreType.DMA((2, half // group)),
        ],
        compiler_params=params(20),
        cost_estimate=takes(4),
        name="finish",
    )(*pieces, xi, ti, part)


def exchange(piece, axis, count, flip):
    return lax.ppermute(piece, axis, [(i, i ^ flip) for i in range(count)])


def between_chips(piece, count):
    return [piece] + [exchange(piece, "py", count, step) for step in range(2, count, 2)]


def between_cores(pieces, count):
    other = [exchange(piece, "py", count, 1) for piece in pieces]
    return [each for pair in zip(pieces, other) for each in pair]


def from_all(piece, axis, count):
    return [piece] + [exchange(piece, axis, count, step) for step in range(1, count)]


def to_all(pieces, axis, count):
    return pieces[:1] + [exchange(pieces[step], axis, count, step) for step in range(1, count)]


def on_device_packed(
    field_in,
    cotangent,
    spectrum_saved,
    weight_store,
    block_slot,
    kx_modes,
    ky_modes,
    pointwise,
    bias_vector,
):
    channels, _, rows_x, width_y = field_in.shape
    count_x, count_y = lax.axis_size("px"), lax.axis_size("py")
    full_x = rows_x * count_x
    planes, local_y, local_x = spectrum_saved.shape[1:4]
    modes_x = kx_modes.shape[0]
    place_x, place_y = lax.axis_index("px"), lax.axis_index("py")
    lanes = 2 * weight_store.shape[0]
    store = jnp.transpose(weight_store, (1, 2, 3, 0))
    place = jnp.stack([place_x, place_y])

    barrier = lax.optimization_barrier
    slots, spectrum, place = barrier((block_slot, spectrum_saved, place))
    spectrum = jnp.transpose(spectrum, (1, 2, 3, 4, 0)).reshape(-1, channels)
    pieces = between_chips(pack(slots, spectrum, lanes), count_y)
    *tables, packed = prepare(place, ky_modes, kx_modes, store, full_x, rows_x, width_y, count_y)
    pieces, tables, packed = barrier((pieces, tables, packed))
    pieces, packed = barrier((between_cores(pieces, count_y), packed))
    kept, slots, mixed = mix(place, packed, pieces, planes, local_x)
    stores = [packed, exchange(packed, "py", count_y, 2), exchange(packed, "py", count_y, 4)]
    mixed = lax.all_to_all(mixed, "py", split_axis=0, concat_axis=0, tiled=True)
    mixed, stores = barrier((mixed, stores))
    low, high = halves(*stores[1:])
    far = [exchange(low, "py", count_y, 4), exchange(high, "py", count_y, 2)]
    received = from_all(to_modes(slots, mixed, modes_x), "px", count_x)
    mapped = pointwise_map(pointwise, bias_vector, field_in[:, 0])
    received, mapped, far = barrier((received, mapped, far))
    stores = between_cores(stores, count_y)
    far = between_cores(far, count_y)
    stores = stores + [far[0], far[1], far[2], far[3]]
    grad, sums = slope_step(received, tables, mapped, cotangent[:, 0])
    sums, grad, stores = barrier((list(sums), grad, stores))
    received = to_all(sums, "px", count_x)
    back = pointwise_back(pointwise, grad)
    received, back = barrier((received, back))
    same, other, mixed = adjoint(place, slots, received, stores, modes_x)
    received = from_all(mixed, "px", count_x)
    pairs = list(pair(same, exchange(other, "py", count_y, 1)))
    pairs = pairs[:1] + [exchange(pairs[i], "py", count_y, 2 * i) for i in range(1, len(pairs))]
    field_grad = finish(received, tables, back)
    blocks = weight_grad(place, kept, pairs)
    return (field_grad[:, None], jnp.transpose(blocks, (3, 0, 1, 2)))


def packs(mesh, channels, planes, rows, width, modes, capacity):
    count_x, count_y = mesh.shape["px"], mesh.shape["py"]
    powers = all(size & (size - 1) == 0 for size in (rows, width))
    return (
        powers
        and (count_x, count_y, planes) == (4, 8, 8)
        and channels == 32
        and 4 * modes == 128
        and 2 * capacity == 128
        and rows // count_x == 128
        and width % 256 == 0
        and modes // count_x == 8
    )


def solution(mesh):
    placed = (
        P(None, "py", "px", None),
        P(None, "py", "px", None),
        P(None, None, "px", "py", None),
        P(("px", "py"), None, None, None),
        P("py", "px"),
        P(),
        P(),
        P(),
        P(),
    )

    def run(*args):
        channels, planes, rows, width = args[0].shape
        capacity = args[3].shape[0] // mesh.size
        packed = packs(mesh, channels, planes, rows, width, args[5].shape[0], capacity)
        return jax.shard_map(
            on_device_packed if packed else on_device,
            mesh=mesh,
            in_specs=placed,
            out_specs=(P(None, "py", "px", None), P(("px", "py"), None, None, None)),
            check_vma=False,
        )(*args)

    return run
```

profile of v0, /device:TPU:0, one launch (start us, length us, event | category | flops | bytes accessed | tf_op | source)
XLA Modules:
  0.0 86.9 jit_solution(13449278837254967986)
XLA Ops:
  0.6 0.1 pad_add_fusion.place_ref
  0.7 1.7 %pack.1.refs_0_ = f32[32,640]{1,0:T(8,128)} custom-call(s32[4,8]{1,0:T(4,128)} %slots_hbm, f32[512,32]{1,0:T(8,128)} %bitcast.16), custom_call_target="tpu_custom_call" | custom-call | tf_op jit(solution)/shard_map/pack/pallas_call | solution.py:342
  2.4 3.0 %collective-permute-start = (f32[32,640]{1,0:T(8,128)}, f32[32,640]{1,0:T(8,128)S(1)}, u32[]{:S(2)}, u32[]{:S(2)}) collective-permute-start(f32[32,640]{1,0:T(8,128)} %pack.1.refs_0_), channel_id=1, source_target_pairs={{0,2},{1,3},{2,0},{3,1},{4,6},{5,7},{6,4},{7,5},{8,10},{9,11},{10,... | collective-permute-start | bytes 245768 | tf_op jit(solution)/shard_map/ppermute | solution.py:814
  5.4 1.5 %collective-permute-start.1 = (f32[32,640]{1,0:T(8,128)}, f32[32,640]{1,0:T(8,128)S(1)}, u32[]{:S(2)}, u32[]{:S(2)}) collective-permute-start(f32[32,640]{1,0:T(8,128)} %pack.1.refs_0_), channel_id=1, source_target_pairs={{0,4},{1,5},{2,6},{3,7},{4,0},{5,1},{6,2},{7,3},{8,12},{9,13},{10,... | collective-permute-start | bytes 245768 | tf_op jit(solution)/shard_map/ppermute | solution.py:814
  7.0 0.0 collective-permute-start.2
  7.0 1.2 %copy-done.4 = f32[64,2,32,32]{0,3,2,1:T(8,128)S(1)} copy-done((f32[64,2,32,32]{0,3,2,1:T(8,128)S(1)}, f32[64,2,32,32]{0,3,2,1:T(8,128)}, u32[]{:S(2)}) %copy-start.4) | copy-done | bytes 524312
  8.2 0.7 copy-done.5
  8.9 0.7 copy-done.6
  9.5 1.3 %prepare.1 = (bf16[2,256,512]{2,1,0:T(8,128)(2,1)S(1)}, bf16[128,512]{1,0:T(8,128)(2,1)S(1)}, bf16[384,512]{1,0:T(8,128)(2,1)S(1)}, bf16[512,256]{1,0:T(8,128)(2,1)S(1)}, f32[1024,128]{1,0:T(8,128)S(1)}) custom-call(s32[2]{0:T(128)S(1)} %pad_add_fusion.place_ref, s32[32]{0:T(128)S(1)} %copy-done.5, s32[32]{0:T(128)S(1)} %copy-done.6, ...), custom_call_target="tpu_custom_call" | custom-call | flops 2000000000 | bytes 1048576 | tf_op jit(solution)/shard_map/prepare/pallas_call | solution.py:299
  10.9 0.0 copy-start.1
  10.9 0.0 copy-start.7
  10.9 0.0 collective-permute-done.refs_2_
  10.9 0.1 collective-permute-done.1.refs_4_
  11.0 1.5 %collective-permute-done.2.refs_6_ = f32[32,640]{1,0:T(8,128)S(1)} collective-permute-done((f32[32,640]{1,0:T(8,128)}, f32[32,640]{1,0:T(8,128)S(1)}, u32[]{:S(2)}, u32[]{:S(2)}) %collective-permute-start.2) | collective-permute-done | bytes 81952 | tf_op jit(solution)/shard_map/ppermute | solution.py:814
  12.5 0.0 collective-permute-start.3
  12.5 0.5 collective-permute-start.4
  13.0 0.0 collective-permute-start.5
  13.0 0.5 collective-permute-start.6
  13.5 0.5 collective-permute-done.3.refs_1_
  14.1 0.2 collective-permute-done.5.refs_5_
  14.3 0.2 collective-permute-done.6.refs_7_
  14.5 0.5 collective-permute-start.7
  15.0 1.4 %collective-permute-start.8 = (f32[1024,128]{1,0:T(8,128)S(1)}, f32[1024,128]{1,0:T(8,128)S(1)}, u32[]{:S(2)}, u32[]{:S(2)}) collective-permute-start(f32[1024,128]{1,0:T(8,128)S(1)} %get-tuple-element.131.packed_ref.refs_4_), channel_id=1, source_target_pairs={{0,4},{1,5},{2,6},{3,7},{4,0},{5,1},{6,2},{7,3},{8,12},{9,13},{10,... | collective-permute-start | bytes 1572872 | tf_op jit(solution)/shard_map/ppermute | solution.py:814
  16.4 0.9 %copy-done = f32[32,640]{1,0:T(8,128)S(1)} copy-done((f32[32,640]{1,0:T(8,128)S(1)}, f32[32,640]{1,0:T(8,128)}, u32[]{:S(2)}) %copy-start) | copy-done | bytes 81944
  17.3 2.9 %mix.1 = (f32[512,128]{1,0:T(8,128)S(1)}, f32[256,128]{1,0:T(8,128)S(1)}, f32[8,32,128]{2,1,0:T(8,128)S(1)}) custom-call(s32[2]{0:T(128)S(1)} %pad_add_fusion.place_ref, f32[1024,128]{1,0:T(8,128)S(1)} %get-tuple-element.131.packed_ref.refs_4_, f32[32,640]{1,0:T(8,128)S(1)} %copy-done, f32[32,640]{1,0:T(8,128)S(1)} %collective-permute-done.3.refs_1_, ...), custom_call_target="tpu_custom_call" | custom-call | flops 3000000000 | bytes 1048576 | tf_op jit(solution)/shard_map/mix/pallas_call | solution.py:406
  20.2 10.1 %all_to_all.5.in_ref = f32[8,32,128]{2,1,0:T(8,128)S(1)} all-to-all(f32[8,32,128]{2,1,0:T(8,128)S(1)} %get-tuple-element.99), channel_id=1, replica_groups=mesh['px'=4,'py'=8] {'py'}, dimensions={0} | all-to-all | bytes 262144 | tf_op jit(solution)/shard_map/all_to_all | solution.py:864
  30.3 0.0 collective-permute-done.7.first_ref.refs_6_
  30.3 0.0 collective-permute-done.8.second_ref.refs_8_
  30.3 0.6 to_modes.1.refs_0_
  30.9 0.0 copy-start.3
  30.9 2.7 %collective-permute-start.10 = (f32[128,128]{1,0:T(8,128)S(1)}, f32[128,128]{1,0:T(8,128)S(1)}, u32[]{:S(2)}, u32[]{:S(2)}) collective-permute-start(f32[128,128]{1,0:T(8,128)S(1)} %to_modes.1.refs_0_), channel_id=1, source_target_pairs={{0,16},{8,24},{16,0},{24,8},{1,17},{9,25},{17,1},{25,9},{2,18},{10... | collective-permute-start | bytes 196616 | tf_op jit(solution)/shard_map/ppermute | solution.py:814
  33.5 1.3 %collective-permute-start.11 = (f32[128,128]{1,0:T(8,128)S(1)}, f32[128,128]{1,0:T(8,128)S(1)}, u32[]{:S(2)}, u32[]{:S(2)}) collective-permute-start(f32[128,128]{1,0:T(8,128)S(1)} %to_modes.1.refs_0_), channel_id=1, source_target_pairs={{0,24},{8,16},{16,8},{24,0},{1,25},{9,17},{17,9},{25,1},{2,26},{10... | collective-permute-start | bytes 196616 | tf_op jit(solution)/shard_map/ppermute | solution.py:814
  34.9 0.2 collective-permute-start.9
  35.2 1.5 %collective-permute-start.12 = (f32[512,128]{1,0:T(8,128)S(1)}, f32[512,128]{1,0:T(8,128)S(1)}, u32[]{:S(2)}, u32[]{:S(2)}) collective-permute-start(f32[512,128]{1,0:T(8,128)S(1)} %get-tuple-element.103), channel_id=1, source_target_pairs={{0,4},{1,5},{2,6},{3,7},{4,0},{5,1},{6,2},{7,3},{8,12},{9,13},{10,... | collective-permute-start | bytes 786440 | tf_op jit(solution)/shard_map/ppermute | solution.py:814
  36.6 0.6 collective-permute-start.13
  37.3 3.3 %pointwise_map.1.refs_8_ = f32[32,128,512]{2,1,0:T(8,128)S(1)} custom-call(bf16[32,32]{1,0:T(8,128)(2,1)S(1)} %copy-done.1, f32[32]{0:T(128)S(1)} %copy-done.7, bf16[32,128,512]{2,1,0:T(8,128)(2,1)S(1)} %bitcast.12), custom_call_target="tpu_custom_call" | custom-call | flops 4000000000 | bytes 1048576 | tf_op jit(solution)/shard_map/pointwise_map/pallas_call | solution.py:642
  40.6 0.1 collective-permute-start.15
  40.7 0.0 collective-permute-done.11.refs_3_
  40.7 0.5 collective-permute-start.16
  41.2 0.0 collective-permute-done.9.refs_1_
  41.2 0.1 collective-permute-start.14
  41.3 1.5 %collective-permute-done.12.refs_10_ = f32[512,128]{1,0:T(8,128)S(1)} collective-permute-done((f32[512,128]{1,0:T(8,128)S(1)}, f32[512,128]{1,0:T(8,128)S(1)}, u32[]{:S(2)}, u32[]{:S(2)}) %collective-permute-start.12) | collective-permute-done | bytes 262176 | tf_op jit(solution)/shard_map/ppermute | solution.py:814
  42.7 1.2 %collective-permute-done.13.refs_12_ = f32[512,128]{1,0:T(8,128)S(1)} collective-permute-done((f32[512,128]{1,0:T(8,128)S(1)}, f32[512,128]{1,0:T(8,128)S(1)}, u32[]{:S(2)}, u32[]{:S(2)}) %collective-permute-start.13) | collective-permute-done | bytes 262176 | tf_op jit(solution)/shard_map/ppermute | solution.py:814
  43.9 0.5 collective-permute-start.18
  44.4 13.3 %slope_step.1 = (f32[32,128,512]{2,1,0:T(8,128)S(1)}, f32[128,128]{1,0:T(8,128)S(1)}, f32[128,128]{1,0:T(8,128)S(1)}, f32[128,128]{1,0:T(8,128)S(1)}, f32[128,128]{1,0:T(8,128)S(1)}) custom-call(f32[128,128]{1,0:T(8,128)S(1)} %to_modes.1.refs_0_, f32[128,128]{1,0:T(8,128)S(1)} %collective-permute-done.9.refs_1_, ...), custom_call_target="tpu_custom_call" | custom-call | flops 12999999488 | bytes 1048576 | tf_op jit(solution)/shard_map/slope_step/pallas_call | solution.py:747
  57.7 0.0 collective-permute-done.14.refs_5_
  57.8 0.0 collective-permute-done.16.refs_9_
  57.8 0.0 collective-permute-done.17.refs_11_
  57.8 1.6 %collective-permute-start.19 = (f32[128,128]{1,0:T(8,128)S(1)}, f32[128,128]{1,0:T(8,128)S(1)}, u32[]{:S(2)}, u32[]{:S(2)}) collective-permute-start(f32[128,128]{1,0:T(8,128)S(1)} %get-tuple-element.123), channel_id=1, source_target_pairs={{0,8},{8,0},{16,24},{24,16},{1,9},{9,1},{17,25},{25,17},{2,10},{10... | collective-permute-start | bytes 196616 | tf_op jit(solution)/shard_map/ppermute | solution.py:814
  59.4 1.7 %collective-permute-start.20 = (f32[128,128]{1,0:T(8,128)S(1)}, f32[128,128]{1,0:T(8,128)S(1)}, u32[]{:S(2)}, u32[]{:S(2)}) collective-permute-start(f32[128,128]{1,0:T(8,128)S(1)} %get-tuple-element.124), channel_id=1, source_target_pairs={{0,16},{8,24},{16,0},{24,8},{1,17},{9,25},{17,1},{25,9},{2,18},{10... | collective-permute-start | bytes 196616 | tf_op jit(solution)/shard_map/ppermute | solution.py:814
  61.1 1.2 %collective-permute-start.21 = (f32[128,128]{1,0:T(8,128)S(1)}, f32[128,128]{1,0:T(8,128)S(1)}, u32[]{:S(2)}, u32[]{:S(2)}) collective-permute-start(f32[128,128]{1,0:T(8,128)S(1)} %get-tuple-element.125), channel_id=1, source_target_pairs={{0,24},{8,16},{16,8},{24,0},{1,25},{9,17},{17,9},{25,1},{2,26},{10... | collective-permute-start | bytes 196616 | tf_op jit(solution)/shard_map/ppermute | solution.py:814
  62.2 5.5 %pointwise_back.1.refs_6_ = f32[32,128,512]{2,1,0:T(8,128)S(1)} custom-call(bf16[32,32]{1,0:T(8,128)(2,1)S(1)} %copy-done.1, f32[32,128,512]{2,1,0:T(8,128)S(1)} %get-tuple-element.126.in_ref), custom_call_target="tpu_custom_call" | custom-call | flops 4000000000 | bytes 1048576 | tf_op jit(solution)/shard_map/pointwise_back/pallas_call | solution.py:674
  67.8 0.0 collective-permute-done.20.refs_2_
  67.8 2.2 %adjoint.1 = (f32[4,32,128]{2,1,0:T(8,128)S(1)}, f32[4,32,128]{2,1,0:T(8,128)S(1)}, f32[128,128]{1,0:T(8,128)S(1)}) custom-call(s32[2]{0:T(128)S(1)} %pad_add_fusion.place_ref, f32[256,128]{1,0:T(8,128)S(1)} %get-tuple-element.98.slots_ref, f32[128,128]{1,0:T(8,128)S(1)} %get-tuple-element.127.refs_0_, f32[128,128]{1,0:T(8,128)S(1)} %collective-permute-done.19.refs_1_, ...), custom_call_target="tpu_custom_call" | custom-call | flops 3000000000 | bytes 1048576 | tf_op jit(solution)/shard_map/adjoint/pallas_call | solution.py:554
  70.0 0.1 collective-permute-start.25
  70.0 1.1 %collective-permute-start.22 = (f32[128,128]{1,0:T(8,128)S(1)}, f32[128,128]{1,0:T(8,128)S(1)}, u32[]{:S(2)}, u32[]{:S(2)}) collective-permute-start(f32[128,128]{1,0:T(8,128)S(1)} %get-tuple-element.141.refs_0_), channel_id=1, source_target_pairs={{0,8},{8,0},{16,24},{24,16},{1,9},{9,1},{17,25},{25,17},{2,10},{10... | collective-permute-start | bytes 196616 | tf_op jit(solution)/shard_map/ppermute | solution.py:814
  71.1 2.2 %collective-permute-start.23 = (f32[128,128]{1,0:T(8,128)S(1)}, f32[128,128]{1,0:T(8,128)S(1)}, u32[]{:S(2)}, u32[]{:S(2)}) collective-permute-start(f32[128,128]{1,0:T(8,128)S(1)} %get-tuple-element.141.refs_0_), channel_id=1, source_target_pairs={{0,16},{8,24},{16,0},{24,8},{1,17},{9,25},{17,1},{25,9},{2,18},{10... | collective-permute-start | bytes 196616 | tf_op jit(solution)/shard_map/ppermute | solution.py:814
  73.3 1.2 %collective-permute-start.24 = (f32[128,128]{1,0:T(8,128)S(1)}, f32[128,128]{1,0:T(8,128)S(1)}, u32[]{:S(2)}, u32[]{:S(2)}) collective-permute-start(f32[128,128]{1,0:T(8,128)S(1)} %get-tuple-element.141.refs_0_), channel_id=1, source_target_pairs={{0,24},{8,16},{16,8},{24,0},{1,25},{9,17},{17,9},{25,1},{2,26},{10... | collective-permute-start | bytes 196616 | tf_op jit(solution)/shard_map/ppermute | solution.py:814
  74.5 0.6 collective-permute-start.26
  75.1 1.5 %collective-permute-start.27 = (f32[2,32,128]{2,1,0:T(8,128)S(1)}, f32[2,32,128]{2,1,0:T(8,128)S(1)}, u32[]{:S(2)}, u32[]{:S(2)}) collective-permute-start(f32[2,32,128]{2,1,0:T(8,128)S(1)} %get-tuple-element.148), channel_id=1, source_target_pairs={{0,4},{1,5},{2,6},{3,7},{4,0},{5,1},{6,2},{7,3},{8,12},{9,13},{10,... | collective-permute-start | bytes 98312 | tf_op jit(solution)/shard_map/ppermute | solution.py:814
  76.5 1.5 %collective-permute-start.28 = (f32[2,32,128]{2,1,0:T(8,128)S(1)}, f32[2,32,128]{2,1,0:T(8,128)S(1)}, u32[]{:S(2)}, u32[]{:S(2)}) collective-permute-start(f32[2,32,128]{2,1,0:T(8,128)S(1)} %get-tuple-element.149), channel_id=1, source_target_pairs={{0,6},{1,7},{2,4},{3,5},{4,2},{5,3},{6,0},{7,1},{8,14},{9,15},{10,... | collective-permute-start | bytes 98312 | tf_op jit(solution)/shard_map/ppermute | solution.py:814
  78.1 1.5 %collective-permute-done.23.refs_2_ = f32[128,128]{1,0:T(8,128)S(1)} collective-permute-done((f32[128,128]{1,0:T(8,128)S(1)}, f32[128,128]{1,0:T(8,128)S(1)}, u32[]{:S(2)}, u32[]{:S(2)}) %collective-permute-start.23) | collective-permute-done | bytes 65568 | tf_op jit(solution)/shard_map/ppermute | solution.py:814
  79.6 4.4 %finish.1 = f32[32,128,512]{2,1,0:T(8,128)} custom-call(f32[128,128]{1,0:T(8,128)S(1)} %get-tuple-element.141.refs_0_, f32[128,128]{1,0:T(8,128)S(1)} %collective-permute-done.22.refs_1_, f32[128,128]{1,0:T(8,128)S(1)} %collective-permute-done.23.refs_2_, f32[128,128]{1,0:T(8,128)S(1)} %collective-permute-done.24.refs_3_, ...), custom_call_target="tpu_custom_call" | custom-call | flops 4000000000 | bytes 1048576 | tf_op jit(solution)/shard_map/finish/pallas_call | solution.py:797
  84.0 2.9 %weight_grad.1 = f32[2,32,32,64]{3,2,1,0:T(8,128)} custom-call(s32[2]{0:T(128)S(1)} %pad_add_fusion.place_ref, f32[512,128]{1,0:T(8,128)S(1)} %get-tuple-element.143.kept_ref, f32[2,32,128]{2,1,0:T(8,128)S(1)} %get-tuple-element.146.refs_0_, f32[2,32,128]{2,1,0:T(8,128)S(1)} %collective-permute-done.26.refs_1_, ...), custom_call_target="tpu_custom_call" | custom-call | flops 2000000000 | bytes 1048576 | tf_op jit(solution)/shard_map/weight_grad/pallas_call | solution.py:454
  (24 shorter events, 0.1 us)
Async XLA Ops:
  2.4 8.5 %collective-permute-start = (f32[32,640]{1,0:T(8,128)}, f32[32,640]{1,0:T(8,128)S(1)}, u32[]{:S(2)}, u32[]{:S(2)}) collective-permute-start(f32[32,640]{1,0:T(8,128)} %pack.1.refs_0_), channel_id=1, source_target_pairs={{0,2},{1,3},{2,0},{3,1},{4,6},{5,7},{6,4},{7,5},{8,10},{9,11},{10,... | collective-permute-start | bytes 245768 | tf_op jit(solution)/shard_map/ppermute | solution.py:814
  5.4 5.5 %collective-permute-start.1 = (f32[32,640]{1,0:T(8,128)}, f32[32,640]{1,0:T(8,128)S(1)}, u32[]{:S(2)}, u32[]{:S(2)}) collective-permute-start(f32[32,640]{1,0:T(8,128)} %pack.1.refs_0_), channel_id=1, source_target_pairs={{0,4},{1,5},{2,6},{3,7},{4,0},{5,1},{6,2},{7,3},{8,12},{9,13},{10,... | collective-permute-start | bytes 245768 | tf_op jit(solution)/shard_map/ppermute | solution.py:814
  7.0 5.6 %collective-permute-start.2 = (f32[32,640]{1,0:T(8,128)}, f32[32,640]{1,0:T(8,128)S(1)}, u32[]{:S(2)}, u32[]{:S(2)}) collective-permute-start(f32[32,640]{1,0:T(8,128)} %pack.1.refs_0_), channel_id=1, source_target_pairs={{0,6},{1,7},{2,4},{3,5},{4,2},{5,3},{6,0},{7,1},{8,14},{9,15},{10,... | collective-permute-start | bytes 245768 | tf_op jit(solution)/shard_map/ppermute | solution.py:814
  7.0 1.2 %copy-start.4 = (f32[64,2,32,32]{0,3,2,1:T(8,128)S(1)}, f32[64,2,32,32]{0,3,2,1:T(8,128)}, u32[]{:S(2)}) copy-start(f32[64,2,32,32]{0,3,2,1:T(8,128)} %param.12) | copy-start | bytes 1572868
  8.2 0.7 copy-start.5
  8.9 0.7 copy-start.6
  9.5 27.8 %copy-start.2 = (bf16[32,1,128,512]{3,2,1,0:T(8,128)(2,1)S(1)}, bf16[32,1,128,512]{3,2,1,0:T(8,128)(2,1)}, u32[]{:S(2)}) copy-start(bf16[32,1,128,512]{3,2,1,0:T(8,128)(2,1)} %param.9) | copy-start | bytes 12582916
  10.9 26.4 %copy-start.1 = (bf16[32,32]{1,0:T(8,128)(2,1)S(1)}, bf16[32,32]{1,0:T(8,128)(2,1)}, u32[]{:S(2)}) copy-start(bf16[32,32]{1,0:T(8,128)(2,1)} %weight_ref.3) | copy-start | bytes 6148
  10.9 26.4 %copy-start.7 = (f32[32]{0:T(128)S(1)}, f32[32]{0:T(128)}, u32[]{:S(2)}) copy-start(f32[32]{0:T(128)} %bias_ref.1) | copy-start | bytes 388
  12.5 1.6 %collective-permute-start.3 = (f32[32,640]{1,0:T(8,128)}, f32[32,640]{1,0:T(8,128)S(1)}, u32[]{:S(2)}, u32[]{:S(2)}) collective-permute-start(f32[32,640]{1,0:T(8,128)} %pack.1.refs_0_), channel_id=1, source_target_pairs={{0,1},{1,0},{2,3},{3,2},{4,5},{5,4},{6,7},{7,6},{8,9},{9,8},{10,11... | collective-permute-start | bytes 245768 | tf_op jit(solution)/shard_map/ppermute | solution.py:814
  12.5 1.6 %collective-permute-start.4 = (f32[32,640]{1,0:T(8,128)S(1)}, f32[32,640]{1,0:T(8,128)S(1)}, u32[]{:S(2)}, u32[]{:S(2)}) collective-permute-start(f32[32,640]{1,0:T(8,128)S(1)} %collective-permute-done.refs_2_), channel_id=1, source_target_pairs={{0,1},{1,0},{2,3},{3,2},{4,5},{5,4},{6,7},{7,6},{8,9},{9,8},{10,11... | collective-permute-start | bytes 245768 | tf_op jit(solution)/shard_map/ppermute | solution.py:814
  13.0 1.3 %collective-permute-start.5 = (f32[32,640]{1,0:T(8,128)S(1)}, f32[32,640]{1,0:T(8,128)S(1)}, u32[]{:S(2)}, u32[]{:S(2)}) collective-permute-start(f32[32,640]{1,0:T(8,128)S(1)} %collective-permute-done.1.refs_4_), channel_id=1, source_target_pairs={{0,1},{1,0},{2,3},{3,2},{4,5},{5,4},{6,7},{7,6},{8,9},{9,8},{10,11... | collective-permute-start | bytes 245768 | tf_op jit(solution)/shard_map/ppermute | solution.py:814
  13.0 1.4 %collective-permute-start.6 = (f32[32,640]{1,0:T(8,128)S(1)}, f32[32,640]{1,0:T(8,128)S(1)}, u32[]{:S(2)}, u32[]{:S(2)}) collective-permute-start(f32[32,640]{1,0:T(8,128)S(1)} %collective-permute-done.2.refs_6_), channel_id=1, source_target_pairs={{0,1},{1,0},{2,3},{3,2},{4,5},{5,4},{6,7},{7,6},{8,9},{9,8},{10,11... | collective-permute-start | bytes 245768 | tf_op jit(solution)/shard_map/ppermute | solution.py:814
  14.5 15.8 %collective-permute-start.7 = (f32[1024,128]{1,0:T(8,128)S(1)}, f32[1024,128]{1,0:T(8,128)S(1)}, u32[]{:S(2)}, u32[]{:S(2)}) collective-permute-start(f32[1024,128]{1,0:T(8,128)S(1)} %get-tuple-element.131.packed_ref.refs_4_), channel_id=1, source_target_pairs={{0,2},{1,3},{2,0},{3,1},{4,6},{5,7},{6,4},{7,5},{8,10},{9,11},{10,... | collective-permute-start | bytes 1572872 | tf_op jit(solution)/shard_map/ppermute | solution.py:814
  15.0 15.3 %collective-permute-start.8 = (f32[1024,128]{1,0:T(8,128)S(1)}, f32[1024,128]{1,0:T(8,128)S(1)}, u32[]{:S(2)}, u32[]{:S(2)}) collective-permute-start(f32[1024,128]{1,0:T(8,128)S(1)} %get-tuple-element.131.packed_ref.refs_4_), channel_id=1, source_target_pairs={{0,4},{1,5},{2,6},{3,7},{4,0},{5,1},{6,2},{7,3},{8,12},{9,13},{10,... | collective-permute-start | bytes 1572872 | tf_op jit(solution)/shard_map/ppermute | solution.py:814
  16.4 0.9 %copy-start = (f32[32,640]{1,0:T(8,128)S(1)}, f32[32,640]{1,0:T(8,128)}, u32[]{:S(2)}) copy-start(f32[32,640]{1,0:T(8,128)} %pack.1.refs_0_) | copy-start | bytes 245764
  30.9 13.6 %copy-start.3 = (bf16[32,1,128,512]{3,2,1,0:T(8,128)(2,1)S(1)}, bf16[32,1,128,512]{3,2,1,0:T(8,128)(2,1)}, u32[]{:S(2)}) copy-start(bf16[32,1,128,512]{3,2,1,0:T(8,128)(2,1)} %param.10) | copy-start | bytes 12582916
  30.9 9.7 %collective-permute-start.10 = (f32[128,128]{1,0:T(8,128)S(1)}, f32[128,128]{1,0:T(8,128)S(1)}, u32[]{:S(2)}, u32[]{:S(2)}) collective-permute-start(f32[128,128]{1,0:T(8,128)S(1)} %to_modes.1.refs_0_), channel_id=1, source_target_pairs={{0,16},{8,24},{16,0},{24,8},{1,17},{9,25},{17,1},{25,9},{2,18},{10... | collective-permute-start | bytes 196616 | tf_op jit(solution)/shard_map/ppermute | solution.py:814
  33.5 7.1 %collective-permute-start.11 = (f32[128,128]{1,0:T(8,128)S(1)}, f32[128,128]{1,0:T(8,128)S(1)}, u32[]{:S(2)}, u32[]{:S(2)}) collective-permute-start(f32[128,128]{1,0:T(8,128)S(1)} %to_modes.1.refs_0_), channel_id=1, source_target_pairs={{0,24},{8,16},{16,8},{24,0},{1,25},{9,17},{17,9},{25,1},{2,26},{10... | collective-permute-start | bytes 196616 | tf_op jit(solution)/shard_map/ppermute | solution.py:814
  34.9 6.3 %collective-permute-start.9 = (f32[128,128]{1,0:T(8,128)S(1)}, f32[128,128]{1,0:T(8,128)S(1)}, u32[]{:S(2)}, u32[]{:S(2)}) collective-permute-start(f32[128,128]{1,0:T(8,128)S(1)} %to_modes.1.refs_0_), channel_id=1, source_target_pairs={{0,8},{8,0},{16,24},{24,16},{1,9},{9,1},{17,25},{25,17},{2,10},{10... | collective-permute-start | bytes 196616 | tf_op jit(solution)/shard_map/ppermute | solution.py:814
  35.2 7.6 %collective-permute-start.12 = (f32[512,128]{1,0:T(8,128)S(1)}, f32[512,128]{1,0:T(8,128)S(1)}, u32[]{:S(2)}, u32[]{:S(2)}) collective-permute-start(f32[512,128]{1,0:T(8,128)S(1)} %get-tuple-element.103), channel_id=1, source_target_pairs={{0,4},{1,5},{2,6},{3,7},{4,0},{5,1},{6,2},{7,3},{8,12},{9,13},{10,... | collective-permute-start | bytes 786440 | tf_op jit(solution)/shard_map/ppermute | solution.py:814
  36.6 7.3 %collective-permute-start.13 = (f32[512,128]{1,0:T(8,128)S(1)}, f32[512,128]{1,0:T(8,128)S(1)}, u32[]{:S(2)}, u32[]{:S(2)}) collective-permute-start(f32[512,128]{1,0:T(8,128)S(1)} %get-tuple-element.104), channel_id=1, source_target_pairs={{0,2},{1,3},{2,0},{3,1},{4,6},{5,7},{6,4},{7,5},{8,10},{9,11},{10,... | collective-permute-start | bytes 786440 | tf_op jit(solution)/shard_map/ppermute | solution.py:814
  40.6 17.1 %collective-permute-start.15 = (f32[1024,128]{1,0:T(8,128)S(1)}, f32[1024,128]{1,0:T(8,128)S(1)}, u32[]{:S(2)}, u32[]{:S(2)}) collective-permute-start(f32[1024,128]{1,0:T(8,128)S(1)} %collective-permute-done.7.first_ref.refs_6_), channel_id=1, source_target_pairs={{0,1},{1,0},{2,3},{3,2},{4,5},{5,4},{6,7},{7,6},{8,9},{9,8},{10,11... | collective-permute-start | bytes 1572872 | tf_op jit(solution)/shard_map/ppermute | solution.py:814
  40.7 17.1 %collective-permute-start.16 = (f32[1024,128]{1,0:T(8,128)S(1)}, f32[1024,128]{1,0:T(8,128)S(1)}, u32[]{:S(2)}, u32[]{:S(2)}) collective-permute-start(f32[1024,128]{1,0:T(8,128)S(1)} %collective-permute-done.8.second_ref.refs_8_), channel_id=1, source_target_pairs={{0,1},{1,0},{2,3},{3,2},{4,5},{5,4},{6,7},{7,6},{8,9},{9,8},{10,11... | collective-permute-start | bytes 1572872 | tf_op jit(solution)/shard_map/ppermute | solution.py:814
  41.2 16.5 %collective-permute-start.14 = (f32[1024,128]{1,0:T(8,128)S(1)}, f32[1024,128]{1,0:T(8,128)S(1)}, u32[]{:S(2)}, u32[]{:S(2)}) collective-permute-start(f32[1024,128]{1,0:T(8,128)S(1)} %get-tuple-element.131.packed_ref.refs_4_), channel_id=1, source_target_pairs={{0,1},{1,0},{2,3},{3,2},{4,5},{5,4},{6,7},{7,6},{8,9},{9,8},{10,11... | collective-permute-start | bytes 1572872 | tf_op jit(solution)/shard_map/ppermute | solution.py:814
  43.9 13.8 %collective-permute-start.17 = (f32[512,128]{1,0:T(8,128)S(1)}, f32[512,128]{1,0:T(8,128)S(1)}, u32[]{:S(2)}, u32[]{:S(2)}) collective-permute-start(f32[512,128]{1,0:T(8,128)S(1)} %collective-permute-done.12.refs_10_), channel_id=1, source_target_pairs={{0,1},{1,0},{2,3},{3,2},{4,5},{5,4},{6,7},{7,6},{8,9},{9,8},{10,11... | collective-permute-start | bytes 786440 | tf_op jit(solution)/shard_map/ppermute | solution.py:814
  43.9 13.9 %collective-permute-start.18 = (f32[512,128]{1,0:T(8,128)S(1)}, f32[512,128]{1,0:T(8,128)S(1)}, u32[]{:S(2)}, u32[]{:S(2)}) collective-permute-start(f32[512,128]{1,0:T(8,128)S(1)} %collective-permute-done.13.refs_12_), channel_id=1, source_target_pairs={{0,1},{1,0},{2,3},{3,2},{4,5},{5,4},{6,7},{7,6},{8,9},{9,8},{10,11... | collective-permute-start | bytes 786440 | tf_op jit(solution)/shard_map/ppermute | solution.py:814
  57.8 10.0 %collective-permute-start.19 = (f32[128,128]{1,0:T(8,128)S(1)}, f32[128,128]{1,0:T(8,128)S(1)}, u32[]{:S(2)}, u32[]{:S(2)}) collective-permute-start(f32[128,128]{1,0:T(8,128)S(1)} %get-tuple-element.123), channel_id=1, source_target_pairs={{0,8},{8,0},{16,24},{24,16},{1,9},{9,1},{17,25},{25,17},{2,10},{10... | collective-permute-start | bytes 196616 | tf_op jit(solution)/shard_map/ppermute | solution.py:814
  59.4 8.4 %collective-permute-start.20 = (f32[128,128]{1,0:T(8,128)S(1)}, f32[128,128]{1,0:T(8,128)S(1)}, u32[]{:S(2)}, u32[]{:S(2)}) collective-permute-start(f32[128,128]{1,0:T(8,128)S(1)} %get-tuple-element.124), channel_id=1, source_target_pairs={{0,16},{8,24},{16,0},{24,8},{1,17},{9,25},{17,1},{25,9},{2,18},{10... | collective-permute-start | bytes 196616 | tf_op jit(solution)/shard_map/ppermute | solution.py:814
  61.1 6.7 %collective-permute-start.21 = (f32[128,128]{1,0:T(8,128)S(1)}, f32[128,128]{1,0:T(8,128)S(1)}, u32[]{:S(2)}, u32[]{:S(2)}) collective-permute-start(f32[128,128]{1,0:T(8,128)S(1)} %get-tuple-element.125), channel_id=1, source_target_pairs={{0,24},{8,16},{16,8},{24,0},{1,25},{9,17},{17,9},{25,1},{2,26},{10... | collective-permute-start | bytes 196616 | tf_op jit(solution)/shard_map/ppermute | solution.py:814
  70.0 4.5 %collective-permute-start.25 = (f32[4,32,128]{2,1,0:T(8,128)S(1)}, f32[4,32,128]{2,1,0:T(8,128)S(1)}, u32[]{:S(2)}, u32[]{:S(2)}) collective-permute-start(f32[4,32,128]{2,1,0:T(8,128)S(1)} %get-tuple-element.145), channel_id=1, source_target_pairs={{0,1},{1,0},{2,3},{3,2},{4,5},{5,4},{6,7},{7,6},{8,9},{9,8},{10,11... | collective-permute-start | bytes 196616 | tf_op jit(solution)/shard_map/ppermute | solution.py:814
  70.0 6.5 %collective-permute-start.22 = (f32[128,128]{1,0:T(8,128)S(1)}, f32[128,128]{1,0:T(8,128)S(1)}, u32[]{:S(2)}, u32[]{:S(2)}) collective-permute-start(f32[128,128]{1,0:T(8,128)S(1)} %get-tuple-element.141.refs_0_), channel_id=1, source_target_pairs={{0,8},{8,0},{16,24},{24,16},{1,9},{9,1},{17,25},{25,17},{2,10},{10... | collective-permute-start | bytes 196616 | tf_op jit(solution)/shard_map/ppermute | solution.py:814
  71.1 8.4 %collective-permute-start.23 = (f32[128,128]{1,0:T(8,128)S(1)}, f32[128,128]{1,0:T(8,128)S(1)}, u32[]{:S(2)}, u32[]{:S(2)}) collective-permute-start(f32[128,128]{1,0:T(8,128)S(1)} %get-tuple-element.141.refs_0_), channel_id=1, source_target_pairs={{0,16},{8,24},{16,0},{24,8},{1,17},{9,25},{17,1},{25,9},{2,18},{10... | collective-permute-start | bytes 196616 | tf_op jit(solution)/shard_map/ppermute | solution.py:814
  73.3 6.3 %collective-permute-start.24 = (f32[128,128]{1,0:T(8,128)S(1)}, f32[128,128]{1,0:T(8,128)S(1)}, u32[]{:S(2)}, u32[]{:S(2)}) collective-permute-start(f32[128,128]{1,0:T(8,128)S(1)} %get-tuple-element.141.refs_0_), channel_id=1, source_target_pairs={{0,24},{8,16},{16,8},{24,0},{1,25},{9,17},{17,9},{25,1},{2,26},{10... | collective-permute-start | bytes 196616 | tf_op jit(solution)/shard_map/ppermute | solution.py:814
  74.5 9.5 %collective-permute-start.26 = (f32[2,32,128]{2,1,0:T(8,128)S(1)}, f32[2,32,128]{2,1,0:T(8,128)S(1)}, u32[]{:S(2)}, u32[]{:S(2)}) collective-permute-start(f32[2,32,128]{2,1,0:T(8,128)S(1)} %get-tuple-element.147), channel_id=1, source_target_pairs={{0,2},{1,3},{2,0},{3,1},{4,6},{5,7},{6,4},{7,5},{8,10},{9,11},{10,... | collective-permute-start | bytes 98312 | tf_op jit(solution)/shard_map/ppermute | solution.py:814
  75.1 8.9 %collective-permute-start.27 = (f32[2,32,128]{2,1,0:T(8,128)S(1)}, f32[2,32,128]{2,1,0:T(8,128)S(1)}, u32[]{:S(2)}, u32[]{:S(2)}) collective-permute-start(f32[2,32,128]{2,1,0:T(8,128)S(1)} %get-tuple-element.148), channel_id=1, source_target_pairs={{0,4},{1,5},{2,6},{3,7},{4,0},{5,1},{6,2},{7,3},{8,12},{9,13},{10,... | collective-permute-start | bytes 98312 | tf_op jit(solution)/shard_map/ppermute | solution.py:814
  76.5 7.5 %collective-permute-start.28 = (f32[2,32,128]{2,1,0:T(8,128)S(1)}, f32[2,32,128]{2,1,0:T(8,128)S(1)}, u32[]{:S(2)}, u32[]{:S(2)}) collective-permute-start(f32[2,32,128]{2,1,0:T(8,128)S(1)} %get-tuple-element.149), channel_id=1, source_target_pairs={{0,6},{1,7},{2,4},{3,5},{4,2},{5,3},{6,0},{7,1},{8,14},{9,15},{10,... | collective-permute-start | bytes 98312 | tf_op jit(solution)/shard_map/ppermute | solution.py:814
where the time goes:
time: 87.2 us; the launch traced here: 86.9 us
  Pallas kernels  38.1 us (44%)
  starting transfers between devices  27.6 us (32%)
  blocking collectives  10.1 us (12%)
  waiting for transfers between devices  6.71 us (8%)
  local copies, waits for them, and re-layouts  3.44 us (4%)
  between operations  0.89 us (1%)
    ppermute x29, starting transfers between devices, exchange(): return lax.ppermute(piece, axis, [(i, i ^ flip) for i in range(count)])  27.6 us
    pallas_call x1, Pallas kernels, slope_step(): pl.pallas_call(functools.partial(slope_kernel, blocks=blocks), out_shape=...  13.3 us
    all_to_all x1, blocking collectives, on_device_packed(): mixed = lax.all_to_all(mixed, 'py', split_axis=0, concat_axis=0, tiled=True)  10.1 us
    ppermute x29, waiting for transfers between devices, exchange(): return lax.ppermute(piece, axis, [(i, i ^ flip) for i in range(count)])  6.71 us
    pallas_call x1, Pallas kernels, pointwise_back(): pl.pallas_call(pointwise_back_kernel, out_shape=jax.ShapeDtypeStruct(valu...  5.49 us
    pallas_call x1, Pallas kernels, finish(): pl.pallas_call(functools.partial(finish_kernel, blocks=blocks, group=grou...  4.4 us
    unnamed x16, local copies, waits for them, and re-layouts  3.44 us
    pallas_call x1, Pallas kernels, pointwise_map(): pl.pallas_call(pointwise_kernel, out_shape=jax.ShapeDtypeStruct(values.sh...  3.29 us
  transfers between devices with their start and end apart: 29, of which 8 were waited for; matrix products, arithmetic and copies ran while one was open for 0% of the time, Pallas kernels for 35%

commit v1 on v0

--- a/solution.py
+++ b/solution.py
@@ -161,6 +161,10 @@
     return (field_grad, store_grad)
 
 
+def place_of():
+    return lax.axis_index("px"), lax.axis_index("py")
+
+
 def split(values):
     high = values.astype(jnp.bfloat16)
     return high, (values - high.astype(jnp.float32)).astype(jnp.bfloat16)
@@ -202,61 +206,64 @@
     return [pl.BlockSpec(memory_space=pltpu.SMEM)] * count
 
 
-BEND_TERMS = (
-    0.7978849414899104,
-    0.03633308440863974,
-    -3.2594744583983906e-05,
-    -5.5306316703040985e-05,
-    3.964773129084329e-06,
-    -1.322662760933859e-07,
-    1.7562773353616594e-09,
-)
 DENSITY = math.sqrt(2.0 / math.pi)
 
 
 def twice_gelu_slope(scaled):
-    square = scaled * scaled
-    total = BEND_TERMS[-1] / DENSITY ** (2 * len(BEND_TERMS) - 1)
-    for power in range(len(BEND_TERMS) - 2, -1, -1):
-        total = total * square + BEND_TERMS[power] / DENSITY ** (2 * power + 1)
-    bell = jnp.exp2(square * (-0.5 * math.log2(math.e) / DENSITY**2))
-    return (1.0 + jnp.tanh(scaled * total)) + scaled * bell
-
-
-def column_of(ref, start, count, rows):
-    shape = (rows, 128)
-    row = rows_of(shape) % count
-    out = jnp.zeros(shape, jnp.int32)
+    normal = 1.0 + lax.erf(scaled * (math.sqrt(0.5) / DENSITY))
+    return normal + scaled * jnp.exp2(scaled * scaled * (-0.5 * math.log2(math.e) / DENSITY**2))
+
+
+def column_of(ref, start, count):
+    shape = (count, 128)
+    row = rows_of(shape)
+    out = jnp.zeros(shape, ref.dtype)
     for i in range(count):
         out = jnp.where(row == i, ref[start(i)], out)
     return out
 
 
 def prepare_kernel(
-    place_ref, ky_ref, kx_ref, store_ref, ti_ref, tf_ref, xi_ref, xf_ref, packed_ref, *, full_x, count_x, count_y
+    small_ref,
+    store_ref,
+    piece_ref,
+    ti_ref,
+    tf_ref,
+    xi_ref,
+    xf_ref,
+    packed_ref,
+    map_ref,
+    back_ref,
+    shift_ref,
+    kept_ref,
+    *,
+    full_x,
+    modes_y,
+    modes_x,
 ):
-    for channel in range(store_ref.shape[1]):
-        rows = pl.ds(channel * store_ref.shape[2], store_ref.shape[2])
-        packed_ref[rows] = jnp.concatenate([store_ref[0, channel], store_ref[1, channel]], 1)
-    modes_y, width = ky_ref.shape[0], tf_ref.shape[1]
-    modes_x, rows_x = kx_ref.shape[0], xf_ref.shape[0] // 4
-    local_y = modes_y // count_x
+    kept_ref[...] = piece_ref[...]
+    channels, width = store_ref.shape[1], tf_ref.shape[1]
+    rows = map_ref.shape[0] // channels
+    ky = small_ref[pl.ds(0, modes_y)].astype(jnp.int32)
+    kx = small_ref[pl.ds(modes_y, modes_x)].astype(jnp.int32)
+    bias = small_ref[pl.ds(modes_y + modes_x, channels)] * DENSITY
+    weight = small_ref[pl.ds(modes_y + modes_x + channels, channels), :][:, :channels].astype(jnp.bfloat16)
+    map_ref[...] = spread(weight, rows, 1, lambda i: i).astype(jnp.bfloat16)
+    pairs = channels // 4
+    back = spread(weight, rows, 0, lambda i: i % 2 * 2 * pairs + i // 2 % pairs * 2 + i // (2 * pairs))
+    back_ref[...] = (0.5 * back).astype(jnp.bfloat16)
+    for channel in range(channels):
+        shift_ref[pl.ds(channel * rows, rows)] = jnp.broadcast_to(bias[channel : channel + 1], (rows, bias.shape[1]))
+        packed = jnp.concatenate([store_ref[0, channel], store_ref[1, channel]], 1)
+        packed_ref[pl.ds(channel * store_ref.shape[2], store_ref.shape[2])] = packed
+    rows_x = xf_ref.shape[0] // 4
     factor = 1.0 / math.sqrt(full_x * width)
-    place = place_ref[0]
-    start = place * rows_x
-    local_x = modes_x // count_y
+    start = place_of()[0] * rows_x
 
     def angles(modes, points, length):
         return ((modes * points) & (length - 1)).astype(jnp.float32) * (2.0 * math.pi / length)
 
-    def ky_at(i):
-        return (place ^ (i // local_y)) * local_y + i % local_y
-
-    def kx_at(i):
-        return (place_ref[1] ^ (i // local_x)) * local_x + i % local_x
-
-    ky = column_of(ky_ref, ky_at, modes_y, modes_y)
-    ky = jnp.concatenate([ky] * (width // 128), 1)
+    ky = jnp.concatenate([ky] * (width // ky.shape[1]), 1)
     angle = angles(ky, lanes_of(ky.shape), width)
     waves = jnp.concatenate([jnp.cos(angle), -jnp.sin(angle)], 0)
     high, low = split(waves)
@@ -264,63 +271,67 @@
     for index, scale in enumerate((DENSITY, 1.0)):
         high, low = split(scale * waves)
         ti_ref[index] = jnp.concatenate([high, high, low, jnp.zeros_like(low)], 0)
-    kx = column_of(kx_ref, kx_at, modes_x, modes_x)
     angle = angles(kx, start + lanes_of((modes_x, rows_x)), full_x)
     cos, sin, zero = factor * jnp.cos(angle), factor * jnp.sin(angle), jnp.zeros_like(angle)
-    rows = [[cos, sin, zero, zero], [-sin, cos, zero, zero], [zero, zero, cos, sin], [zero, zero, -sin, cos]]
-    high, low = split(jnp.concatenate([jnp.concatenate(row, 1) for row in rows], 0))
+    parts = [[cos, sin, zero, zero], [-sin, cos, zero, zero], [zero, zero, cos, sin], [zero, zero, -sin, cos]]
+    high, low = split(jnp.concatenate([jnp.concatenate(part, 1) for part in parts], 0))
     xi_ref[...] = jnp.concatenate([high, high, low], 0)
-    shape = (rows_x, 4 * modes_x)
-    kx = jnp.transpose(column_of(kx_ref, kx_at, modes_x, 4 * modes_x))
-    angle = angles(kx, start + rows_of(shape), full_x)
-    cos, sin, zero = 0.5 * factor * jnp.cos(angle), 0.5 * factor * jnp.sin(angle), jnp.zeros_like(angle)
-    lane = lanes_of(shape)
+    cos = 0.5 * jnp.transpose(jnp.concatenate([cos] * 4, 0))
+    sin = 0.5 * jnp.transpose(jnp.concatenate([sin] * 4, 0))
+    zero = jnp.zeros_like(cos)
+    lane = lanes_of(cos.shape)
     real = (lane // modes_x) % 2 == 0
     first = lane < 2 * modes_x
     from_re, from_im = jnp.where(real, cos, -sin), jnp.where(real, sin, cos)
-    rows = [
+    parts = [
         jnp.where(first, from_re, zero),
         jnp.where(first, from_im, zero),
         jnp.where(first, zero, from_re),
         jnp.where(first, zero, from_im),
     ]
-    high, low = split(jnp.concatenate(rows, 0))
+    high, low = split(jnp.concatenate(parts, 0))
     xf_ref[...] = jnp.concatenate([high, low], 1)
 
 
-def prepare(place, ky, kx, store, full_x, rows_x, width, count_y):
-    modes_y, modes_x = ky.shape[0], kx.shape[0]
+def prepare(small, store, piece, full_x, rows_x, width, modes_y, modes_x, rows=8):
+    channels, capacity = store.shape[2:]
     shapes = (
         (2, 4 * 2 * modes_y, width),
         (2 * 2 * modes_y, width),
         (3 * 4 * modes_x, 4 * rows_x),
         (4 * rows_x, 8 * modes_x),
-    )
-    return pl.pallas_call(
-        functools.partial(prepare_kernel, full_x=full_x, count_x=full_x // rows_x, count_y=count_y),
-        out_shape=[jax.ShapeDtypeStruct(shape, jnp.bfloat16) for shape in shapes]
-        + [jax.ShapeDtypeStruct((store.shape[1] * store.shape[2], 2 * store.shape[3]), jnp.float32)],
-        in_specs=scalars(3) + whole(1),
-        out_specs=whole(5),
+        (channels * channels, 2 * capacity),
+        (channels * rows, channels * rows),
+        (channels * rows, channels * rows),
+        (channels * rows, small.shape[1]),
+        piece.shape,
+    )
+    types = [jnp.float32 if i in (4, 7, 8) else jnp.bfloat16 for i in range(len(shapes))]
+    *tables, packed, full_map, full_back, shift, piece = pl.pallas_call(
+        functools.partial(prepare_kernel, full_x=full_x, modes_y=modes_y, modes_x=modes_x),
+        out_shape=[jax.ShapeDtypeStruct(*each) for each in zip(shapes, types)],
+        in_specs=whole(3),
+        out_specs=whole(len(shapes)),
         compiler_params=params(),
         cost_estimate=takes(2),
         name="prepare",
-    )(place, ky, kx, store)
+    )(small, store, piece)
+    return tables, packed, full_map, full_back, shift, piece
 
 
 def duplicate(values):
     return jnp.concatenate([values, values], -1)
 
 
-def pack_kernel(slots_hbm, spec_hbm, out_ref, slots_ref, spec_ref, sems):
-    copies = [
-        pltpu.make_async_copy(slots_hbm, slots_ref, sems.at[0]),
-        pltpu.make_async_copy(spec_hbm, spec_ref, sems.at[1]),
-    ]
+def pack_kernel(*refs):
+    sources, (out_ref, small_ref), (*targets, sems) = refs[:6], refs[6:8], refs[8:]
+    copies = [pltpu.make_async_copy(*pair, sems.at[i]) for i, pair in enumerate(zip(sources, targets))]
     for copy in copies:
         copy.start()
     for copy in copies:
         copy.wait()
+    slots_ref, spec_ref, ky_ref, kx_ref, bias_ref, weight_ref = targets
+    place_x, place_y = place_of()
     local_x, local_y = slots_ref.shape
     modes = local_x * local_y
     groups = spec_ref.shape[0] // modes
@@ -328,35 +339,44 @@
     for group in range(groups // 2):
         for part in range(2):
             columns.append(spec_ref[pl.ds(group * 2 * modes + part, modes, stride=2)])
-    shape = (modes, out_ref.shape[1] - groups * spec_ref.shape[1])
-    row = rows_of(shape)
-    numbers = jnp.zeros(shape, jnp.int32)
-    for mode in range(modes):
-        numbers = jnp.where(row == mode, slots_ref[mode % local_x, mode // local_x], numbers)
+    lanes = out_ref.shape[1] - groups * spec_ref.shape[1]
+    numbers = column_of(slots_ref, lambda i: (i % local_x, i // local_x), modes)
     out_ref[...] = jnp.concatenate(columns + [numbers.astype(jnp.float32)], 1)
-
-
-def pack(slots, spectrum, lanes):
+    modes_y, modes_x, channels = ky_ref.shape[0], kx_ref.shape[0], bias_ref.shape[0]
+    ky = column_of(ky_ref, lambda i: (place_x ^ (i // local_y)) * local_y + i % local_y, modes_y)
+    kx = column_of(kx_ref, lambda i: (place_y ^ (i // local_x)) * local_x + i % local_x, modes_x)
+    bias = column_of(bias_ref, lambda i: i, channels)
+    weight = weight_ref[...].astype(jnp.float32)
+    weight = jnp.concatenate([weight, jnp.zeros((channels, lanes - channels), jnp.float32)], 1)
+    small_ref[...] = jnp.concatenate([ky.astype(jnp.float32), kx.astype(jnp.float32), bias, weight], 0)
+
+
+def pack(slots, spectrum, ky, kx, bias, weight, lanes):
     modes = slots.size
     width = spectrum.size // modes + lanes
+    sources = (slots, spectrum, ky, kx, bias, weight)
+    held = (pltpu.SMEM, pltpu.VMEM, pltpu.SMEM, pltpu.SMEM, pltpu.SMEM, pltpu.VMEM)
+    rows = ky.shape[0] + kx.shape[0] + bias.shape[0] + weight.shape[0]
     return pl.pallas_call(
         pack_kernel,
-        out_shape=jax.ShapeDtypeStruct((modes, width), jnp.float32),
-        in_specs=outside(2),
-        out_specs=whole(1)[0],
-        scratch_shapes=[
-            pltpu.SMEM(slots.shape, slots.dtype),
-            pltpu.VMEM(spectrum.shape, spectrum.dtype),
-            pltpu.SemaphoreType.DMA((2,)),
+        out_shape=[
+            jax.ShapeDtypeStruct((modes, width), jnp.float32),
+            jax.ShapeDtypeStruct((rows, lanes), jnp.float32),
         ],
+        in_specs=outside(6),
+        out_specs=whole(2),
+        scratch_shapes=[space(each.shape, each.dtype) for space, each in zip(held, sources)]
+        + [pltpu.SemaphoreType.DMA((6,))],
         compiler_params=params(60),
         name="pack",
-    )(slots, spectrum)
-
-
-def mix_kernel(place_ref, packed_ref, *refs, count, local_x):
-    pieces, (kept_ref, slots_ref, out_ref, ra_ref, rb_ref, uc_ref, ud_ref) = refs[:count], refs[count:]
+    )(*sources)
+
+
+def mix_kernel(packed_ref, *refs, count, local_x):
+    pieces, refs = refs[:count], refs[count:]
+    kept_ref, slots_ref, same_ref, other_ref, out_ref, ra_ref, rb_ref, uc_ref, ud_ref = refs
     planes, channels, lanes = out_ref.shape
+    place = place_of()[1]
     capacity = lanes // 2
     wide = pieces[0].shape[1] - lanes
     local_y = pieces[0].shape[0] // local_x
@@ -365,7 +385,7 @@
             rows = pl.ds((mode * count + index) * local_x, local_x)
             slots_ref[rows] = piece[pl.ds(mode * local_x, local_x), pl.ds(wide, lanes)]
     numbers = jnp.transpose(jnp.concatenate([piece[:, pl.ds(wide, lanes)] for piece in pieces], 0))
-    wanted = (place_ref[1] * capacity + rows_of(numbers.shape) % capacity).astype(jnp.float32)
+    wanted = (place * capacity + rows_of(numbers.shape) % capacity).astype(jnp.float32)
     chosen = (numbers == wanted).astype(jnp.bfloat16)
     high, low = split(jnp.concatenate([piece[:, pl.ds(0, wide)] for piece in pieces], 0))
     placed = jnp.transpose(dot(chosen, high) + dot(chosen, low))
@@ -395,12 +415,14 @@
         )
 
     zero = jnp.zeros((channels, lanes), jnp.float32)
-    sums = lax.fori_loop(0, channels, step, (zero,) * planes)
+    sums = lax.fori_loop(0, channels, step, (zero,) * planes, unroll=4)
     for plane in range(planes):
         out_ref[plane] = sums[plane]
-
-
-def mix(place, packed, pieces, planes, local_x):
+    for step in range(planes):
+        (other_ref if step % 2 else same_ref)[step // 2] = out_ref[place ^ step]
+
+
+def mix(packed, pieces, planes, local_x):
     channels, lanes = math.isqrt(packed.shape[0]), packed.shape[1]
     count = len(pieces)
     return pl.pallas_call(
@@ -408,16 +430,18 @@
         out_shape=[
             jax.ShapeDtypeStruct((2 * planes * channels, lanes), jnp.float32),
             jax.ShapeDtypeStruct((count * pieces[0].shape[0], lanes), jnp.float32),
-            jax.ShapeDtypeStruct((planes, channels, lanes), jnp.float32),
+            jax.ShapeDtypeStruct((planes // 2, channels, lanes), jnp.float32),
+            jax.ShapeDtypeStruct((planes // 2, channels, lanes), jnp.float32),
         ],
-        in_specs=scalars(1) + whole(1 + count),
-        out_specs=whole(3),
-        scratch_shapes=[pltpu.VMEM((channels * channels, lanes), jnp.float32)] * 2
+        in_specs=whole(1 + count),
+        out_specs=whole(4),
+        scratch_shapes=[pltpu.VMEM((planes, channels, lanes), jnp.float32)]
+        + [pltpu.VMEM((channels * channels, lanes), jnp.float32)] * 2
         + [pltpu.VMEM((planes * channels, lanes), jnp.float32)] * 2,
         compiler_params=params(),
         cost_estimate=takes(3),
         name="mix",
-    )(place, packed, *pieces)
+    )(packed, *pieces)
 
 
 def swap_halves(values):
@@ -425,8 +449,8 @@
     return jnp.concatenate([values[..., half:], values[..., :half]], -1)
 
 
-def weight_grad_kernel(place_ref, kept_ref, *refs):
-    *pairs, out_ref, gs_ref = refs
+def weight_grad_kernel(kept_ref, *refs):
+    *pairs, out_ref, gs_ref, sum_ref, sems = refs
     grads = [each.at[core] for each in pairs for core in range(2)]
     channels, lanes = grads[0].shape
     capacity = lanes // 2
@@ -434,33 +458,51 @@
     for index, grad in enumerate(grads):
         swapped = swap_halves(grad[...])
         gs_ref[index] = jnp.where(lanes_of(swapped.shape) < capacity, swapped, -swapped)
-        starts.append((place_ref[1] ^ index) * 2 * channels)
-
-    def step(channel, carry):
-        total = jnp.zeros((channels, lanes), jnp.float32)
+        starts.append((place_of()[1] ^ index) * 2 * channels)
+    chunks = sems.shape[0]
+    size = channels // chunks
+
+    def send(chunk):
+        rows = pl.ds(chunk * size, size)
+        return pltpu.make_async_copy(sum_ref.at[:, rows], out_ref.at[:, rows], sems.at[chunk])
+
+    def step(pair, carry):
+        totals = [jnp.zeros((channels, lanes), jnp.float32)] * 2
         for index, start in enumerate(starts):
             real = kept_ref[pl.ds(start, channels)]
             imag = kept_ref[pl.ds(start + channels, channels)]
-            total = total + real * grads[index][pl.ds(channel, 1)] + imag * gs_ref[index, pl.ds(channel, 1)]
-        out_ref[0, channel] = total[:, :capacity]
-        out_ref[1, channel] = total[:, capacity:]
+            for each in range(2):
+                row = pl.ds(2 * pair + each, 1)
+                totals[each] = totals[each] + real * grads[index][row] + imag * gs_ref[index, row]
+        for each, total in enumerate(totals):
+            sum_ref[0, 2 * pair + each] = total[:, :capacity]
+            sum_ref[1, 2 * pair + each] = total[:, capacity:]
         return carry
 
-    lax.fori_loop(0, channels, step, 0, unroll=4)
-
-
-def weight_grad(place, kept, pairs):
+    for chunk in range(chunks):
+        lax.fori_loop(chunk * size // 2, (chunk + 1) * size // 2, step, 0, unroll=2)
+        send(chunk).start()
+    for chunk in range(chunks):
+        send(chunk).wait()
+
+
+def weight_grad(kept, pairs, chunks=4):
     _, channels, lanes = pairs[0].shape
+    shape = (2, channels, channels, lanes // 2)
     return pl.pallas_call(
         weight_grad_kernel,
-        out_shape=jax.ShapeDtypeStruct((2, channels, channels, lanes // 2), jnp.float32),
-        in_specs=scalars(1) + whole(1 + len(pairs)),
-        out_specs=whole(1)[0],
-        scratch_shapes=[pltpu.VMEM((2 * len(pairs), channels, lanes), jnp.float32)],
+        out_shape=jax.ShapeDtypeStruct(shape, jnp.float32),
+        in_specs=whole(1 + len(pairs)),
+        out_specs=outside(1)[0],
+        scratch_shapes=[
+            pltpu.VMEM((2 * len(pairs), channels, lanes), jnp.float32),
+            pltpu.VMEM(shape, jnp.float32),
+            pltpu.SemaphoreType.DMA((chunks,)),
+        ],
         compiler_params=params(),
         cost_estimate=takes(2),
         name="weight_grad",
-    )(place, kept, *pairs)
+    )(kept, *pairs)
 
 
 def fill_selection(slots_ref, chosen_ref, modes_x, capacity, flip=0):
@@ -490,33 +532,35 @@
         out_ref[pl.ds(mode, half, stride=local_y)] = jnp.concatenate([piece[:half], piece[half:]], 1)
 
 
-def to_modes_kernel(slots_ref, in_ref, out_ref, chosen_ref, *, modes_x):
-    owners, _, lanes = in_ref.shape
-    fill_selection(slots_ref, chosen_ref, modes_x, lanes // 2)
-    slots_to_modes([in_ref[owner] for owner in range(owners)], chosen_ref, out_ref, modes_x)
-
-
-def to_modes(slots, values, modes_x):
-    owners, channels, lanes = values.shape
+def to_modes_kernel(slots_ref, *refs, modes_x):
+    *pairs, out_ref, chosen_ref = refs
+    lanes = pairs[0].shape[2]
+    fill_selection(slots_ref, chosen_ref, modes_x, lanes // 2, place_of()[1])
+    slots_to_modes([pair[core] for pair in pairs for core in range(2)], chosen_ref, out_ref, modes_x)
+
+
+def to_modes(slots, pairs, modes_x):
+    _, channels, lanes = pairs[0].shape
     local_y = slots.shape[0] // modes_x
     return pl.pallas_call(
         functools.partial(to_modes_kernel, modes_x=modes_x),
         out_shape=jax.ShapeDtypeStruct((channels // 2 * local_y, 4 * modes_x), jnp.float32),
-        in_specs=whole(2),
+        in_specs=whole(1 + len(pairs)),
         out_specs=whole(1)[0],
-        scratch_shapes=[pltpu.VMEM((2 * slots.shape[0], owners * lanes), jnp.bfloat16)],
+        scratch_shapes=[pltpu.VMEM((2 * slots.shape[0], 2 * len(pairs) * lanes), jnp.bfloat16)],
         compiler_params=params(),
         cost_estimate=takes(1),
         name="to_modes",
-    )(slots, values)
-
-
-def adjoint_kernel(place_ref, slots_ref, *refs, modes_x, blocks, count):
-    pieces, stores, refs = refs[:blocks], refs[blocks : -5], refs[-5:]
+    )(slots, *pairs)
+
+
+def adjoint_kernel(slots_ref, *refs, modes_x, blocks, count):
+    pieces, stores, refs = refs[:blocks], refs[blocks:-5], refs[-5:]
+    place = place_of()[1]
     same_ref, other_ref, out_ref, chosen_ref, sum_ref = refs
     _, channels, lanes = same_ref.shape
     half = channels // 2
-    fill_selection(slots_ref, chosen_ref, modes_x, lanes // 2, place_ref[1])
+    fill_selection(slots_ref, chosen_ref, modes_x, lanes // 2, place)
     sum_ref[...] = sum(piece[...] for piece in pieces)
     local_y = sum_ref.shape[0] // half
     columns = []
@@ -536,8 +580,7 @@
         for channel in range(channels):
             store, row = stores[owner], channel
             if owner >= count - 2:
-                store = stores[owner + (2 if channel >= half else 0)]
-                row = channel % half
+                store, row = stores[owner + channel // half * 2], channel % half
             block = store[pl.ds(row * channels, channels)]
             real = real + block * values[channel : channel + 1]
             imag = imag + block * swapped[channel : channel + 1]
@@ -547,7 +590,7 @@
     slots_to_modes(mixed, chosen_ref, out_ref, modes_x)
 
 
-def adjoint(place, slots, pieces, stores, modes_x):
+def adjoint(slots, pieces, stores, modes_x):
     count, blocks = len(stores) - 2, len(pieces)
     lanes = stores[0].shape[1]
     channels = 2 * pieces[0].shape[0] * modes_x // slots.shape[0]
@@ -555,7 +598,7 @@
         functools.partial(adjoint_kernel, modes_x=modes_x, blocks=blocks, count=count),
         out_shape=[jax.ShapeDtypeStruct((count // 2, channels, lanes), jnp.float32)] * 2
         + [jax.ShapeDtypeStruct(pieces[0].shape, jnp.float32)],
-        in_specs=scalars(1) + whole(1 + blocks + len(stores)),
+        in_specs=whole(1 + blocks + len(stores)),
         out_specs=whole(3),
         scratch_shapes=[
             pltpu.VMEM((2 * slots.shape[0], count * lanes), jnp.bfloat16),
@@ -564,7 +607,7 @@
         compiler_params=params(),
         cost_estimate=takes(3),
         name="adjoint",
-    )(place, slots, *pieces, *stores)
+    )(slots, *pieces, *stores)
 
 
 def pair_kernel(same_ref, other_ref, *outs):
@@ -604,83 +647,79 @@
     )(first, second)
 
 
-def spread(small, rows, axis):
+def spread(small, rows, axis, channel_of):
     count = small.shape[0]
     shape = (count * rows, count)
     take = (rows_of(shape) // rows == lanes_of(shape)).astype(jnp.bfloat16)
     shape = (count, count * rows)
-    put = (lanes_of(shape) // rows == rows_of(shape)).astype(jnp.bfloat16)
+    put = (channel_of(lanes_of(shape) // rows) == rows_of(shape)).astype(jnp.bfloat16)
     picked = dot(take, small) if axis else dot_rows(take, small)
     full = dot(picked.astype(jnp.bfloat16), put)
     shape = full.shape
     return jnp.where(rows_of(shape) % rows == lanes_of(shape) % rows, full, 0.0)
 
 
-def pointwise_kernel(weight_ref, bias_ref, in_ref, out_ref, full_ref, shift_ref):
+def pointwise_kernel(full_ref, shift_ref, in_ref, out_ref):
     channels, rows_x, width = in_ref.shape
     rows = full_ref.shape[0] // channels
-    steps = rows_x // (2 * rows)
-
-    full_ref[...] = spread(weight_ref[...], rows, 1).astype(jnp.bfloat16)
-    for channel in range(channels):
-        shift_ref[channel] = jnp.full(shift_ref.shape[1:], bias_ref[channel] * DENSITY, jnp.float32)
+    shift = jnp.concatenate([shift_ref[...]] * (width // shift_ref.shape[1]), 1)
 
     def step(index, carry):
         values = in_ref[:, pl.ds(index * 2 * rows, 2 * rows), :].astype(jnp.float32)
         for half in range(2):
             block = values[:, half * rows : (half + 1) * rows].reshape(channels * rows, width)
-            out = dot(full_ref[...], block.astype(jnp.bfloat16)).reshape(channels, rows, width)
-            at = index * 2 * rows + half * rows
-            out_ref[:, pl.ds(at, rows), :] = out * DENSITY + shift_ref[...]
+            out = dot(full_ref[...], block.astype(jnp.bfloat16)) * DENSITY + shift
+            out_ref[:, pl.ds(index * 2 * rows + half * rows, rows), :] = out.reshape(channels, rows, width)
         return carry
 
-    lax.fori_loop(0, steps, step, 0)
-
-
-def pointwise_map(weight, bias, values, rows=8):
-    channels, rows_x, width = values.shape
+    lax.fori_loop(0, rows_x // (2 * rows), step, 0)
+
+
+def pointwise_map(full, shift, values):
     return pl.pallas_call(
         pointwise_kernel,
         out_shape=jax.ShapeDtypeStruct(values.shape, jnp.float32),
-        in_specs=whole(1) + scalars(1) + whole(1),
+        in_specs=whole(3),
         out_specs=whole(1)[0],
-        scratch_shapes=[
-            pltpu.VMEM((channels * rows, channels * rows), jnp.bfloat16),
-            pltpu.VMEM((channels, rows, width), jnp.float32),
-        ],
         compiler_params=params(),
-        cost_estimate=takes(4),
+        cost_estimate=takes(3),
         name="pointwise_map",
-    )(weight, bias, values)
-
-
-def pointwise_back_kernel(weight_ref, in_ref, out_ref, full_ref):
-    channels, rows_x, width = in_ref.shape
+    )(full, shift, values)
+
+
+def pointwise_back_kernel(full_ref, *refs):
+    *terms, out_ref = refs
+    channels, rows_x, width = out_ref.shape
     rows = full_ref.shape[0] // channels
-    full_ref[...] = (0.5 * spread(weight_ref[...], rows, 0)).astype(jnp.bfloat16)
 
     def step(index, carry):
-        block = in_ref[:, pl.ds(index * rows, rows), :].reshape(channels * rows, width)
-        high, low = split(block)
-        out = dot(full_ref[...], high) + dot(full_ref[...], low)
-        out_ref[:, pl.ds(index * rows, rows), :] = out.reshape(channels, rows, width)
+        at = pl.ds(pl.multiple_of(index * 2 * rows, 2 * rows), 2 * rows)
+        total = [0.0, 0.0]
+        for term in range(2):
+            values = [each[:, :, at, :].reshape(channels // 2, 2 * rows, width) for each in terms[term::2]]
+            values = jnp.concatenate(values, 0).astype(jnp.float32)
+            for half in range(2):
+                block = values[:, half * rows : (half + 1) * rows].reshape(channels * rows, width)
+                total[half] = total[half] + dot(full_ref[...], block.astype(jnp.bfloat16))
+        for half in range(2):
+            rows_at = pl.ds(index * 2 * rows + half * rows, rows)
+            out_ref[:, rows_at, :] = total[half].reshape(channels, rows, width)
         return carry
 
-    lax.fori_loop(0, rows_x // rows, step, 0)
-
-
-def pointwise_back(weight, values, rows=8):
-    channels = values.shape[0]
+    lax.fori_loop(0, rows_x // (2 * rows), step, 0)
+
+
+def pointwise_back(full, terms):
+    pairs, halves, rows_x, width = terms[0].shape
     return pl.pallas_call(
         pointwise_back_kernel,
-        out_shape=jax.ShapeDtypeStruct(values.shape, jnp.float32),
-        in_specs=whole(2),
+        out_shape=jax.ShapeDtypeStruct((2 * pairs * halves, rows_x, width), jnp.float32),
+        in_specs=whole(1 + len(terms)),
         out_specs=whole(1)[0],
-        scratch_shapes=[pltpu.VMEM((channels * rows, channels * rows), jnp.bfloat16)],
         compiler_params=params(),
         cost_estimate=takes(4),
         name="pointwise_back",
-    )(weight, values)
+    )(full, *terms)
 
 
 def invert_x(pieces, xi_ref, st_ref):
@@ -705,20 +744,31 @@
 
 def slope_kernel(*refs, blocks):
     pieces, (xi_ref, ti_ref, tf_ref, xf_ref, mapped_ref, cot_ref) = refs[:blocks], refs[blocks : blocks + 6]
-    (grad_ref, *sums), (st_ref, yt_ref) = refs[blocks + 6 : -2], refs[-2:]
+    terms, sums = refs[blocks + 6 : blocks + 10], refs[blocks + 10 : 2 * blocks + 10]
+    st_ref, yt_ref, *before = refs[2 * blocks + 10 :]
     channels, rows_x, _ = mapped_ref.shape
+    half_channels = channels // 2
     deep = tf_ref.shape[0] // 2
     modes_y = deep // 2
     local_y = modes_y // blocks
     invert_x(pieces, xi_ref, st_ref)
 
-    def step(index, carry):
+    def invert(index, parity):
         for half in range(2):
-            channel = half * (channels // 2) + index
-            before = mapped_ref[channel] + spectral_part(index, half, st_ref, ti_ref[0])
-            grad = cot_ref[channel].astype(jnp.float32) * twice_gelu_slope(before)
-            grad_ref[channel] = grad
+            channel = half * half_channels + index
+            before[parity][half] = mapped_ref[channel] + spectral_part(index, half, st_ref, ti_ref[0])
+
+    def slope(index, parity):
+        for half in range(2):
+            channel = half * half_channels + index
+            grad = cot_ref[channel].astype(jnp.float32) * twice_gelu_slope(before[parity][half])
             high, low = split(grad)
+            terms[2 * parity][index // 2, half] = high
+            terms[2 * parity + 1][index // 2, half] = low
+
+    def forward(index, parity):
+        for half in range(2):
+            high, low = terms[2 * parity][index // 2, half], terms[2 * parity + 1][index // 2, half]
             both = dot_rows(tf_ref[...], high)
             found = both[:deep] + both[deep:] + dot_rows(tf_ref[pl.ds(0, deep)], low)
             for block in range(blocks):
@@ -726,9 +776,20 @@
                     at = part * modes_y + block * local_y
                     columns = pl.ds((2 * half + part) * rows_x, rows_x)
                     yt_ref[block, index, :, columns] = found[at : at + local_y]
+
+    def step(pair, carry):
+        index = 2 * pair
+        forward(jnp.maximum(index - 1, 1), 1)
+        invert(index + 1, 1)
+        slope(index, 0)
+        forward(index, 0)
+        invert(jnp.minimum(index + 2, half_channels - 2), 0)
+        slope(index + 1, 1)
         return carry
 
-    lax.fori_loop(0, channels // 2, step, 0, unroll=2)
+    invert(0, 0)
+    lax.fori_loop(0, half_channels // 2, step, 0, unroll=2)
+    forward(half_channels - 1, 1)
     high, low = split(yt_ref[...].reshape(-1, yt_ref.shape[-1]))
     lanes = xf_ref.shape[1] // 2
     both = dot(high, xf_ref[...])
@@ -741,21 +802,22 @@
 def slope_step(pieces, tables, mapped, cotangent):
     ti, tf, xi, xf = tables
     blocks = len(pieces)
-    channels, rows_x, _ = mapped.shape
+    channels, rows_x, width = mapped.shape
     half = channels // 2
     local_y = pieces[0].shape[0] // half
-    grad, *sums = pl.pallas_call(
+    results = pl.pallas_call(
         functools.partial(slope_kernel, blocks=blocks),
-        out_shape=[jax.ShapeDtypeStruct(mapped.shape, jnp.float32)]
+        out_shape=[jax.ShapeDtypeStruct((half // 2, 2, rows_x, width), jnp.bfloat16)] * 4
         + [jax.ShapeDtypeStruct(pieces[0].shape, jnp.float32)] * blocks,
         in_specs=whole(blocks + 6),
-        out_specs=whole(1 + blocks),
-        scratch_shapes=[pltpu.VMEM((blocks, half, local_y, 4 * rows_x), jnp.float32)] * 2,
+        out_specs=whole(4 + blocks),
+        scratch_shapes=[pltpu.VMEM((blocks, half, local_y, 4 * rows_x), jnp.float32)] * 2
+        + [pltpu.VMEM((2, rows_x, width), jnp.float32)] * 2,
         compiler_params=params(),
         cost_estimate=takes(13),
         name="slope_step",
     )(*pieces, xi, ti, tf, xf, mapped, cotangent)
-    return grad, sums
+    return results[:4], results[4:]
 
 
 def finish_kernel(*refs, blocks, group):
@@ -814,21 +876,26 @@
     return lax.ppermute(piece, axis, [(i, i ^ flip) for i in range(count)])
 
 
+def to_owners(same, other, count):
+    pairs = list(pair(same, exchange(other, "py", count, 1)))
+    return pairs[:1] + [exchange(pairs[i], "py", count, 2 * i) for i in range(1, len(pairs))]
+
+
 def between_chips(piece, count):
     return [piece] + [exchange(piece, "py", count, step) for step in range(2, count, 2)]
 
 
-def between_cores(pieces, count):
-    other = [exchange(piece, "py", count, 1) for piece in pieces]
+def between_cores(pieces, count, beside):
+    other = [beside] + [exchange(piece, "py", count, 1) for piece in pieces[1:]]
     return [each for pair in zip(pieces, other) for each in pair]
 
 
 def from_all(piece, axis, count):
-    return [piece] + [exchange(piece, axis, count, step) for step in range(1, count)]
+    return [piece] + [exchange(piece, axis, count, step) for step in range(count - 1, 0, -1)][::-1]
 
 
 def to_all(pieces, axis, count):
-    return pieces[:1] + [exchange(pieces[step], axis, count, step) for step in range(1, count)]
+    return pieces[:1] + [exchange(pieces[step], axis, count, step) for step in range(count - 1, 0, -1)][::-1]
 
 
 def on_device_packed(
@@ -847,41 +914,41 @@
     full_x = rows_x * count_x
     planes, local_y, local_x = spectrum_saved.shape[1:4]
     modes_x = kx_modes.shape[0]
-    place_x, place_y = lax.axis_index("px"), lax.axis_index("py")
     lanes = 2 * weight_store.shape[0]
     store = jnp.transpose(weight_store, (1, 2, 3, 0))
-    place = jnp.stack([place_x, place_y])
-
     barrier = lax.optimization_barrier
-    slots, spectrum, place = barrier((block_slot, spectrum_saved, place))
-    spectrum = jnp.transpose(spectrum, (1, 2, 3, 4, 0)).reshape(-1, channels)
-    pieces = between_chips(pack(slots, spectrum, lanes), count_y)
-    *tables, packed = prepare(place, ky_modes, kx_modes, store, full_x, rows_x, width_y, count_y)
-    pieces, tables, packed = barrier((pieces, tables, packed))
-    pieces, packed = barrier((between_cores(pieces, count_y), packed))
-    kept, slots, mixed = mix(place, packed, pieces, planes, local_x)
-    stores = [packed, exchange(packed, "py", count_y, 2), exchange(packed, "py", count_y, 4)]
-    mixed = lax.all_to_all(mixed, "py", split_axis=0, concat_axis=0, tiled=True)
-    mixed, stores = barrier((mixed, stores))
-    low, high = halves(*stores[1:])
+    spectrum = jnp.transpose(spectrum_saved, (1, 2, 3, 4, 0)).reshape(-1, channels)
+    piece, small = pack(block_slot, spectrum, ky_modes, kx_modes, bias_vector, pointwise, lanes)
+    pieces = between_chips(piece, count_y)
+    beside = exchange(piece, "py", count_y, 1)
+    tables, packed, full_map, full_back, shift, piece = prepare(
+        small, store, piece, full_x, rows_x, width_y, ky_modes.shape[0], modes_x
+    )
+    pieces, beside, tables, full_map, piece = barrier((pieces, beside, tables, full_map, piece))
+    pieces = between_cores([piece] + pieces[1:], count_y, beside)
+    kept, slots, *mixed = mix(packed, pieces, planes, local_x)
+    pairs = to_owners(*mixed, count_y)
+    pairs, packed, beside = barrier((pairs, packed, exchange(packed, "py", count_y, 1)))
+    across = [exchange(packed, "py", count_y, step) for step in (2, 4)]
+    received = from_all(to_modes(slots, pairs, modes_x), "px", count_x)
+    mapped = pointwise_map(full_map, shift, field_in[:, 0])
+    received, mapped, across = barrier((received, mapped, across))
+    low, high = halves(*across)
     far = [exchange(low, "py", count_y, 4), exchange(high, "py", count_y, 2)]
-    received = from_all(to_modes(slots, mixed, modes_x), "px", count_x)
-    mapped = pointwise_map(pointwise, bias_vector, field_in[:, 0])
-    received, mapped, far = barrier((received, mapped, far))
-    stores = between_cores(stores, count_y)
-    far = between_cores(far, count_y)
-    stores = stores + [far[0], far[1], far[2], far[3]]
-    grad, sums = slope_step(received, tables, mapped, cotangent[:, 0])
-    sums, grad, stores = barrier((list(sums), grad, stores))
+    other = [exchange(each, "py", count_y, 1) for each in across]
+    terms, sums = slope_step(received, tables, mapped, cotangent[:, 0])
+    sums, terms, far, other = barrier((list(sums), list(terms), far, other))
     received = to_all(sums, "px", count_x)
-    back = pointwise_back(pointwise, grad)
-    received, back = barrier((received, back))
-    same, other, mixed = adjoint(place, slots, received, stores, modes_x)
+    back = pointwise_back(full_back, terms)
+    stores = [packed, beside, across[0], other[0], across[1], other[1]]
+    low, high = far
+    stores += [low, exchange(low, "py", count_y, 1), high, exchange(high, "py", count_y, 1)]
+    received, back, stores = barrier((received, back, stores))
+    same, other, mixed = adjoint(slots, received, stores, modes_x)
     received = from_all(mixed, "px", count_x)
-    pairs = list(pair(same, exchange(other, "py", count_y, 1)))
-    pairs = pairs[:1] + [exchange(pairs[i], "py", count_y, 2 * i) for i in range(1, len(pairs))]
+    pairs = to_owners(same, other, count_y)
     field_grad = finish(received, tables, back)
-    blocks = weight_grad(place, kept, pairs)
+    blocks = weight_grad(kept, pairs)
     return (field_grad[:, None], jnp.transpose(blocks, (3, 0, 1, 2)))
 
 

time: 87.2 us -> 77 us (0.88)
  Pallas kernels: 38.1 us -> 27.5 us
  blocking collectives: 10.1 us -> 0 us
  waiting for transfers between devices: 6.71 us -> 14.2 us
  starting transfers between devices: 27.6 us -> 31.3 us
    all_to_all x1 -> x0, blocking collectives: 10.1 us -> none  [on_device_packed(): mixed = lax.all_to_all(mixed, 'py', split_axis=0, concat_axis=0, tiled=True)]
    ppermute x29 -> x33, waiting for transfers between devices: 6.71 us -> 14.2 us  [exchange(): return lax.ppermute(piece, axis, [(i, i ^ flip) for i in range(count)])]
    pallas_call x1, Pallas kernels: 13.3 us -> 8.25 us  [slope_step(): pl.pallas_call(functools.partial(slope_kernel, blocks=blocks), out_shape=...]
    ppermute x29 -> x33, starting transfers between devices: 27.6 us -> 31.3 us  [exchange(): return lax.ppermute(piece, axis, [(i, i ^ flip) for i in range(count)])]
    pallas_call x4, Pallas kernels: 11.5 us -> 8.25 us  [the longest x1 3.53 us: pointwise_back(): pl.pallas_call(pointwise_back_kernel, out_shape=jax.ShapeDtypeStruct((2 *...]
    unnamed x16 -> x10, local copies, waits for them, and re-layouts: 3.44 us -> 2.96 us
  transfers between devices with their start and end apart: 29 -> 33, of which waited for: 8 -> 14; matrix products, arithmetic and copies ran while one was open for 0% -> 0% of each run, Pallas kernels for 35% -> 29%
where the time goes in v1:
time: 77 us; the launch traced here: 76.7 us
  starting transfers between devices  31.3 us (41%)
  Pallas kernels  27.5 us (36%)
  waiting for transfers between devices  14.2 us (18%)
  local copies, waits for them, and re-layouts  2.96 us (4%)
  between operations  0.83 us (1%)
    ppermute x33, starting transfers between devices, exchange(): return lax.ppermute(piece, axis, [(i, i ^ flip) for i in range(count)])  31.3 us
    ppermute x33, waiting for transfers between devices, exchange(): return lax.ppermute(piece, axis, [(i, i ^ flip) for i in range(count)])  14.2 us
    pallas_call x1, Pallas kernels, slope_step(): pl.pallas_call(functools.partial(slope_kernel, blocks=blocks), out_shape=...  8.25 us
    pallas_call x1, Pallas kernels, finish(): pl.pallas_call(functools.partial(finish_kernel, blocks=blocks, group=grou...  4.39 us
    pallas_call x1, Pallas kernels, pointwise_back(): pl.pallas_call(pointwise_back_kernel, out_shape=jax.ShapeDtypeStruct((2 *...  3.53 us
    unnamed x10, local copies, waits for them, and re-layouts  2.96 us
    pallas_call x1, Pallas kernels, pointwise_map(): pl.pallas_call(pointwise_kernel, out_shape=jax.ShapeDtypeStruct(values.sh...  2.45 us
    pallas_call x1, Pallas kernels, weight_grad(): pl.pallas_call(weight_grad_kernel, out_shape=jax.ShapeDtypeStruct(shape,...  2.12 us
  transfers between devices with their start and end apart: 33, of which 14 were waited for; matrix products, arithmetic and copies ran while one was open for 0% of the time, Pallas kernels for 29%

profile of v1, /device:TPU:0, one launch (start us, length us, event | category | flops | bytes accessed | tf_op | source)
XLA Modules:
  0.0 76.7 jit_solution(16276933794802626502)
XLA Ops:
  0.6 1.8 %pack.1 = (f32[32,640]{1,0:T(8,128)}, f32[128,128]{1,0:T(8,128)}) custom-call(s32[4,8]{1,0:T(4,128)} %refs_0_.1, f32[512,32]{1,0:T(8,128)} %bitcast.14, s32[32]{0:T(128)} %refs_2_.1, s32[32]{0:T(128)} %refs_3_.1, f32[32]{0:T(128)} %refs_4_.1, bf16[32,32]{1,0:T(8,128)(2,1)} %refs_5_.1), custom_call_target="tpu_custom_call" | custom-call | tf_op jit(solution)/shard_map/pack/pallas_call | solution.py:360
  2.4 3.0 %collective-permute-start = (f32[32,640]{1,0:T(8,128)}, f32[32,640]{1,0:T(8,128)S(1)}, u32[]{:S(2)}, u32[]{:S(2)}) collective-permute-start(f32[32,640]{1,0:T(8,128)} %get-tuple-element.89.piece_ref), channel_id=1, source_target_pairs={{0,2},{1,3},{2,0},{3,1},{4,6},{5,7},{6,4},{7,5},{8,10},{9,11},{10,... | collective-permute-start | bytes 245768 | tf_op jit(solution)/shard_map/ppermute | solution.py:876
  5.4 1.5 %collective-permute-start.1 = (f32[32,640]{1,0:T(8,128)}, f32[32,640]{1,0:T(8,128)S(1)}, u32[]{:S(2)}, u32[]{:S(2)}) collective-permute-start(f32[32,640]{1,0:T(8,128)} %get-tuple-element.89.piece_ref), channel_id=1, source_target_pairs={{0,4},{1,5},{2,6},{3,7},{4,0},{5,1},{6,2},{7,3},{8,12},{9,13},{10,... | collective-permute-start | bytes 245768 | tf_op jit(solution)/shard_map/ppermute | solution.py:876
  6.9 0.0 collective-permute-start.2
  7.0 0.0 collective-permute-start.3
  7.0 1.2 %copy-done.2 = f32[64,2,32,32]{0,3,2,1:T(8,128)S(1)} copy-done((f32[64,2,32,32]{0,3,2,1:T(8,128)S(1)}, f32[64,2,32,32]{0,3,2,1:T(8,128)}, u32[]{:S(2)}) %copy-start.2) | copy-done | bytes 524312
  8.2 0.9 %copy-done.3 = f32[32,640]{1,0:T(8,128)S(1)} copy-done((f32[32,640]{1,0:T(8,128)S(1)}, f32[32,640]{1,0:T(8,128)}, u32[]{:S(2)}) %copy-start.3) | copy-done | bytes 81944
  9.1 0.8 %copy-done.4 = f32[128,128]{1,0:T(8,128)S(1)} copy-done((f32[128,128]{1,0:T(8,128)S(1)}, f32[128,128]{1,0:T(8,128)}, u32[]{:S(2)}) %copy-start.4) | copy-done | bytes 65560
  9.9 0.8 %prepare.1 = (bf16[2,256,512]{2,1,0:T(8,128)(2,1)S(1)}, bf16[128,512]{1,0:T(8,128)(2,1)S(1)}, bf16[384,512]{1,0:T(8,128)(2,1)S(1)}, bf16[512,256]{1,0:T(8,128)(2...) custom-call(f32[128,128]{1,0:T(8,128)S(1)} %copy-done.4, ...), custom_call_target="tpu_custom_call" | custom-call | flops 2000000000 | bytes 1048576 | tf_op jit(solution)/shard_map/prepare/pallas_call | solution.py:310
  10.8 0.6 collective-permute-start.11
  11.3 0.0 collective-permute-done.refs_2_
  11.3 0.0 collective-permute-done.1.refs_4_
  11.3 1.2 %collective-permute-done.2.refs_6_ = f32[32,640]{1,0:T(8,128)S(1)} collective-permute-done((f32[32,640]{1,0:T(8,128)}, f32[32,640]{1,0:T(8,128)S(1)}, u32[]{:S(2)}, u32[]{:S(2)}) %collective-permute-start.2) | collective-permute-done | bytes 81952 | tf_op jit(solution)/shard_map/ppermute | solution.py:876
  12.5 0.0 collective-permute-done.3.refs_1_
  12.5 0.0 collective-permute-start.4
  12.5 0.5 collective-permute-start.5
  13.0 0.0 collective-permute-start.6
  13.0 0.8 collective-permute-done.4.refs_3_
  13.8 0.2 collective-permute-done.5.refs_5_
  13.9 0.4 collective-permute-done.6.refs_7_
  14.3 2.0 %mix.1 = (f32[512,128]{1,0:T(8,128)S(1)}, f32[256,128]{1,0:T(8,128)S(1)}, f32[4,32,128]{2,1,0:T(8,128)S(1)}, f32[4,32,128]{2,1,0:T(8,128)S(1)}) custom-call(f32[1024,128]{1,0:T(8,128)S(1)} %get-tuple-element.155.packed_ref.refs_4_, f32[32,640]{1,0:T(8,128)S(1)} %get-tuple-element.97.refs_0_, f32[32,640]{1,0:T(8,128)S(1)} %collective-permute-done.3.refs_1_, ...), custom_call_target="tpu_custom_call" | custom-call | flops 3000000000 | bytes 1048576 | tf_op jit(solution)/shard_map/mix/pallas_call | solution.py:428
  16.3 0.0 copy-start
  16.3 0.2 collective-permute-start.7
  16.5 1.1 %collective-permute-done.7.other_ref = f32[4,32,128]{2,1,0:T(8,128)S(1)} collective-permute-done((f32[4,32,128]{2,1,0:T(8,128)S(1)}, f32[4,32,128]{2,1,0:T(8,128)S(1)}, u32[]{:S(2)}, u32[]{:S(2)}) %collective-permute-start.7) | collective-permute-done | bytes 65568 | tf_op jit(solution)/shard_map/ppermute | solution.py:876
  17.6 1.9 %collective-permute-start.10 = (f32[2,32,128]{2,1,0:T(8,128)S(1)}, f32[2,32,128]{2,1,0:T(8,128)S(1)}, u32[]{:S(2)}, u32[]{:S(2)}) collective-permute-start(f32[2,32,128]{2,1,0:T(8,128)S(1)} %get-tuple-element.108), channel_id=1, source_target_pairs={{0,6},{1,7},{2,4},{3,5},{4,2},{5,3},{6,0},{7,1},{8,14},{9,15},{10,... | collective-permute-start | bytes 98312 | tf_op jit(solution)/shard_map/ppermute | solution.py:876
  19.6 0.5 collective-permute-start.8
  20.1 1.1 %collective-permute-start.9 = (f32[2,32,128]{2,1,0:T(8,128)S(1)}, f32[2,32,128]{2,1,0:T(8,128)S(1)}, u32[]{:S(2)}, u32[]{:S(2)}) collective-permute-start(f32[2,32,128]{2,1,0:T(8,128)S(1)} %get-tuple-element.107), channel_id=1, source_target_pairs={{0,4},{1,5},{2,6},{3,7},{4,0},{5,1},{6,2},{7,3},{8,12},{9,13},{10,... | collective-permute-start | bytes 98312 | tf_op jit(solution)/shard_map/ppermute | solution.py:876
  21.2 1.7 %collective-permute-done.10.refs_3_ = f32[2,32,128]{2,1,0:T(8,128)S(1)} collective-permute-done((f32[2,32,128]{2,1,0:T(8,128)S(1)}, f32[2,32,128]{2,1,0:T(8,128)S(1)}, u32[]{:S(2)}, u32[]{:S(2)}) %collective-permute-start.10) | collective-permute-done | bytes 32800 | tf_op jit(solution)/shard_map/ppermute | solution.py:876
  22.9 0.6 collective-permute-done.8.refs_1_
  23.5 0.5 collective-permute-done.9.refs_2_
  24.0 0.0 collective-permute-done.11.refs_5_
  24.0 1.5 %collective-permute-start.15 = (f32[1024,128]{1,0:T(8,128)S(1)}, f32[1024,128]{1,0:T(8,128)S(1)}, u32[]{:S(2)}, u32[]{:S(2)}) collective-permute-start(f32[1024,128]{1,0:T(8,128)S(1)} %get-tuple-element.155.packed_ref.refs_4_), channel_id=1, source_target_pairs={{0,2},{1,3},{2,0},{3,1},{4,6},{5,7},{6,4},{7,5},{8,10},{9,11},{10,... | collective-permute-start | bytes 1572872 | tf_op jit(solution)/shard_map/ppermute | solution.py:876
  25.5 0.5 collective-permute-start.16
  26.0 0.6 to_modes.1.refs_0_
  26.6 1.6 %collective-permute-start.12 = (f32[128,128]{1,0:T(8,128)S(1)}, f32[128,128]{1,0:T(8,128)S(1)}, u32[]{:S(2)}, u32[]{:S(2)}) collective-permute-start(f32[128,128]{1,0:T(8,128)S(1)} %to_modes.1.refs_0_), channel_id=1, source_target_pairs={{0,8},{8,0},{16,24},{24,16},{1,9},{9,1},{17,25},{25,17},{2,10},{10... | collective-permute-start | bytes 196616 | tf_op jit(solution)/shard_map/ppermute | solution.py:876
  28.2 2.6 %collective-permute-start.13 = (f32[128,128]{1,0:T(8,128)S(1)}, f32[128,128]{1,0:T(8,128)S(1)}, u32[]{:S(2)}, u32[]{:S(2)}) collective-permute-start(f32[128,128]{1,0:T(8,128)S(1)} %to_modes.1.refs_0_), channel_id=1, source_target_pairs={{0,16},{8,24},{16,0},{24,8},{1,17},{9,25},{17,1},{25,9},{2,18},{10... | collective-permute-start | bytes 196616 | tf_op jit(solution)/shard_map/ppermute | solution.py:876
  30.8 0.2 collective-permute-start.14
  31.0 2.4 %pointwise_map.1.refs_8_ = f32[32,128,512]{2,1,0:T(8,128)S(1)} custom-call(bf16[256,256]{1,0:T(8,128)(2,1)S(1)} %get-tuple-element.113.full_ref, f32[256,128]{1,0:T(8,128)S(1)} %get-tuple-element.114.shift_ref, bf16[32,128,512]{2,1,0:T(8,128)(2,1)S(1)} %bitcast.10), custom_call_target="tpu_custom_call" | custom-call | flops 3000000000 | bytes 1048576 | tf_op jit(solution)/shard_map/pointwise_map/pallas_call | solution.py:679
  33.5 1.3 %collective-permute-done.13.refs_2_ = f32[128,128]{1,0:T(8,128)S(1)} collective-permute-done((f32[128,128]{1,0:T(8,128)S(1)}, f32[128,128]{1,0:T(8,128)S(1)}, u32[]{:S(2)}, u32[]{:S(2)}) %collective-permute-start.13) | collective-permute-done | bytes 65568 | tf_op jit(solution)/shard_map/ppermute | solution.py:876
  34.8 2.1 %collective-permute-done.14.refs_3_ = f32[128,128]{1,0:T(8,128)S(1)} collective-permute-done((f32[128,128]{1,0:T(8,128)S(1)}, f32[128,128]{1,0:T(8,128)S(1)}, u32[]{:S(2)}, u32[]{:S(2)}) %collective-permute-start.14) | collective-permute-done | bytes 65568 | tf_op jit(solution)/shard_map/ppermute | solution.py:876
  36.9 0.8 %collective-permute-done.16.second_ref.refs_8_ = f32[1024,128]{1,0:T(8,128)S(1)} collective-permute-done((f32[1024,128]{1,0:T(8,128)S(1)}, f32[1024,128]{1,0:T(8,128)S(1)}, u32[]{:S(2)}, u32[]{:S(2)}) %collective-permute-start.16) | collective-permute-done | bytes 524320 | tf_op jit(solution)/shard_map/ppermute | solution.py:876
  37.7 0.6 collective-permute-start.20
  38.3 1.1 %collective-permute-start.17 = (f32[512,128]{1,0:T(8,128)S(1)}, f32[512,128]{1,0:T(8,128)S(1)}, u32[]{:S(2)}, u32[]{:S(2)}) collective-permute-start(f32[512,128]{1,0:T(8,128)S(1)} %get-tuple-element.135), channel_id=1, source_target_pairs={{0,4},{1,5},{2,6},{3,7},{4,0},{5,1},{6,2},{7,3},{8,12},{9,13},{10,... | collective-permute-start | bytes 786440 | tf_op jit(solution)/shard_map/ppermute | solution.py:876
  39.4 0.7 collective-permute-start.18
  40.1 8.3 %slope_step.1 = (bf16[8,2,128,512]{3,2,1,0:T(8,128)(2,1)S(1)}, bf16[8,2,128,512]{3,2,1,0:T(8,128)(2,1)S(1)}, bf16[8,2,128,512]{3,2,1,0:T(8,128)(2,1)S(1)}, bf16[...) custom-call(f32[128,128]{1,0:T(8,128)S(1)} %to_modes.1.refs_0_, ...), custom_call_target="tpu_custom_call" | custom-call | flops 12999999488 | bytes 1048576 | tf_op jit(solution)/shard_map/slope_step/pallas_call | solution.py:808
  48.4 0.1 collective-permute-start.24
  48.5 0.5 collective-permute-start.25
  49.0 1.6 %collective-permute-start.21 = (f32[128,128]{1,0:T(8,128)S(1)}, f32[128,128]{1,0:T(8,128)S(1)}, u32[]{:S(2)}, u32[]{:S(2)}) collective-permute-start(f32[128,128]{1,0:T(8,128)S(1)} %get-tuple-element.138), channel_id=1, source_target_pairs={{0,8},{8,0},{16,24},{24,16},{1,9},{9,1},{17,25},{25,17},{2,10},{10... | collective-permute-start | bytes 196616 | tf_op jit(solution)/shard_map/ppermute | solution.py:876
  50.6 2.6 %collective-permute-start.22 = (f32[128,128]{1,0:T(8,128)S(1)}, f32[128,128]{1,0:T(8,128)S(1)}, u32[]{:S(2)}, u32[]{:S(2)}) collective-permute-start(f32[128,128]{1,0:T(8,128)S(1)} %get-tuple-element.139), channel_id=1, source_target_pairs={{0,16},{8,24},{16,0},{24,8},{1,17},{9,25},{17,1},{25,9},{2,18},{10... | collective-permute-start | bytes 196616 | tf_op jit(solution)/shard_map/ppermute | solution.py:876
  53.2 0.2 collective-permute-start.23
  53.4 3.5 %pointwise_back.1.refs_6_ = f32[32,128,512]{2,1,0:T(8,128)S(1)} custom-call(bf16[256,256]{1,0:T(8,128)(2,1)S(1)} %get-tuple-element.141.full_ref, bf16[8,2,128,512]{3,2,1,0:T(8,128)(2,1)S(1)} %get-tuple-element.142.refs_0_, bf16[8,2,128,512]{3,2,1,0:T(8,128)(2,1)S(1)} %get-tuple-element.143.refs_1_, bf16[8,2,128,512]{3,2,1,0:T(8,128)(2,1)S(1)} %get-tuple-element.144.refs_2_, ...), custom_call_target="tpu_custom_call" | custom-call | flops 4000000000 | bytes 1048576 | tf_op jit(solution)/shard_map/pointwise_back/pallas_call | solution.py:714
  56.9 1.1 %collective-permute-done.22.refs_2_ = f32[128,128]{1,0:T(8,128)S(1)} collective-permute-done((f32[128,128]{1,0:T(8,128)S(1)}, f32[128,128]{1,0:T(8,128)S(1)}, u32[]{:S(2)}, u32[]{:S(2)}) %collective-permute-start.22) | collective-permute-done | bytes 65568 | tf_op jit(solution)/shard_map/ppermute | solution.py:876
  58.1 1.3 %collective-permute-done.23.refs_3_ = f32[128,128]{1,0:T(8,128)S(1)} collective-permute-done((f32[128,128]{1,0:T(8,128)S(1)}, f32[128,128]{1,0:T(8,128)S(1)}, u32[]{:S(2)}, u32[]{:S(2)}) %collective-permute-start.23) | collective-permute-done | bytes 65568 | tf_op jit(solution)/shard_map/ppermute | solution.py:876
  59.3 1.5 %adjoint.1 = (f32[4,32,128]{2,1,0:T(8,128)S(1)}, f32[4,32,128]{2,1,0:T(8,128)S(1)}, f32[128,128]{1,0:T(8,128)S(1)}) custom-call(f32[256,128]{1,0:T(8,128)S(1)} %get-tuple-element.102.slots_ref, f32[128,128]{1,0:T(8,128)S(1)} %get-tuple-element.151.refs_0_, f32[128,128]{1,0:T(8,128)S(1)} %collective-permute-done.21.refs_1_, ...), custom_call_target="tpu_custom_call" | custom-call | flops 3000000000 | bytes 1048576 | tf_op jit(solution)/shard_map/adjoint/pallas_call | solution.py:597
  60.8 0.1 collective-permute-start.29
  60.9 0.8 %collective-permute-start.26 = (f32[128,128]{1,0:T(8,128)S(1)}, f32[128,128]{1,0:T(8,128)S(1)}, u32[]{:S(2)}, u32[]{:S(2)}) collective-permute-start(f32[128,128]{1,0:T(8,128)S(1)} %get-tuple-element.165.refs_0_), channel_id=1, source_target_pairs={{0,8},{8,0},{16,24},{24,16},{1,9},{9,1},{17,25},{25,17},{2,10},{10... | collective-permute-start | bytes 196616 | tf_op jit(solution)/shard_map/ppermute | solution.py:876
  61.7 1.7 %collective-permute-start.27 = (f32[128,128]{1,0:T(8,128)S(1)}, f32[128,128]{1,0:T(8,128)S(1)}, u32[]{:S(2)}, u32[]{:S(2)}) collective-permute-start(f32[128,128]{1,0:T(8,128)S(1)} %get-tuple-element.165.refs_0_), channel_id=1, source_target_pairs={{0,16},{8,24},{16,0},{24,8},{1,17},{9,25},{17,1},{25,9},{2,18},{10... | collective-permute-start | bytes 196616 | tf_op jit(solution)/shard_map/ppermute | solution.py:876
  63.5 1.9 %collective-permute-start.28 = (f32[128,128]{1,0:T(8,128)S(1)}, f32[128,128]{1,0:T(8,128)S(1)}, u32[]{:S(2)}, u32[]{:S(2)}) collective-permute-start(f32[128,128]{1,0:T(8,128)S(1)} %get-tuple-element.165.refs_0_), channel_id=1, source_target_pairs={{0,24},{8,16},{16,8},{24,0},{1,25},{9,17},{17,9},{25,1},{2,26},{10... | collective-permute-start | bytes 196616 | tf_op jit(solution)/shard_map/ppermute | solution.py:876
  65.4 1.4 %collective-permute-start.30 = (f32[2,32,128]{2,1,0:T(8,128)S(1)}, f32[2,32,128]{2,1,0:T(8,128)S(1)}, u32[]{:S(2)}, u32[]{:S(2)}) collective-permute-start(f32[2,32,128]{2,1,0:T(8,128)S(1)} %get-tuple-element.171), channel_id=1, source_target_pairs={{0,2},{1,3},{2,0},{3,1},{4,6},{5,7},{6,4},{7,5},{8,10},{9,11},{10,... | collective-permute-start | bytes 98312 | tf_op jit(solution)/shard_map/ppermute | solution.py:876
  66.8 0.9 %collective-permute-start.31 = (f32[2,32,128]{2,1,0:T(8,128)S(1)}, f32[2,32,128]{2,1,0:T(8,128)S(1)}, u32[]{:S(2)}, u32[]{:S(2)}) collective-permute-start(f32[2,32,128]{2,1,0:T(8,128)S(1)} %get-tuple-element.172), channel_id=1, source_target_pairs={{0,4},{1,5},{2,6},{3,7},{4,0},{5,1},{6,2},{7,3},{8,12},{9,13},{10,... | collective-permute-start | bytes 98312 | tf_op jit(solution)/shard_map/ppermute | solution.py:876
  67.7 1.2 %collective-permute-start.32 = (f32[2,32,128]{2,1,0:T(8,128)S(1)}, f32[2,32,128]{2,1,0:T(8,128)S(1)}, u32[]{:S(2)}, u32[]{:S(2)}) collective-permute-start(f32[2,32,128]{2,1,0:T(8,128)S(1)} %get-tuple-element.173), channel_id=1, source_target_pairs={{0,6},{1,7},{2,4},{3,5},{4,2},{5,3},{6,0},{7,1},{8,14},{9,15},{10,... | collective-permute-start | bytes 98312 | tf_op jit(solution)/shard_map/ppermute | solution.py:876
  68.9 1.2 %collective-permute-done.27.refs_2_ = f32[128,128]{1,0:T(8,128)S(1)} collective-permute-done((f32[128,128]{1,0:T(8,128)S(1)}, f32[128,128]{1,0:T(8,128)S(1)}, u32[]{:S(2)}, u32[]{:S(2)}) %collective-permute-start.27) | collective-permute-done | bytes 65568 | tf_op jit(solution)/shard_map/ppermute | solution.py:876
  70.2 4.4 %finish.1 = f32[32,128,512]{2,1,0:T(8,128)} custom-call(f32[128,128]{1,0:T(8,128)S(1)} %get-tuple-element.165.refs_0_, f32[128,128]{1,0:T(8,128)S(1)} %collective-permute-done.26.refs_1_, f32[128,128]{1,0:T(8,128)S(1)} %collective-permute-done.27.refs_2_, f32[128,128]{1,0:T(8,128)S(1)} %collective-permute-done.28.refs_3_, ...), custom_call_target="tpu_custom_call" | custom-call | flops 4000000000 | bytes 1048576 | tf_op jit(solution)/shard_map/finish/pallas_call | solution.py:859
  74.6 2.1 %weight_grad.1 = f32[2,32,32,64]{3,2,1,0:T(8,128)} custom-call(f32[512,128]{1,0:T(8,128)S(1)} %get-tuple-element.167.kept_ref, f32[2,32,128]{2,1,0:T(8,128)S(1)} %get-tuple-element.170.refs_0_, f32[2,32,128]{2,1,0:T(8,128)S(1)} %collective-permute-done.30.refs_1_, f32[2,32,128]{2,1,0:T(8,128)S(1)} %collective-permute-done.31.refs_2_, ...), custom_call_target="tpu_custom_call" | custom-call | flops 2000000000 | bytes 1048576 | tf_op jit(solution)/shard_map/weight_grad/pallas_call | solution.py:492
  (25 shorter events, 0.1 us)
Async XLA Ops:
  2.4 8.9 %collective-permute-start = (f32[32,640]{1,0:T(8,128)}, f32[32,640]{1,0:T(8,128)S(1)}, u32[]{:S(2)}, u32[]{:S(2)}) collective-permute-start(f32[32,640]{1,0:T(8,128)} %get-tuple-element.89.piece_ref), channel_id=1, source_target_pairs={{0,2},{1,3},{2,0},{3,1},{4,6},{5,7},{6,4},{7,5},{8,10},{9,11},{10,... | collective-permute-start | bytes 245768 | tf_op jit(solution)/shard_map/ppermute | solution.py:876
  5.4 5.9 %collective-permute-start.1 = (f32[32,640]{1,0:T(8,128)}, f32[32,640]{1,0:T(8,128)S(1)}, u32[]{:S(2)}, u32[]{:S(2)}) collective-permute-start(f32[32,640]{1,0:T(8,128)} %get-tuple-element.89.piece_ref), channel_id=1, source_target_pairs={{0,4},{1,5},{2,6},{3,7},{4,0},{5,1},{6,2},{7,3},{8,12},{9,13},{10,... | collective-permute-start | bytes 245768 | tf_op jit(solution)/shard_map/ppermute | solution.py:876
  6.9 5.6 %collective-permute-start.2 = (f32[32,640]{1,0:T(8,128)}, f32[32,640]{1,0:T(8,128)S(1)}, u32[]{:S(2)}, u32[]{:S(2)}) collective-permute-start(f32[32,640]{1,0:T(8,128)} %get-tuple-element.89.piece_ref), channel_id=1, source_target_pairs={{0,6},{1,7},{2,4},{3,5},{4,2},{5,3},{6,0},{7,1},{8,14},{9,15},{10,... | collective-permute-start | bytes 245768 | tf_op jit(solution)/shard_map/ppermute | solution.py:876
  7.0 5.5 %collective-permute-start.3 = (f32[32,640]{1,0:T(8,128)}, f32[32,640]{1,0:T(8,128)S(1)}, u32[]{:S(2)}, u32[]{:S(2)}) collective-permute-start(f32[32,640]{1,0:T(8,128)} %get-tuple-element.89.piece_ref), channel_id=1, source_target_pairs={{0,1},{1,0},{2,3},{3,2},{4,5},{5,4},{6,7},{7,6},{8,9},{9,8},{10,11... | collective-permute-start | bytes 245768 | tf_op jit(solution)/shard_map/ppermute | solution.py:876
  7.0 1.2 %copy-start.2 = (f32[64,2,32,32]{0,3,2,1:T(8,128)S(1)}, f32[64,2,32,32]{0,3,2,1:T(8,128)}, u32[]{:S(2)}) copy-start(f32[64,2,32,32]{0,3,2,1:T(8,128)} %param.12) | copy-start | bytes 1572868
  8.2 0.9 %copy-start.3 = (f32[32,640]{1,0:T(8,128)S(1)}, f32[32,640]{1,0:T(8,128)}, u32[]{:S(2)}) copy-start(f32[32,640]{1,0:T(8,128)} %get-tuple-element.89.piece_ref) | copy-start | bytes 245764
  9.1 0.8 %copy-start.4 = (f32[128,128]{1,0:T(8,128)S(1)}, f32[128,128]{1,0:T(8,128)}, u32[]{:S(2)}) copy-start(f32[128,128]{1,0:T(8,128)} %get-tuple-element.88.small_ref) | copy-start | bytes 196612
  10.8 13.3 %collective-permute-start.11 = (f32[1024,128]{1,0:T(8,128)S(1)}, f32[1024,128]{1,0:T(8,128)S(1)}, u32[]{:S(2)}, u32[]{:S(2)}) collective-permute-start(f32[1024,128]{1,0:T(8,128)S(1)} %get-tuple-element.155.packed_ref.refs_4_), channel_id=1, source_target_pairs={{0,1},{1,0},{2,3},{3,2},{4,5},{5,4},{6,7},{7,6},{8,9},{9,8},{10,11... | collective-permute-start | bytes 1572872 | tf_op jit(solution)/shard_map/ppermute | solution.py:876
  12.5 1.3 %collective-permute-start.4 = (f32[32,640]{1,0:T(8,128)S(1)}, f32[32,640]{1,0:T(8,128)S(1)}, u32[]{:S(2)}, u32[]{:S(2)}) collective-permute-start(f32[32,640]{1,0:T(8,128)S(1)} %collective-permute-done.refs_2_), channel_id=1, source_target_pairs={{0,1},{1,0},{2,3},{3,2},{4,5},{5,4},{6,7},{7,6},{8,9},{9,8},{10,11... | collective-permute-start | bytes 245768 | tf_op jit(solution)/shard_map/ppermute | solution.py:876
  12.5 1.4 %collective-permute-start.5 = (f32[32,640]{1,0:T(8,128)S(1)}, f32[32,640]{1,0:T(8,128)S(1)}, u32[]{:S(2)}, u32[]{:S(2)}) collective-permute-start(f32[32,640]{1,0:T(8,128)S(1)} %collective-permute-done.1.refs_4_), channel_id=1, source_target_pairs={{0,1},{1,0},{2,3},{3,2},{4,5},{5,4},{6,7},{7,6},{8,9},{9,8},{10,11... | collective-permute-start | bytes 245768 | tf_op jit(solution)/shard_map/ppermute | solution.py:876
  13.0 1.3 %collective-permute-start.6 = (f32[32,640]{1,0:T(8,128)S(1)}, f32[32,640]{1,0:T(8,128)S(1)}, u32[]{:S(2)}, u32[]{:S(2)}) collective-permute-start(f32[32,640]{1,0:T(8,128)S(1)} %collective-permute-done.2.refs_6_), channel_id=1, source_target_pairs={{0,1},{1,0},{2,3},{3,2},{4,5},{5,4},{6,7},{7,6},{8,9},{9,8},{10,11... | collective-permute-start | bytes 245768 | tf_op jit(solution)/shard_map/ppermute | solution.py:876
  16.3 14.7 %copy-start = (bf16[32,1,128,512]{3,2,1,0:T(8,128)(2,1)S(1)}, bf16[32,1,128,512]{3,2,1,0:T(8,128)(2,1)}, u32[]{:S(2)}) copy-start(bf16[32,1,128,512]{3,2,1,0:T(8,128)(2,1)} %param.9) | copy-start | bytes 12582916
  16.3 1.3 %collective-permute-start.7 = (f32[4,32,128]{2,1,0:T(8,128)S(1)}, f32[4,32,128]{2,1,0:T(8,128)S(1)}, u32[]{:S(2)}, u32[]{:S(2)}) collective-permute-start(f32[4,32,128]{2,1,0:T(8,128)S(1)} %get-tuple-element.104), channel_id=1, source_target_pairs={{0,1},{1,0},{2,3},{3,2},{4,5},{5,4},{6,7},{7,6},{8,9},{9,8},{10,11... | collective-permute-start | bytes 196616 | tf_op jit(solution)/shard_map/ppermute | solution.py:876
  17.6 5.2 %collective-permute-start.10 = (f32[2,32,128]{2,1,0:T(8,128)S(1)}, f32[2,32,128]{2,1,0:T(8,128)S(1)}, u32[]{:S(2)}, u32[]{:S(2)}) collective-permute-start(f32[2,32,128]{2,1,0:T(8,128)S(1)} %get-tuple-element.108), channel_id=1, source_target_pairs={{0,6},{1,7},{2,4},{3,5},{4,2},{5,3},{6,0},{7,1},{8,14},{9,15},{10,... | collective-permute-start | bytes 98312 | tf_op jit(solution)/shard_map/ppermute | solution.py:876
  19.6 3.9 %collective-permute-start.8 = (f32[2,32,128]{2,1,0:T(8,128)S(1)}, f32[2,32,128]{2,1,0:T(8,128)S(1)}, u32[]{:S(2)}, u32[]{:S(2)}) collective-permute-start(f32[2,32,128]{2,1,0:T(8,128)S(1)} %get-tuple-element.106), channel_id=1, source_target_pairs={{0,2},{1,3},{2,0},{3,1},{4,6},{5,7},{6,4},{7,5},{8,10},{9,11},{10,... | collective-permute-start | bytes 98312 | tf_op jit(solution)/shard_map/ppermute | solution.py:876
  20.1 3.9 %collective-permute-start.9 = (f32[2,32,128]{2,1,0:T(8,128)S(1)}, f32[2,32,128]{2,1,0:T(8,128)S(1)}, u32[]{:S(2)}, u32[]{:S(2)}) collective-permute-start(f32[2,32,128]{2,1,0:T(8,128)S(1)} %get-tuple-element.107), channel_id=1, source_target_pairs={{0,4},{1,5},{2,6},{3,7},{4,0},{5,1},{6,2},{7,3},{8,12},{9,13},{10,... | collective-permute-start | bytes 98312 | tf_op jit(solution)/shard_map/ppermute | solution.py:876
  24.0 12.9 %collective-permute-start.15 = (f32[1024,128]{1,0:T(8,128)S(1)}, f32[1024,128]{1,0:T(8,128)S(1)}, u32[]{:S(2)}, u32[]{:S(2)}) collective-permute-start(f32[1024,128]{1,0:T(8,128)S(1)} %get-tuple-element.155.packed_ref.refs_4_), channel_id=1, source_target_pairs={{0,2},{1,3},{2,0},{3,1},{4,6},{5,7},{6,4},{7,5},{8,10},{9,11},{10,... | collective-permute-start | bytes 1572872 | tf_op jit(solution)/shard_map/ppermute | solution.py:876
  25.5 12.2 %collective-permute-start.16 = (f32[1024,128]{1,0:T(8,128)S(1)}, f32[1024,128]{1,0:T(8,128)S(1)}, u32[]{:S(2)}, u32[]{:S(2)}) collective-permute-start(f32[1024,128]{1,0:T(8,128)S(1)} %get-tuple-element.155.packed_ref.refs_4_), channel_id=1, source_target_pairs={{0,4},{1,5},{2,6},{3,7},{4,0},{5,1},{6,2},{7,3},{8,12},{9,13},{10,... | collective-permute-start | bytes 1572872 | tf_op jit(solution)/shard_map/ppermute | solution.py:876
  26.6 6.9 %collective-permute-start.12 = (f32[128,128]{1,0:T(8,128)S(1)}, f32[128,128]{1,0:T(8,128)S(1)}, u32[]{:S(2)}, u32[]{:S(2)}) collective-permute-start(f32[128,128]{1,0:T(8,128)S(1)} %to_modes.1.refs_0_), channel_id=1, source_target_pairs={{0,8},{8,0},{16,24},{24,16},{1,9},{9,1},{17,25},{25,17},{2,10},{10... | collective-permute-start | bytes 196616 | tf_op jit(solution)/shard_map/ppermute | solution.py:876
  28.2 6.6 %collective-permute-start.13 = (f32[128,128]{1,0:T(8,128)S(1)}, f32[128,128]{1,0:T(8,128)S(1)}, u32[]{:S(2)}, u32[]{:S(2)}) collective-permute-start(f32[128,128]{1,0:T(8,128)S(1)} %to_modes.1.refs_0_), channel_id=1, source_target_pairs={{0,16},{8,24},{16,0},{24,8},{1,17},{9,25},{17,1},{25,9},{2,18},{10... | collective-permute-start | bytes 196616 | tf_op jit(solution)/shard_map/ppermute | solution.py:876
  30.8 6.1 %collective-permute-start.14 = (f32[128,128]{1,0:T(8,128)S(1)}, f32[128,128]{1,0:T(8,128)S(1)}, u32[]{:S(2)}, u32[]{:S(2)}) collective-permute-start(f32[128,128]{1,0:T(8,128)S(1)} %to_modes.1.refs_0_), channel_id=1, source_target_pairs={{0,24},{8,16},{16,8},{24,0},{1,25},{9,17},{17,9},{25,1},{2,26},{10... | collective-permute-start | bytes 196616 | tf_op jit(solution)/shard_map/ppermute | solution.py:876
  31.0 9.1 %copy-start.1 = (bf16[32,1,128,512]{3,2,1,0:T(8,128)(2,1)S(1)}, bf16[32,1,128,512]{3,2,1,0:T(8,128)(2,1)}, u32[]{:S(2)}) copy-start(bf16[32,1,128,512]{3,2,1,0:T(8,128)(2,1)} %param.10) | copy-start | bytes 12582916
  37.7 10.7 %collective-permute-start.19 = (f32[1024,128]{1,0:T(8,128)S(1)}, f32[1024,128]{1,0:T(8,128)S(1)}, u32[]{:S(2)}, u32[]{:S(2)}) collective-permute-start(f32[1024,128]{1,0:T(8,128)S(1)} %collective-permute-done.15.first_ref.refs_6_), channel_id=1, source_target_pairs={{0,1},{1,0},{2,3},{3,2},{4,5},{5,4},{6,7},{7,6},{8,9},{9,8},{10,11... | collective-permute-start | bytes 1572872 | tf_op jit(solution)/shard_map/ppermute | solution.py:876
  37.7 10.7 %collective-permute-start.20 = (f32[1024,128]{1,0:T(8,128)S(1)}, f32[1024,128]{1,0:T(8,128)S(1)}, u32[]{:S(2)}, u32[]{:S(2)}) collective-permute-start(f32[1024,128]{1,0:T(8,128)S(1)} %collective-permute-done.16.second_ref.refs_8_), channel_id=1, source_target_pairs={{0,1},{1,0},{2,3},{3,2},{4,5},{5,4},{6,7},{7,6},{8,9},{9,8},{10,11... | collective-permute-start | bytes 1572872 | tf_op jit(solution)/shard_map/ppermute | solution.py:876
  38.3 10.1 %collective-permute-start.17 = (f32[512,128]{1,0:T(8,128)S(1)}, f32[512,128]{1,0:T(8,128)S(1)}, u32[]{:S(2)}, u32[]{:S(2)}) collective-permute-start(f32[512,128]{1,0:T(8,128)S(1)} %get-tuple-element.135), channel_id=1, source_target_pairs={{0,4},{1,5},{2,6},{3,7},{4,0},{5,1},{6,2},{7,3},{8,12},{9,13},{10,... | collective-permute-start | bytes 786440 | tf_op jit(solution)/shard_map/ppermute | solution.py:876
  39.4 9.0 %collective-permute-start.18 = (f32[512,128]{1,0:T(8,128)S(1)}, f32[512,128]{1,0:T(8,128)S(1)}, u32[]{:S(2)}, u32[]{:S(2)}) collective-permute-start(f32[512,128]{1,0:T(8,128)S(1)} %get-tuple-element.136), channel_id=1, source_target_pairs={{0,2},{1,3},{2,0},{3,1},{4,6},{5,7},{6,4},{7,5},{8,10},{9,11},{10,... | collective-permute-start | bytes 786440 | tf_op jit(solution)/shard_map/ppermute | solution.py:876
  48.4 10.9 %collective-permute-start.24 = (f32[512,128]{1,0:T(8,128)S(1)}, f32[512,128]{1,0:T(8,128)S(1)}, u32[]{:S(2)}, u32[]{:S(2)}) collective-permute-start(f32[512,128]{1,0:T(8,128)S(1)} %collective-permute-done.17.refs_10_), channel_id=1, source_target_pairs={{0,1},{1,0},{2,3},{3,2},{4,5},{5,4},{6,7},{7,6},{8,9},{9,8},{10,11... | collective-permute-start | bytes 786440 | tf_op jit(solution)/shard_map/ppermute | solution.py:876
  48.5 10.8 %collective-permute-start.25 = (f32[512,128]{1,0:T(8,128)S(1)}, f32[512,128]{1,0:T(8,128)S(1)}, u32[]{:S(2)}, u32[]{:S(2)}) collective-permute-start(f32[512,128]{1,0:T(8,128)S(1)} %collective-permute-done.18.refs_12_), channel_id=1, source_target_pairs={{0,1},{1,0},{2,3},{3,2},{4,5},{5,4},{6,7},{7,6},{8,9},{9,8},{10,11... | collective-permute-start | bytes 786440 | tf_op jit(solution)/shard_map/ppermute | solution.py:876
  49.0 7.9 %collective-permute-start.21 = (f32[128,128]{1,0:T(8,128)S(1)}, f32[128,128]{1,0:T(8,128)S(1)}, u32[]{:S(2)}, u32[]{:S(2)}) collective-permute-start(f32[128,128]{1,0:T(8,128)S(1)} %get-tuple-element.138), channel_id=1, source_target_pairs={{0,8},{8,0},{16,24},{24,16},{1,9},{9,1},{17,25},{25,17},{2,10},{10... | collective-permute-start | bytes 196616 | tf_op jit(solution)/shard_map/ppermute | solution.py:876
  50.6 7.5 %collective-permute-start.22 = (f32[128,128]{1,0:T(8,128)S(1)}, f32[128,128]{1,0:T(8,128)S(1)}, u32[]{:S(2)}, u32[]{:S(2)}) collective-permute-start(f32[128,128]{1,0:T(8,128)S(1)} %get-tuple-element.139), channel_id=1, source_target_pairs={{0,16},{8,24},{16,0},{24,8},{1,17},{9,25},{17,1},{25,9},{2,18},{10... | collective-permute-start | bytes 196616 | tf_op jit(solution)/shard_map/ppermute | solution.py:876
  53.2 6.2 %collective-permute-start.23 = (f32[128,128]{1,0:T(8,128)S(1)}, f32[128,128]{1,0:T(8,128)S(1)}, u32[]{:S(2)}, u32[]{:S(2)}) collective-permute-start(f32[128,128]{1,0:T(8,128)S(1)} %get-tuple-element.140), channel_id=1, source_target_pairs={{0,24},{8,16},{16,8},{24,0},{1,25},{9,17},{17,9},{25,1},{2,26},{10... | collective-permute-start | bytes 196616 | tf_op jit(solution)/shard_map/ppermute | solution.py:876
  60.8 4.5 %collective-permute-start.29 = (f32[4,32,128]{2,1,0:T(8,128)S(1)}, f32[4,32,128]{2,1,0:T(8,128)S(1)}, u32[]{:S(2)}, u32[]{:S(2)}) collective-permute-start(f32[4,32,128]{2,1,0:T(8,128)S(1)} %get-tuple-element.169), channel_id=1, source_target_pairs={{0,1},{1,0},{2,3},{3,2},{4,5},{5,4},{6,7},{7,6},{8,9},{9,8},{10,11... | collective-permute-start | bytes 196616 | tf_op jit(solution)/shard_map/ppermute | solution.py:876
  60.9 6.8 %collective-permute-start.26 = (f32[128,128]{1,0:T(8,128)S(1)}, f32[128,128]{1,0:T(8,128)S(1)}, u32[]{:S(2)}, u32[]{:S(2)}) collective-permute-start(f32[128,128]{1,0:T(8,128)S(1)} %get-tuple-element.165.refs_0_), channel_id=1, source_target_pairs={{0,8},{8,0},{16,24},{24,16},{1,9},{9,1},{17,25},{25,17},{2,10},{10... | collective-permute-start | bytes 196616 | tf_op jit(solution)/shard_map/ppermute | solution.py:876
  61.7 8.4 %collective-permute-start.27 = (f32[128,128]{1,0:T(8,128)S(1)}, f32[128,128]{1,0:T(8,128)S(1)}, u32[]{:S(2)}, u32[]{:S(2)}) collective-permute-start(f32[128,128]{1,0:T(8,128)S(1)} %get-tuple-element.165.refs_0_), channel_id=1, source_target_pairs={{0,16},{8,24},{16,0},{24,8},{1,17},{9,25},{17,1},{25,9},{2,18},{10... | collective-permute-start | bytes 196616 | tf_op jit(solution)/shard_map/ppermute | solution.py:876
  63.5 6.7 %collective-permute-start.28 = (f32[128,128]{1,0:T(8,128)S(1)}, f32[128,128]{1,0:T(8,128)S(1)}, u32[]{:S(2)}, u32[]{:S(2)}) collective-permute-start(f32[128,128]{1,0:T(8,128)S(1)} %get-tuple-element.165.refs_0_), channel_id=1, source_target_pairs={{0,24},{8,16},{16,8},{24,0},{1,25},{9,17},{17,9},{25,1},{2,26},{10... | collective-permute-start | bytes 196616 | tf_op jit(solution)/shard_map/ppermute | solution.py:876
  65.4 9.2 %collective-permute-start.30 = (f32[2,32,128]{2,1,0:T(8,128)S(1)}, f32[2,32,128]{2,1,0:T(8,128)S(1)}, u32[]{:S(2)}, u32[]{:S(2)}) collective-permute-start(f32[2,32,128]{2,1,0:T(8,128)S(1)} %get-tuple-element.171), channel_id=1, source_target_pairs={{0,2},{1,3},{2,0},{3,1},{4,6},{5,7},{6,4},{7,5},{8,10},{9,11},{10,... | collective-permute-start | bytes 98312 | tf_op jit(solution)/shard_map/ppermute | solution.py:876
  66.8 7.8 %collective-permute-start.31 = (f32[2,32,128]{2,1,0:T(8,128)S(1)}, f32[2,32,128]{2,1,0:T(8,128)S(1)}, u32[]{:S(2)}, u32[]{:S(2)}) collective-permute-start(f32[2,32,128]{2,1,0:T(8,128)S(1)} %get-tuple-element.172), channel_id=1, source_target_pairs={{0,4},{1,5},{2,6},{3,7},{4,0},{5,1},{6,2},{7,3},{8,12},{9,13},{10,... | collective-permute-start | bytes 98312 | tf_op jit(solution)/shard_map/ppermute | solution.py:876
  67.7 6.9 %collective-permute-start.32 = (f32[2,32,128]{2,1,0:T(8,128)S(1)}, f32[2,32,128]{2,1,0:T(8,128)S(1)}, u32[]{:S(2)}, u32[]{:S(2)}) collective-permute-start(f32[2,32,128]{2,1,0:T(8,128)S(1)} %get-tuple-element.173), channel_id=1, source_target_pairs={{0,6},{1,7},{2,4},{3,5},{4,2},{5,3},{6,0},{7,1},{8,14},{9,15},{10,... | collective-permute-start | bytes 98312 | tf_op jit(solution)/shard_map/ppermute | solution.py:876

commit v2 on v1

--- a/solution.py
+++ b/solution.py
@@ -223,40 +223,44 @@
     return out
 
 
-def prepare_kernel(
-    small_ref,
-    store_ref,
-    piece_ref,
-    ti_ref,
-    tf_ref,
-    xi_ref,
-    xf_ref,
-    packed_ref,
-    map_ref,
-    back_ref,
-    shift_ref,
-    kept_ref,
-    *,
-    full_x,
-    modes_y,
-    modes_x,
-):
-    kept_ref[...] = piece_ref[...]
-    channels, width = store_ref.shape[1], tf_ref.shape[1]
+def unpack_kernel(all_ref, store_ref, kept_ref, small_ref, packed_ref):
+    wide, channels = kept_ref.shape[1], store_ref.shape[1]
+    kept_ref[...] = all_ref[:, :wide]
+    small_ref[...] = all_ref[:, wide:]
+    for channel in range(channels):
+        packed = jnp.concatenate([store_ref[0, channel], store_ref[1, channel]], 1)
+        packed_ref[pl.ds(channel * channels, channels)] = packed
+
+
+def unpack(everything, store, wide):
+    rows, full = everything.shape
+    channels, capacity = store.shape[2:]
+    shapes = (rows, wide), (rows, full - wide), (channels * channels, 2 * capacity)
+    return pl.pallas_call(
+        unpack_kernel,
+        out_shape=[jax.ShapeDtypeStruct(shape, jnp.float32) for shape in shapes],
+        in_specs=whole(2),
+        out_specs=whole(3),
+        compiler_params=params(),
+        cost_estimate=takes(0.5),
+        name="unpack",
+    )(everything, store)
+
+
+def tables_kernel(small_ref, ti_ref, tf_ref, xi_ref, xf_ref, map_ref, back_ref, shift_ref, *, full_x):
+    lanes, width = shift_ref.shape[1], tf_ref.shape[1]
+    channels = small_ref.shape[0]
     rows = map_ref.shape[0] // channels
-    ky = small_ref[pl.ds(0, modes_y)].astype(jnp.int32)
-    kx = small_ref[pl.ds(modes_y, modes_x)].astype(jnp.int32)
-    bias = small_ref[pl.ds(modes_y + modes_x, channels)] * DENSITY
-    weight = small_ref[pl.ds(modes_y + modes_x + channels, channels), :][:, :channels].astype(jnp.bfloat16)
+    ky, kx, bias, weight = (small_ref[:, pl.ds(i * lanes, lanes)] for i in range(4))
+    ky, kx, bias = ky.astype(jnp.int32), kx.astype(jnp.int32), bias * DENSITY
+    weight = weight[:, :channels].astype(jnp.bfloat16)
     map_ref[...] = spread(weight, rows, 1, lambda i: i).astype(jnp.bfloat16)
     pairs = channels // 4
     back = spread(weight, rows, 0, lambda i: i % 2 * 2 * pairs + i // 2 % pairs * 2 + i // (2 * pairs))
     back_ref[...] = (0.5 * back).astype(jnp.bfloat16)
     for channel in range(channels):
         shift_ref[pl.ds(channel * rows, rows)] = jnp.broadcast_to(bias[channel : channel + 1], (rows, bias.shape[1]))
-        packed = jnp.concatenate([store_ref[0, channel], store_ref[1, channel]], 1)
-        packed_ref[pl.ds(channel * store_ref.shape[2], store_ref.shape[2])] = packed
-    rows_x = xf_ref.shape[0] // 4
+    modes_x, rows_x = kx.shape[0], xf_ref.shape[0] // 4
     factor = 1.0 / math.sqrt(full_x * width)
     start = place_of()[0] * rows_x
 
@@ -293,30 +297,28 @@
     xf_ref[...] = jnp.concatenate([high, low], 1)
 
 
-def prepare(small, store, piece, full_x, rows_x, width, modes_y, modes_x, rows=8):
-    channels, capacity = store.shape[2:]
+def make_tables(small, full_x, rows_x, width, modes_y, modes_x, rows=8):
+    channels, lanes = small.shape[0], small.shape[1] // 4
     shapes = (
         (2, 4 * 2 * modes_y, width),
         (2 * 2 * modes_y, width),
         (3 * 4 * modes_x, 4 * rows_x),
         (4 * rows_x, 8 * modes_x),
-        (channels * channels, 2 * capacity),
         (channels * rows, channels * rows),
         (channels * rows, channels * rows),
-        (channels * rows, small.shape[1]),
-        piece.shape,
-    )
-    types = [jnp.float32 if i in (4, 7, 8) else jnp.bfloat16 for i in range(len(shapes))]
-    *tables, packed, full_map, full_back, shift, piece = pl.pallas_call(
-        functools.partial(prepare_kernel, full_x=full_x, modes_y=modes_y, modes_x=modes_x),
+        (channels * rows, lanes),
+    )
+    types = [jnp.float32 if i == 6 else jnp.bfloat16 for i in range(len(shapes))]
+    *tables, full_map, full_back, shift = pl.pallas_call(
+        functools.partial(tables_kernel, full_x=full_x),
         out_shape=[jax.ShapeDtypeStruct(*each) for each in zip(shapes, types)],
-        in_specs=whole(3),
+        in_specs=whole(1),
         out_specs=whole(len(shapes)),
         compiler_params=params(),
-        cost_estimate=takes(2),
-        name="prepare",
-    )(small, store, piece)
-    return tables, packed, full_map, full_back, shift, piece
+        cost_estimate=takes(1),
+        name="tables",
+    )(small)
+    return tables, full_map, full_back, shift
 
 
 def duplicate(values):
@@ -324,7 +326,7 @@
 
 
 def pack_kernel(*refs):
-    sources, (out_ref, small_ref), (*targets, sems) = refs[:6], refs[6:8], refs[8:]
+    sources, (out_ref, all_ref), (*targets, sems) = refs[:6], refs[6:8], refs[8:]
     copies = [pltpu.make_async_copy(*pair, sems.at[i]) for i, pair in enumerate(zip(sources, targets))]
     for copy in copies:
         copy.start()
@@ -341,14 +343,15 @@
             columns.append(spec_ref[pl.ds(group * 2 * modes + part, modes, stride=2)])
     lanes = out_ref.shape[1] - groups * spec_ref.shape[1]
     numbers = column_of(slots_ref, lambda i: (i % local_x, i // local_x), modes)
-    out_ref[...] = jnp.concatenate(columns + [numbers.astype(jnp.float32)], 1)
+    piece = jnp.concatenate(columns + [numbers.astype(jnp.float32)], 1)
+    out_ref[...] = piece
     modes_y, modes_x, channels = ky_ref.shape[0], kx_ref.shape[0], bias_ref.shape[0]
     ky = column_of(ky_ref, lambda i: (place_x ^ (i // local_y)) * local_y + i % local_y, modes_y)
     kx = column_of(kx_ref, lambda i: (place_y ^ (i // local_x)) * local_x + i % local_x, modes_x)
     bias = column_of(bias_ref, lambda i: i, channels)
     weight = weight_ref[...].astype(jnp.float32)
     weight = jnp.concatenate([weight, jnp.zeros((channels, lanes - channels), jnp.float32)], 1)
-    small_ref[...] = jnp.concatenate([ky.astype(jnp.float32), kx.astype(jnp.float32), bias, weight], 0)
+    all_ref[...] = jnp.concatenate([piece, ky.astype(jnp.float32), kx.astype(jnp.float32), bias, weight], 1)
 
 
 def pack(slots, spectrum, ky, kx, bias, weight, lanes):
@@ -356,12 +359,11 @@
     width = spectrum.size // modes + lanes
     sources = (slots, spectrum, ky, kx, bias, weight)
     held = (pltpu.SMEM, pltpu.VMEM, pltpu.SMEM, pltpu.SMEM, pltpu.SMEM, pltpu.VMEM)
-    rows = ky.shape[0] + kx.shape[0] + bias.shape[0] + weight.shape[0]
     return pl.pallas_call(
         pack_kernel,
         out_shape=[
             jax.ShapeDtypeStruct((modes, width), jnp.float32),
-            jax.ShapeDtypeStruct((rows, lanes), jnp.float32),
+            jax.ShapeDtypeStruct((modes, width + 4 * lanes), jnp.float32),
         ],
         in_specs=outside(6),
         out_specs=whole(2),
@@ -374,7 +376,7 @@
 
 def mix_kernel(packed_ref, *refs, count, local_x):
     pieces, refs = refs[:count], refs[count:]
-    kept_ref, slots_ref, same_ref, other_ref, out_ref, ra_ref, rb_ref, uc_ref, ud_ref = refs
+    kept_ref, slots_ref, same_ref, other_ref, out_ref, uc_ref, ud_ref = refs
     planes, channels, lanes = out_ref.shape
     place = place_of()[1]
     capacity = lanes // 2
@@ -396,28 +398,18 @@
         rows = pl.ds(plane * channels, channels)
         uc_ref[rows] = jnp.where(first, parts[plane, 0], parts[plane, 1])
         ud_ref[rows] = jnp.where(first, parts[plane, 1], parts[plane, 0])
-    for part in range(channels):
-        rows = pl.ds(part * channels, channels)
-        block = packed_ref[rows]
+    def step(channel, carry):
+        block = packed_ref[pl.ds(pl.multiple_of(channel * channels, channels), channels)]
         swapped = swap_halves(block)
-        low_half = lanes_of(block.shape) < capacity
-        ra_ref[rows] = jnp.where(low_half, block, swapped)
-        rb_ref[rows] = jnp.where(low_half, -swapped, block)
-
-    def step(channel, sums):
-        ra = ra_ref[pl.ds(channel, channels, stride=channels)]
-        rb = rb_ref[pl.ds(channel, channels, stride=channels)]
-        return tuple(
-            total
-            + ra * uc_ref[pl.ds(plane * channels + channel, 1)]
-            + rb * ud_ref[pl.ds(plane * channels + channel, 1)]
-            for plane, total in enumerate(sums)
-        )
-
-    zero = jnp.zeros((channels, lanes), jnp.float32)
-    sums = lax.fori_loop(0, channels, step, (zero,) * planes, unroll=4)
-    for plane in range(planes):
-        out_ref[plane] = sums[plane]
+        ra = jnp.where(first, block, swapped)
+        rb = jnp.where(first, -swapped, block)
+        for plane in range(planes):
+            rows = pl.ds(plane * channels, channels)
+            product = ra * uc_ref[rows] + rb * ud_ref[rows]
+            out_ref[plane, pl.ds(channel, 1)] = jnp.sum(product, 0, keepdims=True)
+        return carry
+
+    lax.fori_loop(0, channels, step, 0, unroll=4)
     for step in range(planes):
         (other_ref if step % 2 else same_ref)[step // 2] = out_ref[place ^ step]
 
@@ -436,7 +428,6 @@
         in_specs=whole(1 + count),
         out_specs=whole(4),
         scratch_shapes=[pltpu.VMEM((planes, channels, lanes), jnp.float32)]
-        + [pltpu.VMEM((channels * channels, lanes), jnp.float32)] * 2
         + [pltpu.VMEM((planes * channels, lanes), jnp.float32)] * 2,
         compiler_params=params(),
         cost_estimate=takes(3),
@@ -505,8 +496,10 @@
     )(kept, *pairs)
 
 
-def fill_selection(slots_ref, chosen_ref, modes_x, capacity, flip=0):
+def select_kernel(slots_ref, chosen_ref, *, modes_x):
+    capacity = slots_ref.shape[1] // 2
     lanes = 2 * capacity
+    place = place_of()[1]
     shape = (modes_x, lanes)
     lane = lanes_of(shape)
     first = lane < capacity
@@ -514,10 +507,22 @@
     for mode in range(slots_ref.shape[0] // modes_x):
         numbers = slots_ref[pl.ds(mode * modes_x, modes_x)]
         for owner in range(chosen_ref.shape[1] // lanes):
-            wanted = ((owner ^ flip) * capacity + lane % capacity).astype(jnp.float32)
+            wanted = ((owner ^ place) * capacity + lane % capacity).astype(jnp.float32)
             hit = jnp.where(numbers == wanted, 1.0, 0.0)
             both = jnp.concatenate([jnp.where(first, hit, zero), jnp.where(first, zero, hit)], 0)
             chosen_ref[pl.ds(mode * 2 * modes_x, 2 * modes_x), pl.ds(owner * lanes, lanes)] = both.astype(jnp.bfloat16)
+
+
+def select(slots, modes_x, count):
+    return pl.pallas_call(
+        functools.partial(select_kernel, modes_x=modes_x),
+        out_shape=jax.ShapeDtypeStruct((2 * slots.shape[0], count * slots.shape[1]), jnp.bfloat16),
+        in_specs=whole(1),
+        out_specs=whole(1)[0],
+        compiler_params=params(),
+        cost_estimate=takes(0.5),
+        name="select",
+    )(slots)
 
 
 def slots_to_modes(blocks, chosen_ref, out_ref, modes_x):
@@ -532,35 +537,42 @@
         out_ref[pl.ds(mode, half, stride=local_y)] = jnp.concatenate([piece[:half], piece[half:]], 1)
 
 
-def to_modes_kernel(slots_ref, *refs, modes_x):
-    *pairs, out_ref, chosen_ref = refs
-    lanes = pairs[0].shape[2]
-    fill_selection(slots_ref, chosen_ref, modes_x, lanes // 2, place_of()[1])
+def to_modes_kernel(chosen_ref, *refs, modes_x):
+    *pairs, out_ref = refs
     slots_to_modes([pair[core] for pair in pairs for core in range(2)], chosen_ref, out_ref, modes_x)
 
 
-def to_modes(slots, pairs, modes_x):
-    _, channels, lanes = pairs[0].shape
-    local_y = slots.shape[0] // modes_x
+def to_modes(chosen, pairs, modes_x):
+    _, channels, _ = pairs[0].shape
+    local_y = chosen.shape[0] // (2 * modes_x)
     return pl.pallas_call(
         functools.partial(to_modes_kernel, modes_x=modes_x),
         out_shape=jax.ShapeDtypeStruct((channels // 2 * local_y, 4 * modes_x), jnp.float32),
         in_specs=whole(1 + len(pairs)),
         out_specs=whole(1)[0],
-        scratch_shapes=[pltpu.VMEM((2 * slots.shape[0], 2 * len(pairs) * lanes), jnp.bfloat16)],
         compiler_params=params(),
         cost_estimate=takes(1),
         name="to_modes",
-    )(slots, *pairs)
-
-
-def adjoint_kernel(slots_ref, *refs, modes_x, blocks, count):
-    pieces, stores, refs = refs[:blocks], refs[blocks:-5], refs[-5:]
-    place = place_of()[1]
-    same_ref, other_ref, out_ref, chosen_ref, sum_ref = refs
-    _, channels, lanes = same_ref.shape
+    )(chosen, *pairs)
+
+
+def mix_back(store, row, values):
+    channels, lanes = values.shape
+    swapped = swap_halves(values)
+    real = jnp.zeros((channels, lanes), jnp.float32)
+    imag = real
+    for channel in range(channels):
+        block = store[pl.ds(row + channel * channels, channels)]
+        real = real + block * values[channel : channel + 1]
+        imag = imag + block * swapped[channel : channel + 1]
+    other_re, other_im = swap_halves(real), swap_halves(imag)
+    return jnp.where(lanes_of(real.shape) < lanes // 2, real + other_re, other_im - imag)
+
+
+def adjoint_kernel(chosen_ref, *refs, modes_x, blocks):
+    pieces, stores, (same_ref, other_ref, out_ref, sum_ref) = refs[:blocks], refs[blocks:-4], refs[-4:]
+    steps, channels, lanes = same_ref.shape
     half = channels // 2
-    fill_selection(slots_ref, chosen_ref, modes_x, lanes // 2, place)
     sum_ref[...] = sum(piece[...] for piece in pieces)
     local_y = sum_ref.shape[0] // half
     columns = []
@@ -571,43 +583,29 @@
     found = dot(jnp.concatenate([high, low], 0), chosen_ref[...])
     found = found[:channels] + found[channels:]
     mixed = []
-    for owner in range(count):
+    for owner in range(2 * steps):
         values = found[:, owner * lanes : (owner + 1) * lanes]
         (other_ref if owner % 2 else same_ref)[owner // 2] = values
-        swapped = swap_halves(values)
-        real = jnp.zeros((channels, lanes), jnp.float32)
-        imag = real
-        for channel in range(channels):
-            store, row = stores[owner], channel
-            if owner >= count - 2:
-                store, row = stores[owner + channel // half * 2], channel % half
-            block = store[pl.ds(row * channels, channels)]
-            real = real + block * values[channel : channel + 1]
-            imag = imag + block * swapped[channel : channel + 1]
-        other_re, other_im = swap_halves(real), swap_halves(imag)
-        first = lanes_of(real.shape) < lanes // 2
-        mixed.append(jnp.where(first, real + other_re, other_im - imag))
+        row = max(owner // 2 - 1, 0) * channels * channels
+        mixed.append(mix_back(stores[owner % 2 + (2 if owner > 1 else 0)], row, values))
     slots_to_modes(mixed, chosen_ref, out_ref, modes_x)
 
 
-def adjoint(slots, pieces, stores, modes_x):
-    count, blocks = len(stores) - 2, len(pieces)
-    lanes = stores[0].shape[1]
-    channels = 2 * pieces[0].shape[0] * modes_x // slots.shape[0]
-    return pl.pallas_call(
-        functools.partial(adjoint_kernel, modes_x=modes_x, blocks=blocks, count=count),
-        out_shape=[jax.ShapeDtypeStruct((count // 2, channels, lanes), jnp.float32)] * 2
+def adjoint(chosen, pieces, stores, modes_x):
+    blocks = len(pieces)
+    channels, lanes = math.isqrt(stores[0].shape[0]), stores[0].shape[1]
+    steps = chosen.shape[1] // (2 * lanes)
+    return pl.pallas_call(
+        functools.partial(adjoint_kernel, modes_x=modes_x, blocks=blocks),
+        out_shape=[jax.ShapeDtypeStruct((steps, channels, lanes), jnp.float32)] * 2
         + [jax.ShapeDtypeStruct(pieces[0].shape, jnp.float32)],
         in_specs=whole(1 + blocks + len(stores)),
         out_specs=whole(3),
-        scratch_shapes=[
-            pltpu.VMEM((2 * slots.shape[0], count * lanes), jnp.bfloat16),
-            pltpu.VMEM(pieces[0].shape, jnp.float32),
-        ],
-        compiler_params=params(),
-        cost_estimate=takes(3),
+        scratch_shapes=[pltpu.VMEM(pieces[0].shape, jnp.float32)],
+        compiler_params=params(),
+        cost_estimate=takes(2),
         name="adjoint",
-    )(slots, *pieces, *stores)
+    )(chosen, *pieces, *stores)
 
 
 def pair_kernel(same_ref, other_ref, *outs):
@@ -642,9 +640,30 @@
         in_specs=whole(2),
         out_specs=whole(2),
         compiler_params=params(),
-        cost_estimate=takes(0.3),
+        cost_estimate=takes(0.1),
         name="halves",
     )(first, second)
+
+
+def join_kernel(*refs):
+    *parts, out_ref = refs
+    start = 0
+    for part in parts:
+        out_ref[pl.ds(start, part.shape[0])] = part[...]
+        start += part.shape[0]
+
+
+def join(parts):
+    rows = sum(part.shape[0] for part in parts)
+    return pl.pallas_call(
+        join_kernel,
+        out_shape=jax.ShapeDtypeStruct((rows, parts[0].shape[1]), parts[0].dtype),
+        in_specs=whole(len(parts)),
+        out_specs=whole(1)[0],
+        compiler_params=params(),
+        cost_estimate=takes(0.1),
+        name="join",
+    )(*parts)
 
 
 def spread(small, rows, axis, channel_of):
@@ -814,7 +833,7 @@
         scratch_shapes=[pltpu.VMEM((blocks, half, local_y, 4 * rows_x), jnp.float32)] * 2
         + [pltpu.VMEM((2, rows_x, width), jnp.float32)] * 2,
         compiler_params=params(),
-        cost_estimate=takes(13),
+        cost_estimate=takes(8),
         name="slope_step",
     )(*pieces, xi, ti, tf, xf, mapped, cotangent)
     return results[:4], results[4:]
@@ -918,33 +937,32 @@
     store = jnp.transpose(weight_store, (1, 2, 3, 0))
     barrier = lax.optimization_barrier
     spectrum = jnp.transpose(spectrum_saved, (1, 2, 3, 4, 0)).reshape(-1, channels)
-    piece, small = pack(block_slot, spectrum, ky_modes, kx_modes, bias_vector, pointwise, lanes)
+    piece, everything = pack(block_slot, spectrum, ky_modes, kx_modes, bias_vector, pointwise, lanes)
     pieces = between_chips(piece, count_y)
     beside = exchange(piece, "py", count_y, 1)
-    tables, packed, full_map, full_back, shift, piece = prepare(
-        small, store, piece, full_x, rows_x, width_y, ky_modes.shape[0], modes_x
-    )
-    pieces, beside, tables, full_map, piece = barrier((pieces, beside, tables, full_map, piece))
+    piece, small, packed = unpack(everything, store, piece.shape[1])
+    pieces, beside, piece = barrier((pieces, beside, piece))
     pieces = between_cores([piece] + pieces[1:], count_y, beside)
     kept, slots, *mixed = mix(packed, pieces, planes, local_x)
+    chosen = select(slots, modes_x, count_y)
     pairs = to_owners(*mixed, count_y)
-    pairs, packed, beside = barrier((pairs, packed, exchange(packed, "py", count_y, 1)))
-    across = [exchange(packed, "py", count_y, step) for step in (2, 4)]
-    received = from_all(to_modes(slots, pairs, modes_x), "px", count_x)
+    beside = exchange(packed, "py", count_y, 1)
+    tables, full_map, full_back, shift = make_tables(small, full_x, rows_x, width_y, ky_modes.shape[0], modes_x)
+    pairs, chosen, full_map, packed, beside = barrier((pairs, chosen, full_map, packed, beside))
+    near = [exchange(packed, "py", count_y, step) for step in (2, 4)]
+    received = from_all(to_modes(chosen, pairs, modes_x), "px", count_x)
     mapped = pointwise_map(full_map, shift, field_in[:, 0])
-    received, mapped, across = barrier((received, mapped, across))
-    low, high = halves(*across)
+    received, mapped, near = barrier((received, mapped, near))
+    low, high = halves(*near)
     far = [exchange(low, "py", count_y, 4), exchange(high, "py", count_y, 2)]
-    other = [exchange(each, "py", count_y, 1) for each in across]
     terms, sums = slope_step(received, tables, mapped, cotangent[:, 0])
-    sums, terms, far, other = barrier((list(sums), list(terms), far, other))
+    sums, terms, far = barrier((list(sums), list(terms), far))
+    others = join(near + far)
+    others_beside = exchange(others, "py", count_y, 1)
     received = to_all(sums, "px", count_x)
     back = pointwise_back(full_back, terms)
-    stores = [packed, beside, across[0], other[0], across[1], other[1]]
-    low, high = far
-    stores += [low, exchange(low, "py", count_y, 1), high, exchange(high, "py", count_y, 1)]
-    received, back, stores = barrier((received, back, stores))
-    same, other, mixed = adjoint(slots, received, stores, modes_x)
+    received, back, others_beside = barrier((received, back, others_beside))
+    same, other, mixed = adjoint(chosen, received, [packed, beside, others, others_beside], modes_x)
     received = from_all(mixed, "px", count_x)
     pairs = to_owners(same, other, count_y)
     field_grad = finish(received, tables, back)

time: 77 us -> 75.9 us (0.986)
  local copies, waits for them, and re-layouts: 2.96 us -> 2.14 us
    unnamed x10 -> x8, local copies, waits for them, and re-layouts: 2.96 us -> 2.14 us
    ppermute x33 -> x30, waiting for transfers between devices: 14.2 us -> 13.9 us  [exchange(): return lax.ppermute(piece, axis, [(i, i ^ flip) for i in range(count)])]
    ppermute x33 -> x30, starting transfers between devices: 31.3 us -> 31 us  [exchange(): return lax.ppermute(piece, axis, [(i, i ^ flip) for i in range(count)])]
  transfers between devices with their start and end apart: 33 -> 30, of which waited for: 14 -> 14; matrix products, arithmetic and copies ran while one was open for 0% -> 0% of each run, Pallas kernels for 29% -> 29%
where the time goes in v2:
time: 75.9 us; the launch traced here: 75.7 us
  starting transfers between devices  31 us (41%)
  Pallas kernels  27.7 us (36%)
  waiting for transfers between devices  13.9 us (18%)
  local copies, waits for them, and re-layouts  2.14 us (3%)
  between operations  0.84 us (1%)
    ppermute x30, starting transfers between devices, exchange(): return lax.ppermute(piece, axis, [(i, i ^ flip) for i in range(count)])  31 us
    ppermute x30, waiting for transfers between devices, exchange(): return lax.ppermute(piece, axis, [(i, i ^ flip) for i in range(count)])  13.9 us
    pallas_call x1, Pallas kernels, slope_step(): pl.pallas_call(functools.partial(slope_kernel, blocks=blocks), out_shape=...  8.25 us
    pallas_call x1, Pallas kernels, finish(): pl.pallas_call(functools.partial(finish_kernel, blocks=blocks, group=grou...  4.4 us
    pallas_call x1, Pallas kernels, pointwise_back(): pl.pallas_call(pointwise_back_kernel, out_shape=jax.ShapeDtypeStruct((2 *...  3.52 us
    pallas_call x1, Pallas kernels, pointwise_map(): pl.pallas_call(pointwise_kernel, out_shape=jax.ShapeDtypeStruct(values.sh...  2.45 us
    unnamed x8, local copies, waits for them, and re-layouts  2.14 us
    pallas_call x1, Pallas kernels, weight_grad(): pl.pallas_call(weight_grad_kernel, out_shape=jax.ShapeDtypeStruct(shape,...  2.12 us
  transfers between devices with their start and end apart: 30, of which 14 were waited for; matrix products, arithmetic and copies ran while one was open for 0% of the time, Pallas kernels for 29%

profile of v2, /device:TPU:0, one launch (start us, length us, event | category | flops | bytes accessed | tf_op | source)
XLA Modules:
  0.0 75.7 jit_solution(13091631221684094229)
XLA Ops:
  0.6 1.8 %pack.1 = (f32[32,640]{1,0:T(8,128)}, f32[32,1152]{1,0:T(8,128)}) custom-call(s32[4,8]{1,0:T(4,128)} %refs_0_.1, f32[512,32]{1,0:T(8,128)} %bitcast.14, s32[32]{0:T(128)} %refs_2_.1, s32[32]{0:T(128)} %refs_3_.1, f32[32]{0:T(128)} %refs_4_.1, bf16[32,32]{1,0:T(8,128)(2,1)} %refs_5_.1), custom_call_target="tpu_custom_call" | custom-call | tf_op jit(solution)/shard_map/pack/pallas_call | solution.py:362
  2.5 3.0 %collective-permute-start = (f32[32,640]{1,0:T(8,128)}, f32[32,640]{1,0:T(8,128)S(1)}, u32[]{:S(2)}, u32[]{:S(2)}) collective-permute-start(f32[32,640]{1,0:T(8,128)} %get-tuple-element.77), channel_id=1, source_target_pairs={{0,2},{1,3},{2,0},{3,1},{4,6},{5,7},{6,4},{7,5},{8,10},{9,11},{10,... | collective-permute-start | bytes 245768 | tf_op jit(solution)/shard_map/ppermute | solution.py:895
  5.5 1.5 %collective-permute-start.1 = (f32[32,640]{1,0:T(8,128)}, f32[32,640]{1,0:T(8,128)S(1)}, u32[]{:S(2)}, u32[]{:S(2)}) collective-permute-start(f32[32,640]{1,0:T(8,128)} %get-tuple-element.77), channel_id=1, source_target_pairs={{0,4},{1,5},{2,6},{3,7},{4,0},{5,1},{6,2},{7,3},{8,12},{9,13},{10,... | collective-permute-start | bytes 245768 | tf_op jit(solution)/shard_map/ppermute | solution.py:895
  7.0 0.0 collective-permute-start.2
  7.0 0.0 collective-permute-start.3
  7.0 1.2 %copy-done.2 = f32[64,2,32,32]{0,3,2,1:T(8,128)S(1)} copy-done((f32[64,2,32,32]{0,3,2,1:T(8,128)S(1)}, f32[64,2,32,32]{0,3,2,1:T(8,128)}, u32[]{:S(2)}) %copy-start.2) | copy-done | bytes 524312
  8.3 0.9 %copy-done.3 = f32[32,1152]{1,0:T(8,128)S(1)} copy-done((f32[32,1152]{1,0:T(8,128)S(1)}, f32[32,1152]{1,0:T(8,128)}, u32[]{:S(2)}) %copy-start.3) | copy-done | bytes 147480
  9.2 0.2 unpack.1
  9.4 0.0 collective-permute-done.refs_2_
  9.4 1.6 %collective-permute-done.1.refs_4_ = f32[32,640]{1,0:T(8,128)S(1)} collective-permute-done((f32[32,640]{1,0:T(8,128)}, f32[32,640]{1,0:T(8,128)S(1)}, u32[]{:S(2)}, u32[]{:S(2)}) %collective-permute-start.1) | collective-permute-done | bytes 81952 | tf_op jit(solution)/shard_map/ppermute | solution.py:895
  11.0 1.5 %collective-permute-done.2.refs_6_ = f32[32,640]{1,0:T(8,128)S(1)} collective-permute-done((f32[32,640]{1,0:T(8,128)}, f32[32,640]{1,0:T(8,128)S(1)}, u32[]{:S(2)}, u32[]{:S(2)}) %collective-permute-start.2) | collective-permute-done | bytes 81952 | tf_op jit(solution)/shard_map/ppermute | solution.py:895
  12.6 0.0 collective-permute-done.3.refs_1_
  12.6 0.0 collective-permute-start.4
  12.6 0.5 collective-permute-start.5
  13.1 0.0 collective-permute-start.6
  13.1 0.5 collective-permute-start.11
  13.6 0.3 collective-permute-done.4.refs_3_
  13.8 0.2 collective-permute-done.5.refs_5_
  14.0 0.4 collective-permute-done.6.refs_7_
  14.3 1.8 %mix.1 = (f32[512,128]{1,0:T(8,128)S(1)}, f32[256,128]{1,0:T(8,128)S(1)}, f32[4,32,128]{2,1,0:T(8,128)S(1)}, f32[4,32,128]{2,1,0:T(8,128)S(1)}) custom-call(f32[1024,128]{1,0:T(8,128)S(1)} %get-tuple-element.100.packed_ref.refs_4_, f32[32,640]{1,0:T(8,128)S(1)} %get-tuple-element.79.refs_0_, f32[32,640]{1,0:T(8,128)S(1)} %collective-permute-done.3.refs_1_, ...), custom_call_target="tpu_custom_call" | custom-call | flops 3000000000 | bytes 1048576 | tf_op jit(solution)/shard_map/mix/pallas_call | solution.py:420
  16.2 0.2 collective-permute-start.7
  16.4 0.8 %tables.1 = (bf16[2,256,512]{2,1,0:T(8,128)(2,1)S(1)}, bf16[128,512]{1,0:T(8,128)(2,1)S(1)}, bf16[384,512]{1,0:T(8,128)(2,1)S(1)}, bf16[512,256]{1,0:T(8,128)(2,...) custom-call(f32[32,512]{1,0:T(8,128)S(1)} %get-tuple-element.91.small_ref), custom_call_target="tpu_custom_call" | custom-call | flops 1000000000 | bytes 1048576 | tf_op jit(solution)/shard_map/tables/pallas_call | solution.py:312
  17.2 0.3 collective-permute-done.7.other_ref
  17.5 0.6 collective-permute-start.8
  18.1 0.6 collective-permute-start.9
  18.7 2.3 %collective-permute-start.10 = (f32[2,32,128]{2,1,0:T(8,128)S(1)}, f32[2,32,128]{2,1,0:T(8,128)S(1)}, u32[]{:S(2)}, u32[]{:S(2)}) collective-permute-start(f32[2,32,128]{2,1,0:T(8,128)S(1)} %get-tuple-element.89), channel_id=1, source_target_pairs={{0,6},{1,7},{2,4},{3,5},{4,2},{5,3},{6,0},{7,1},{8,14},{9,15},{10,... | collective-permute-start | bytes 98312 | tf_op jit(solution)/shard_map/ppermute | solution.py:895
  21.1 0.2 select.1.chosen_ref
  21.3 0.2 collective-permute-done.8.refs_1_
  21.5 0.9 %collective-permute-done.9.refs_2_ = f32[2,32,128]{2,1,0:T(8,128)S(1)} collective-permute-done((f32[2,32,128]{2,1,0:T(8,128)S(1)}, f32[2,32,128]{2,1,0:T(8,128)S(1)}, u32[]{:S(2)}, u32[]{:S(2)}) %collective-permute-start.9) | collective-permute-done | bytes 32800 | tf_op jit(solution)/shard_map/ppermute | solution.py:895
  22.4 1.2 %collective-permute-done.10.refs_3_ = f32[2,32,128]{2,1,0:T(8,128)S(1)} collective-permute-done((f32[2,32,128]{2,1,0:T(8,128)S(1)}, f32[2,32,128]{2,1,0:T(8,128)S(1)}, u32[]{:S(2)}, u32[]{:S(2)}) %collective-permute-start.10) | collective-permute-done | bytes 32800 | tf_op jit(solution)/shard_map/ppermute | solution.py:895
  23.6 0.0 collective-permute-done.11.refs_5_
  23.6 1.4 %collective-permute-start.15 = (f32[1024,128]{1,0:T(8,128)S(1)}, f32[1024,128]{1,0:T(8,128)S(1)}, u32[]{:S(2)}, u32[]{:S(2)}) collective-permute-start(f32[1024,128]{1,0:T(8,128)S(1)} %get-tuple-element.100.packed_ref.refs_4_), channel_id=1, source_target_pairs={{0,2},{1,3},{2,0},{3,1},{4,6},{5,7},{6,4},{7,5},{8,10},{9,11},{10,... | collective-permute-start | bytes 1572872 | tf_op jit(solution)/shard_map/ppermute | solution.py:895
  25.0 1.5 %collective-permute-start.16 = (f32[1024,128]{1,0:T(8,128)S(1)}, f32[1024,128]{1,0:T(8,128)S(1)}, u32[]{:S(2)}, u32[]{:S(2)}) collective-permute-start(f32[1024,128]{1,0:T(8,128)S(1)} %get-tuple-element.100.packed_ref.refs_4_), channel_id=1, source_target_pairs={{0,4},{1,5},{2,6},{3,7},{4,0},{5,1},{6,2},{7,3},{8,12},{9,13},{10,... | collective-permute-start | bytes 1572872 | tf_op jit(solution)/shard_map/ppermute | solution.py:895
  26.4 0.5 to_modes.1.refs_0_
  27.0 1.6 %collective-permute-start.12 = (f32[128,128]{1,0:T(8,128)S(1)}, f32[128,128]{1,0:T(8,128)S(1)}, u32[]{:S(2)}, u32[]{:S(2)}) collective-permute-start(f32[128,128]{1,0:T(8,128)S(1)} %to_modes.1.refs_0_), channel_id=1, source_target_pairs={{0,8},{8,0},{16,24},{24,16},{1,9},{9,1},{17,25},{25,17},{2,10},{10... | collective-permute-start | bytes 196616 | tf_op jit(solution)/shard_map/ppermute | solution.py:895
  28.6 2.6 %collective-permute-start.13 = (f32[128,128]{1,0:T(8,128)S(1)}, f32[128,128]{1,0:T(8,128)S(1)}, u32[]{:S(2)}, u32[]{:S(2)}) collective-permute-start(f32[128,128]{1,0:T(8,128)S(1)} %to_modes.1.refs_0_), channel_id=1, source_target_pairs={{0,16},{8,24},{16,0},{24,8},{1,17},{9,25},{17,1},{25,9},{2,18},{10... | collective-permute-start | bytes 196616 | tf_op jit(solution)/shard_map/ppermute | solution.py:895
  31.2 0.2 collective-permute-start.14
  31.4 2.4 %pointwise_map.1.refs_8_ = f32[32,128,512]{2,1,0:T(8,128)S(1)} custom-call(bf16[256,256]{1,0:T(8,128)(2,1)S(1)} %get-tuple-element.98.full_ref, f32[256,128]{1,0:T(8,128)S(1)} %get-tuple-element.99.shift_ref, bf16[32,128,512]{2,1,0:T(8,128)(2,1)S(1)} %bitcast.10), custom_call_target="tpu_custom_call" | custom-call | flops 3000000000 | bytes 1048576 | tf_op jit(solution)/shard_map/pointwise_map/pallas_call | solution.py:698
  33.9 0.0 collective-permute-done.12.refs_1_
  33.9 1.2 %collective-permute-done.13.refs_2_ = f32[128,128]{1,0:T(8,128)S(1)} collective-permute-done((f32[128,128]{1,0:T(8,128)S(1)}, f32[128,128]{1,0:T(8,128)S(1)}, u32[]{:S(2)}, u32[]{:S(2)}) %collective-permute-start.13) | collective-permute-done | bytes 65568 | tf_op jit(solution)/shard_map/ppermute | solution.py:895
  35.1 2.2 %collective-permute-done.14.refs_3_ = f32[128,128]{1,0:T(8,128)S(1)} collective-permute-done((f32[128,128]{1,0:T(8,128)S(1)}, f32[128,128]{1,0:T(8,128)S(1)}, u32[]{:S(2)}, u32[]{:S(2)}) %collective-permute-start.14) | collective-permute-done | bytes 65568 | tf_op jit(solution)/shard_map/ppermute | solution.py:895
  37.3 1.2 %collective-permute-start.17 = (f32[512,128]{1,0:T(8,128)S(1)}, f32[512,128]{1,0:T(8,128)S(1)}, u32[]{:S(2)}, u32[]{:S(2)}) collective-permute-start(f32[512,128]{1,0:T(8,128)S(1)} %get-tuple-element.120), channel_id=1, source_target_pairs={{0,4},{1,5},{2,6},{3,7},{4,0},{5,1},{6,2},{7,3},{8,12},{9,13},{10,... | collective-permute-start | bytes 786440 | tf_op jit(solution)/shard_map/ppermute | solution.py:895
  38.5 0.5 collective-permute-start.18
  39.1 8.3 %slope_step.1 = (bf16[8,2,128,512]{3,2,1,0:T(8,128)(2,1)S(1)}, bf16[8,2,128,512]{3,2,1,0:T(8,128)(2,1)S(1)}, bf16[8,2,128,512]{3,2,1,0:T(8,128)(2,1)S(1)}, bf16[...) custom-call(f32[128,128]{1,0:T(8,128)S(1)} %to_modes.1.refs_0_, ...), custom_call_target="tpu_custom_call" | custom-call | flops 8000000000 | bytes 1048576 | tf_op jit(solution)/shard_map/slope_step/pallas_call | solution.py:827
  47.3 0.0 collective-permute-done.17.refs_2_
  47.4 0.1 join.1.refs_6_
  47.5 0.1 collective-permute-start.22
  47.5 1.6 %collective-permute-start.19 = (f32[128,128]{1,0:T(8,128)S(1)}, f32[128,128]{1,0:T(8,128)S(1)}, u32[]{:S(2)}, u32[]{:S(2)}) collective-permute-start(f32[128,128]{1,0:T(8,128)S(1)} %get-tuple-element.123), channel_id=1, source_target_pairs={{0,8},{8,0},{16,24},{24,16},{1,9},{9,1},{17,25},{25,17},{2,10},{10... | collective-permute-start | bytes 196616 | tf_op jit(solution)/shard_map/ppermute | solution.py:895
  49.2 2.6 %collective-permute-start.20 = (f32[128,128]{1,0:T(8,128)S(1)}, f32[128,128]{1,0:T(8,128)S(1)}, u32[]{:S(2)}, u32[]{:S(2)}) collective-permute-start(f32[128,128]{1,0:T(8,128)S(1)} %get-tuple-element.124), channel_id=1, source_target_pairs={{0,16},{8,24},{16,0},{24,8},{1,17},{9,25},{17,1},{25,9},{2,18},{10... | collective-permute-start | bytes 196616 | tf_op jit(solution)/shard_map/ppermute | solution.py:895
  51.8 0.2 collective-permute-start.21
  52.0 3.5 %pointwise_back.1.refs_6_ = f32[32,128,512]{2,1,0:T(8,128)S(1)} custom-call(bf16[256,256]{1,0:T(8,128)(2,1)S(1)} %get-tuple-element.126.full_ref, bf16[8,2,128,512]{3,2,1,0:T(8,128)(2,1)S(1)} %get-tuple-element.127.refs_0_, bf16[8,2,128,512]{3,2,1,0:T(8,128)(2,1)S(1)} %get-tuple-element.128.refs_1_, bf16[8,2,128,512]{3,2,1,0:T(8,128)(2,1)S(1)} %get-tuple-element.129.refs_2_, ...), custom_call_target="tpu_custom_call" | custom-call | flops 4000000000 | bytes 1048576 | tf_op jit(solution)/shard_map/pointwise_back/pallas_call | solution.py:733
  55.5 1.4 %collective-permute-done.20.refs_2_ = f32[128,128]{1,0:T(8,128)S(1)} collective-permute-done((f32[128,128]{1,0:T(8,128)S(1)}, f32[128,128]{1,0:T(8,128)S(1)}, u32[]{:S(2)}, u32[]{:S(2)}) %collective-permute-start.20) | collective-permute-done | bytes 65568 | tf_op jit(solution)/shard_map/ppermute | solution.py:895
  56.9 1.0 %collective-permute-done.21.refs_3_ = f32[128,128]{1,0:T(8,128)S(1)} collective-permute-done((f32[128,128]{1,0:T(8,128)S(1)}, f32[128,128]{1,0:T(8,128)S(1)}, u32[]{:S(2)}, u32[]{:S(2)}) %collective-permute-start.21) | collective-permute-done | bytes 65568 | tf_op jit(solution)/shard_map/ppermute | solution.py:895
  57.9 1.4 %adjoint.1 = (f32[4,32,128]{2,1,0:T(8,128)S(1)}, f32[4,32,128]{2,1,0:T(8,128)S(1)}, f32[128,128]{1,0:T(8,128)S(1)}) custom-call(bf16[512,1024]{1,0:T(8,128)(2,1)S(1)} %select.1.chosen_ref, f32[128,128]{1,0:T(8,128)S(1)} %get-tuple-element.133.refs_0_, f32[128,128]{1,0:T(8,128)S(1)} %collective-permute-done.19.refs_1_, ...), custom_call_target="tpu_custom_call" | custom-call | flops 2000000000 | bytes 1048576 | tf_op jit(solution)/shard_map/adjoint/pallas_call | solution.py:598
  59.3 0.1 collective-permute-start.26
  59.4 1.3 %collective-permute-start.23 = (f32[128,128]{1,0:T(8,128)S(1)}, f32[128,128]{1,0:T(8,128)S(1)}, u32[]{:S(2)}, u32[]{:S(2)}) collective-permute-start(f32[128,128]{1,0:T(8,128)S(1)} %get-tuple-element.139.refs_0_), channel_id=1, source_target_pairs={{0,8},{8,0},{16,24},{24,16},{1,9},{9,1},{17,25},{25,17},{2,10},{10... | collective-permute-start | bytes 196616 | tf_op jit(solution)/shard_map/ppermute | solution.py:895
  60.7 1.7 %collective-permute-start.24 = (f32[128,128]{1,0:T(8,128)S(1)}, f32[128,128]{1,0:T(8,128)S(1)}, u32[]{:S(2)}, u32[]{:S(2)}) collective-permute-start(f32[128,128]{1,0:T(8,128)S(1)} %get-tuple-element.139.refs_0_), channel_id=1, source_target_pairs={{0,16},{8,24},{16,0},{24,8},{1,17},{9,25},{17,1},{25,9},{2,18},{10... | collective-permute-start | bytes 196616 | tf_op jit(solution)/shard_map/ppermute | solution.py:895
  62.4 1.5 %collective-permute-start.25 = (f32[128,128]{1,0:T(8,128)S(1)}, f32[128,128]{1,0:T(8,128)S(1)}, u32[]{:S(2)}, u32[]{:S(2)}) collective-permute-start(f32[128,128]{1,0:T(8,128)S(1)} %get-tuple-element.139.refs_0_), channel_id=1, source_target_pairs={{0,24},{8,16},{16,8},{24,0},{1,25},{9,17},{17,9},{25,1},{2,26},{10... | collective-permute-start | bytes 196616 | tf_op jit(solution)/shard_map/ppermute | solution.py:895
  63.9 1.6 %collective-permute-start.27 = (f32[2,32,128]{2,1,0:T(8,128)S(1)}, f32[2,32,128]{2,1,0:T(8,128)S(1)}, u32[]{:S(2)}, u32[]{:S(2)}) collective-permute-start(f32[2,32,128]{2,1,0:T(8,128)S(1)} %get-tuple-element.145), channel_id=1, source_target_pairs={{0,2},{1,3},{2,0},{3,1},{4,6},{5,7},{6,4},{7,5},{8,10},{9,11},{10,... | collective-permute-start | bytes 98312 | tf_op jit(solution)/shard_map/ppermute | solution.py:895
  65.4 0.7 collective-permute-start.28
  66.1 1.3 %collective-permute-start.29 = (f32[2,32,128]{2,1,0:T(8,128)S(1)}, f32[2,32,128]{2,1,0:T(8,128)S(1)}, u32[]{:S(2)}, u32[]{:S(2)}) collective-permute-start(f32[2,32,128]{2,1,0:T(8,128)S(1)} %get-tuple-element.147), channel_id=1, source_target_pairs={{0,6},{1,7},{2,4},{3,5},{4,2},{5,3},{6,0},{7,1},{8,14},{9,15},{10,... | collective-permute-start | bytes 98312 | tf_op jit(solution)/shard_map/ppermute | solution.py:895
  67.4 1.7 %collective-permute-done.24.refs_2_ = f32[128,128]{1,0:T(8,128)S(1)} collective-permute-done((f32[128,128]{1,0:T(8,128)S(1)}, f32[128,128]{1,0:T(8,128)S(1)}, u32[]{:S(2)}, u32[]{:S(2)}) %collective-permute-start.24) | collective-permute-done | bytes 65568 | tf_op jit(solution)/shard_map/ppermute | solution.py:895
  69.1 4.4 %finish.1 = f32[32,128,512]{2,1,0:T(8,128)} custom-call(f32[128,128]{1,0:T(8,128)S(1)} %get-tuple-element.139.refs_0_, f32[128,128]{1,0:T(8,128)S(1)} %collective-permute-done.23.refs_1_, f32[128,128]{1,0:T(8,128)S(1)} %collective-permute-done.24.refs_2_, f32[128,128]{1,0:T(8,128)S(1)} %collective-permute-done.25.refs_3_, ...), custom_call_target="tpu_custom_call" | custom-call | flops 4000000000 | bytes 1048576 | tf_op jit(solution)/shard_map/finish/pallas_call | solution.py:878
  73.5 2.1 %weight_grad.1 = f32[2,32,32,64]{3,2,1,0:T(8,128)} custom-call(f32[512,128]{1,0:T(8,128)S(1)} %get-tuple-element.141.kept_ref, f32[2,32,128]{2,1,0:T(8,128)S(1)} %get-tuple-element.144.refs_0_, f32[2,32,128]{2,1,0:T(8,128)S(1)} %collective-permute-done.27.refs_1_, f32[2,32,128]{2,1,0:T(8,128)S(1)} %collective-permute-done.28.refs_2_, ...), custom_call_target="tpu_custom_call" | custom-call | flops 2000000000 | bytes 1048576 | tf_op jit(solution)/shard_map/weight_grad/pallas_call | solution.py:483
  (20 shorter events, 0.1 us)
Async XLA Ops:
  2.5 6.9 %collective-permute-start = (f32[32,640]{1,0:T(8,128)}, f32[32,640]{1,0:T(8,128)S(1)}, u32[]{:S(2)}, u32[]{:S(2)}) collective-permute-start(f32[32,640]{1,0:T(8,128)} %get-tuple-element.77), channel_id=1, source_target_pairs={{0,2},{1,3},{2,0},{3,1},{4,6},{5,7},{6,4},{7,5},{8,10},{9,11},{10,... | collective-permute-start | bytes 245768 | tf_op jit(solution)/shard_map/ppermute | solution.py:895
  5.5 5.5 %collective-permute-start.1 = (f32[32,640]{1,0:T(8,128)}, f32[32,640]{1,0:T(8,128)S(1)}, u32[]{:S(2)}, u32[]{:S(2)}) collective-permute-start(f32[32,640]{1,0:T(8,128)} %get-tuple-element.77), channel_id=1, source_target_pairs={{0,4},{1,5},{2,6},{3,7},{4,0},{5,1},{6,2},{7,3},{8,12},{9,13},{10,... | collective-permute-start | bytes 245768 | tf_op jit(solution)/shard_map/ppermute | solution.py:895
  7.0 5.6 %collective-permute-start.2 = (f32[32,640]{1,0:T(8,128)}, f32[32,640]{1,0:T(8,128)S(1)}, u32[]{:S(2)}, u32[]{:S(2)}) collective-permute-start(f32[32,640]{1,0:T(8,128)} %get-tuple-element.77), channel_id=1, source_target_pairs={{0,6},{1,7},{2,4},{3,5},{4,2},{5,3},{6,0},{7,1},{8,14},{9,15},{10,... | collective-permute-start | bytes 245768 | tf_op jit(solution)/shard_map/ppermute | solution.py:895
  7.0 5.5 %collective-permute-start.3 = (f32[32,640]{1,0:T(8,128)}, f32[32,640]{1,0:T(8,128)S(1)}, u32[]{:S(2)}, u32[]{:S(2)}) collective-permute-start(f32[32,640]{1,0:T(8,128)} %get-tuple-element.77), channel_id=1, source_target_pairs={{0,1},{1,0},{2,3},{3,2},{4,5},{5,4},{6,7},{7,6},{8,9},{9,8},{10,11... | collective-permute-start | bytes 245768 | tf_op jit(solution)/shard_map/ppermute | solution.py:895
  7.0 1.2 %copy-start.2 = (f32[64,2,32,32]{0,3,2,1:T(8,128)S(1)}, f32[64,2,32,32]{0,3,2,1:T(8,128)}, u32[]{:S(2)}) copy-start(f32[64,2,32,32]{0,3,2,1:T(8,128)} %param.12) | copy-start | bytes 1572868
  8.2 0.9 %copy-start.3 = (f32[32,1152]{1,0:T(8,128)S(1)}, f32[32,1152]{1,0:T(8,128)}, u32[]{:S(2)}) copy-start(f32[32,1152]{1,0:T(8,128)} %get-tuple-element.75.all_ref) | copy-start | bytes 442372
  12.6 1.3 %collective-permute-start.4 = (f32[32,640]{1,0:T(8,128)S(1)}, f32[32,640]{1,0:T(8,128)S(1)}, u32[]{:S(2)}, u32[]{:S(2)}) collective-permute-start(f32[32,640]{1,0:T(8,128)S(1)} %collective-permute-done.refs_2_), channel_id=1, source_target_pairs={{0,1},{1,0},{2,3},{3,2},{4,5},{5,4},{6,7},{7,6},{8,9},{9,8},{10,11... | collective-permute-start | bytes 245768 | tf_op jit(solution)/shard_map/ppermute | solution.py:895
  12.6 1.4 %collective-permute-start.5 = (f32[32,640]{1,0:T(8,128)S(1)}, f32[32,640]{1,0:T(8,128)S(1)}, u32[]{:S(2)}, u32[]{:S(2)}) collective-permute-start(f32[32,640]{1,0:T(8,128)S(1)} %collective-permute-done.1.refs_4_), channel_id=1, source_target_pairs={{0,1},{1,0},{2,3},{3,2},{4,5},{5,4},{6,7},{7,6},{8,9},{9,8},{10,11... | collective-permute-start | bytes 245768 | tf_op jit(solution)/shard_map/ppermute | solution.py:895
  13.1 1.3 %collective-permute-start.6 = (f32[32,640]{1,0:T(8,128)S(1)}, f32[32,640]{1,0:T(8,128)S(1)}, u32[]{:S(2)}, u32[]{:S(2)}) collective-permute-start(f32[32,640]{1,0:T(8,128)S(1)} %collective-permute-done.2.refs_6_), channel_id=1, source_target_pairs={{0,1},{1,0},{2,3},{3,2},{4,5},{5,4},{6,7},{7,6},{8,9},{9,8},{10,11... | collective-permute-start | bytes 245768 | tf_op jit(solution)/shard_map/ppermute | solution.py:895
  13.1 10.5 %collective-permute-start.11 = (f32[1024,128]{1,0:T(8,128)S(1)}, f32[1024,128]{1,0:T(8,128)S(1)}, u32[]{:S(2)}, u32[]{:S(2)}) collective-permute-start(f32[1024,128]{1,0:T(8,128)S(1)} %get-tuple-element.100.packed_ref.refs_4_), channel_id=1, source_target_pairs={{0,1},{1,0},{2,3},{3,2},{4,5},{5,4},{6,7},{7,6},{8,9},{9,8},{10,11... | collective-permute-start | bytes 1572872 | tf_op jit(solution)/shard_map/ppermute | solution.py:895
  16.2 1.3 %collective-permute-start.7 = (f32[4,32,128]{2,1,0:T(8,128)S(1)}, f32[4,32,128]{2,1,0:T(8,128)S(1)}, u32[]{:S(2)}, u32[]{:S(2)}) collective-permute-start(f32[4,32,128]{2,1,0:T(8,128)S(1)} %get-tuple-element.85), channel_id=1, source_target_pairs={{0,1},{1,0},{2,3},{3,2},{4,5},{5,4},{6,7},{7,6},{8,9},{9,8},{10,11... | collective-permute-start | bytes 196616 | tf_op jit(solution)/shard_map/ppermute | solution.py:895
  17.5 4.0 %collective-permute-start.8 = (f32[2,32,128]{2,1,0:T(8,128)S(1)}, f32[2,32,128]{2,1,0:T(8,128)S(1)}, u32[]{:S(2)}, u32[]{:S(2)}) collective-permute-start(f32[2,32,128]{2,1,0:T(8,128)S(1)} %get-tuple-element.87), channel_id=1, source_target_pairs={{0,2},{1,3},{2,0},{3,1},{4,6},{5,7},{6,4},{7,5},{8,10},{9,11},{10,... | collective-permute-start | bytes 98312 | tf_op jit(solution)/shard_map/ppermute | solution.py:895
  18.1 4.3 %collective-permute-start.9 = (f32[2,32,128]{2,1,0:T(8,128)S(1)}, f32[2,32,128]{2,1,0:T(8,128)S(1)}, u32[]{:S(2)}, u32[]{:S(2)}) collective-permute-start(f32[2,32,128]{2,1,0:T(8,128)S(1)} %get-tuple-element.88), channel_id=1, source_target_pairs={{0,4},{1,5},{2,6},{3,7},{4,0},{5,1},{6,2},{7,3},{8,12},{9,13},{10,... | collective-permute-start | bytes 98312 | tf_op jit(solution)/shard_map/ppermute | solution.py:895
  18.7 4.8 %collective-permute-start.10 = (f32[2,32,128]{2,1,0:T(8,128)S(1)}, f32[2,32,128]{2,1,0:T(8,128)S(1)}, u32[]{:S(2)}, u32[]{:S(2)}) collective-permute-start(f32[2,32,128]{2,1,0:T(8,128)S(1)} %get-tuple-element.89), channel_id=1, source_target_pairs={{0,6},{1,7},{2,4},{3,5},{4,2},{5,3},{6,0},{7,1},{8,14},{9,15},{10,... | collective-permute-start | bytes 98312 | tf_op jit(solution)/shard_map/ppermute | solution.py:895
  21.1 10.4 %copy-start = (bf16[32,1,128,512]{3,2,1,0:T(8,128)(2,1)S(1)}, bf16[32,1,128,512]{3,2,1,0:T(8,128)(2,1)}, u32[]{:S(2)}) copy-start(bf16[32,1,128,512]{3,2,1,0:T(8,128)(2,1)} %param.9) | copy-start | bytes 12582916
  23.6 13.7 %collective-permute-start.15 = (f32[1024,128]{1,0:T(8,128)S(1)}, f32[1024,128]{1,0:T(8,128)S(1)}, u32[]{:S(2)}, u32[]{:S(2)}) collective-permute-start(f32[1024,128]{1,0:T(8,128)S(1)} %get-tuple-element.100.packed_ref.refs_4_), channel_id=1, source_target_pairs={{0,2},{1,3},{2,0},{3,1},{4,6},{5,7},{6,4},{7,5},{8,10},{9,11},{10,... | collective-permute-start | bytes 1572872 | tf_op jit(solution)/shard_map/ppermute | solution.py:895
  25.0 12.3 %collective-permute-start.16 = (f32[1024,128]{1,0:T(8,128)S(1)}, f32[1024,128]{1,0:T(8,128)S(1)}, u32[]{:S(2)}, u32[]{:S(2)}) collective-permute-start(f32[1024,128]{1,0:T(8,128)S(1)} %get-tuple-element.100.packed_ref.refs_4_), channel_id=1, source_target_pairs={{0,4},{1,5},{2,6},{3,7},{4,0},{5,1},{6,2},{7,3},{8,12},{9,13},{10,... | collective-permute-start | bytes 1572872 | tf_op jit(solution)/shard_map/ppermute | solution.py:895
  27.0 6.9 %collective-permute-start.12 = (f32[128,128]{1,0:T(8,128)S(1)}, f32[128,128]{1,0:T(8,128)S(1)}, u32[]{:S(2)}, u32[]{:S(2)}) collective-permute-start(f32[128,128]{1,0:T(8,128)S(1)} %to_modes.1.refs_0_), channel_id=1, source_target_pairs={{0,8},{8,0},{16,24},{24,16},{1,9},{9,1},{17,25},{25,17},{2,10},{10... | collective-permute-start | bytes 196616 | tf_op jit(solution)/shard_map/ppermute | solution.py:895
  28.6 6.5 %collective-permute-start.13 = (f32[128,128]{1,0:T(8,128)S(1)}, f32[128,128]{1,0:T(8,128)S(1)}, u32[]{:S(2)}, u32[]{:S(2)}) collective-permute-start(f32[128,128]{1,0:T(8,128)S(1)} %to_modes.1.refs_0_), channel_id=1, source_target_pairs={{0,16},{8,24},{16,0},{24,8},{1,17},{9,25},{17,1},{25,9},{2,18},{10... | collective-permute-start | bytes 196616 | tf_op jit(solution)/shard_map/ppermute | solution.py:895
  31.2 6.1 %collective-permute-start.14 = (f32[128,128]{1,0:T(8,128)S(1)}, f32[128,128]{1,0:T(8,128)S(1)}, u32[]{:S(2)}, u32[]{:S(2)}) collective-permute-start(f32[128,128]{1,0:T(8,128)S(1)} %to_modes.1.refs_0_), channel_id=1, source_target_pairs={{0,24},{8,16},{16,8},{24,0},{1,25},{9,17},{17,9},{25,1},{2,26},{10... | collective-permute-start | bytes 196616 | tf_op jit(solution)/shard_map/ppermute | solution.py:895
  31.4 7.7 %copy-start.1 = (bf16[32,1,128,512]{3,2,1,0:T(8,128)(2,1)S(1)}, bf16[32,1,128,512]{3,2,1,0:T(8,128)(2,1)}, u32[]{:S(2)}) copy-start(bf16[32,1,128,512]{3,2,1,0:T(8,128)(2,1)} %param.10) | copy-start | bytes 12582916
  37.3 10.0 %collective-permute-start.17 = (f32[512,128]{1,0:T(8,128)S(1)}, f32[512,128]{1,0:T(8,128)S(1)}, u32[]{:S(2)}, u32[]{:S(2)}) collective-permute-start(f32[512,128]{1,0:T(8,128)S(1)} %get-tuple-element.120), channel_id=1, source_target_pairs={{0,4},{1,5},{2,6},{3,7},{4,0},{5,1},{6,2},{7,3},{8,12},{9,13},{10,... | collective-permute-start | bytes 786440 | tf_op jit(solution)/shard_map/ppermute | solution.py:895
  38.5 8.8 %collective-permute-start.18 = (f32[512,128]{1,0:T(8,128)S(1)}, f32[512,128]{1,0:T(8,128)S(1)}, u32[]{:S(2)}, u32[]{:S(2)}) collective-permute-start(f32[512,128]{1,0:T(8,128)S(1)} %get-tuple-element.121), channel_id=1, source_target_pairs={{0,2},{1,3},{2,0},{3,1},{4,6},{5,7},{6,4},{7,5},{8,10},{9,11},{10,... | collective-permute-start | bytes 786440 | tf_op jit(solution)/shard_map/ppermute | solution.py:895
  47.5 10.4 %collective-permute-start.22 = (f32[3072,128]{1,0:T(8,128)S(1)}, f32[3072,128]{1,0:T(8,128)S(1)}, u32[]{:S(2)}, u32[]{:S(2)}) collective-permute-start(f32[3072,128]{1,0:T(8,128)S(1)} %join.1.refs_6_), channel_id=1, source_target_pairs={{0,1},{1,0},{2,3},{3,2},{4,5},{5,4},{6,7},{7,6},{8,9},{9,8},{10,11... | collective-permute-start | bytes 4718600 | tf_op jit(solution)/shard_map/ppermute | solution.py:895
  47.5 8.0 %collective-permute-start.19 = (f32[128,128]{1,0:T(8,128)S(1)}, f32[128,128]{1,0:T(8,128)S(1)}, u32[]{:S(2)}, u32[]{:S(2)}) collective-permute-start(f32[128,128]{1,0:T(8,128)S(1)} %get-tuple-element.123), channel_id=1, source_target_pairs={{0,8},{8,0},{16,24},{24,16},{1,9},{9,1},{17,25},{25,17},{2,10},{10... | collective-permute-start | bytes 196616 | tf_op jit(solution)/shard_map/ppermute | solution.py:895
  49.2 7.7 %collective-permute-start.20 = (f32[128,128]{1,0:T(8,128)S(1)}, f32[128,128]{1,0:T(8,128)S(1)}, u32[]{:S(2)}, u32[]{:S(2)}) collective-permute-start(f32[128,128]{1,0:T(8,128)S(1)} %get-tuple-element.124), channel_id=1, source_target_pairs={{0,16},{8,24},{16,0},{24,8},{1,17},{9,25},{17,1},{25,9},{2,18},{10... | collective-permute-start | bytes 196616 | tf_op jit(solution)/shard_map/ppermute | solution.py:895
  51.8 6.1 %collective-permute-start.21 = (f32[128,128]{1,0:T(8,128)S(1)}, f32[128,128]{1,0:T(8,128)S(1)}, u32[]{:S(2)}, u32[]{:S(2)}) collective-permute-start(f32[128,128]{1,0:T(8,128)S(1)} %get-tuple-element.125), channel_id=1, source_target_pairs={{0,24},{8,16},{16,8},{24,0},{1,25},{9,17},{17,9},{25,1},{2,26},{10... | collective-permute-start | bytes 196616 | tf_op jit(solution)/shard_map/ppermute | solution.py:895
  59.3 4.5 %collective-permute-start.26 = (f32[4,32,128]{2,1,0:T(8,128)S(1)}, f32[4,32,128]{2,1,0:T(8,128)S(1)}, u32[]{:S(2)}, u32[]{:S(2)}) collective-permute-start(f32[4,32,128]{2,1,0:T(8,128)S(1)} %get-tuple-element.143), channel_id=1, source_target_pairs={{0,1},{1,0},{2,3},{3,2},{4,5},{5,4},{6,7},{7,6},{8,9},{9,8},{10,11... | collective-permute-start | bytes 196616 | tf_op jit(solution)/shard_map/ppermute | solution.py:895
  59.4 6.7 %collective-permute-start.23 = (f32[128,128]{1,0:T(8,128)S(1)}, f32[128,128]{1,0:T(8,128)S(1)}, u32[]{:S(2)}, u32[]{:S(2)}) collective-permute-start(f32[128,128]{1,0:T(8,128)S(1)} %get-tuple-element.139.refs_0_), channel_id=1, source_target_pairs={{0,8},{8,0},{16,24},{24,16},{1,9},{9,1},{17,25},{25,17},{2,10},{10... | collective-permute-start | bytes 196616 | tf_op jit(solution)/shard_map/ppermute | solution.py:895
  60.7 8.4 %collective-permute-start.24 = (f32[128,128]{1,0:T(8,128)S(1)}, f32[128,128]{1,0:T(8,128)S(1)}, u32[]{:S(2)}, u32[]{:S(2)}) collective-permute-start(f32[128,128]{1,0:T(8,128)S(1)} %get-tuple-element.139.refs_0_), channel_id=1, source_target_pairs={{0,16},{8,24},{16,0},{24,8},{1,17},{9,25},{17,1},{25,9},{2,18},{10... | collective-permute-start | bytes 196616 | tf_op jit(solution)/shard_map/ppermute | solution.py:895
  62.4 6.7 %collective-permute-start.25 = (f32[128,128]{1,0:T(8,128)S(1)}, f32[128,128]{1,0:T(8,128)S(1)}, u32[]{:S(2)}, u32[]{:S(2)}) collective-permute-start(f32[128,128]{1,0:T(8,128)S(1)} %get-tuple-element.139.refs_0_), channel_id=1, source_target_pairs={{0,24},{8,16},{16,8},{24,0},{1,25},{9,17},{17,9},{25,1},{2,26},{10... | collective-permute-start | bytes 196616 | tf_op jit(solution)/shard_map/ppermute | solution.py:895
  63.9 9.6 %collective-permute-start.27 = (f32[2,32,128]{2,1,0:T(8,128)S(1)}, f32[2,32,128]{2,1,0:T(8,128)S(1)}, u32[]{:S(2)}, u32[]{:S(2)}) collective-permute-start(f32[2,32,128]{2,1,0:T(8,128)S(1)} %get-tuple-element.145), channel_id=1, source_target_pairs={{0,2},{1,3},{2,0},{3,1},{4,6},{5,7},{6,4},{7,5},{8,10},{9,11},{10,... | collective-permute-start | bytes 98312 | tf_op jit(solution)/shard_map/ppermute | solution.py:895
  65.4 8.1 %collective-permute-start.28 = (f32[2,32,128]{2,1,0:T(8,128)S(1)}, f32[2,32,128]{2,1,0:T(8,128)S(1)}, u32[]{:S(2)}, u32[]{:S(2)}) collective-permute-start(f32[2,32,128]{2,1,0:T(8,128)S(1)} %get-tuple-element.146), channel_id=1, source_target_pairs={{0,4},{1,5},{2,6},{3,7},{4,0},{5,1},{6,2},{7,3},{8,12},{9,13},{10,... | collective-permute-start | bytes 98312 | tf_op jit(solution)/shard_map/ppermute | solution.py:895
  66.1 7.4 %collective-permute-start.29 = (f32[2,32,128]{2,1,0:T(8,128)S(1)}, f32[2,32,128]{2,1,0:T(8,128)S(1)}, u32[]{:S(2)}, u32[]{:S(2)}) collective-permute-start(f32[2,32,128]{2,1,0:T(8,128)S(1)} %get-tuple-element.147), channel_id=1, source_target_pairs={{0,6},{1,7},{2,4},{3,5},{4,2},{5,3},{6,0},{7,1},{8,14},{9,15},{10,... | collective-permute-start | bytes 98312 | tf_op jit(solution)/shard_map/ppermute | solution.py:895

commit v3 on v2

--- a/solution.py
+++ b/solution.py
@@ -556,13 +556,13 @@
     )(chosen, *pairs)
 
 
-def mix_back(store, row, values):
+def mix_back(block_of, values):
     channels, lanes = values.shape
     swapped = swap_halves(values)
     real = jnp.zeros((channels, lanes), jnp.float32)
     imag = real
     for channel in range(channels):
-        block = store[pl.ds(row + channel * channels, channels)]
+        block = block_of(channel)
         real = real + block * values[channel : channel + 1]
         imag = imag + block * swapped[channel : channel + 1]
     other_re, other_im = swap_halves(real), swap_halves(imag)
@@ -582,12 +582,29 @@
     high, low = split(jnp.concatenate(columns, 1))
     found = dot(jnp.concatenate([high, low], 0), chosen_ref[...])
     found = found[:channels] + found[channels:]
+    core = place_of()[1] % 2
+    size = channels * channels
+    here, beside, others, over = stores
+
+    def block_at(owner):
+        chip, other = owner // 2, owner % 2
+        if chip == 0:
+            return lambda channel: (beside if other else here)[pl.ds(channel * channels, channels)]
+        if chip == 3:
+            return lambda channel: (over if other else others)[pl.ds(2 * size + channel * channels, channels)]
+
+        def block(channel):
+            own = others[pl.ds(other * size + channel * channels, channels)]
+            came = over[pl.ds((1 - other) * size + channel * channels, channels)]
+            return jnp.where(core == 2 - chip, own, came)
+
+        return block
+
     mixed = []
     for owner in range(2 * steps):
         values = found[:, owner * lanes : (owner + 1) * lanes]
         (other_ref if owner % 2 else same_ref)[owner // 2] = values
-        row = max(owner // 2 - 1, 0) * channels * channels
-        mixed.append(mix_back(stores[owner % 2 + (2 if owner > 1 else 0)], row, values))
+        mixed.append(mix_back(block_at(owner), values))
     slots_to_modes(mixed, chosen_ref, out_ref, modes_x)
 
 
@@ -624,25 +641,6 @@
         cost_estimate=takes(0.3),
         name="pair",
     )(same, other)
-
-
-def halves_kernel(first_ref, second_ref, low_ref, high_ref):
-    half = low_ref.shape[0]
-    low_ref[...] = first_ref[pl.ds(0, half)]
-    high_ref[...] = second_ref[pl.ds(half, half)]
-
-
-def halves(first, second):
-    shape = (first.shape[0] // 2, first.shape[1])
-    return pl.pallas_call(
-        halves_kernel,
-        out_shape=[jax.ShapeDtypeStruct(shape, first.dtype)] * 2,
-        in_specs=whole(2),
-        out_specs=whole(2),
-        compiler_params=params(),
-        cost_estimate=takes(0.1),
-        name="halves",
-    )(first, second)
 
 
 def join_kernel(*refs):
@@ -893,6 +891,10 @@
 
 def exchange(piece, axis, count, flip):
     return lax.ppermute(piece, axis, [(i, i ^ flip) for i in range(count)])
+
+
+def exchange_two(piece, axis, count, *flips):
+    return lax.ppermute(piece, axis, [(i, i ^ flips[i % 2]) for i in range(count)])
 
 
 def to_owners(same, other, count):
@@ -949,15 +951,15 @@
     beside = exchange(packed, "py", count_y, 1)
     tables, full_map, full_back, shift = make_tables(small, full_x, rows_x, width_y, ky_modes.shape[0], modes_x)
     pairs, chosen, full_map, packed, beside = barrier((pairs, chosen, full_map, packed, beside))
-    near = [exchange(packed, "py", count_y, step) for step in (2, 4)]
+    near = exchange_two(packed, "py", count_y, 4, 2)
+    near_other = exchange_two(beside, "py", count_y, 4, 2)
     received = from_all(to_modes(chosen, pairs, modes_x), "px", count_x)
     mapped = pointwise_map(full_map, shift, field_in[:, 0])
     received, mapped, near = barrier((received, mapped, near))
-    low, high = halves(*near)
-    far = [exchange(low, "py", count_y, 4), exchange(high, "py", count_y, 2)]
+    far = exchange_two(near, "py", count_y, 2, 4)
     terms, sums = slope_step(received, tables, mapped, cotangent[:, 0])
-    sums, terms, far = barrier((list(sums), list(terms), far))
-    others = join(near + far)
+    sums, terms, far, near_other = barrier((list(sums), list(terms), far, near_other))
+    others = join([near, near_other, far])
     others_beside = exchange(others, "py", count_y, 1)
     received = to_all(sums, "px", count_x)
     back = pointwise_back(full_back, terms)

time: 75.9 us -> 72.8 us (0.959)
  waiting for transfers between devices: 13.9 us -> 12 us
  starting transfers between devices: 31 us -> 29.9 us
    ppermute x30 -> x26, starting transfers between devices: 31 us -> 26.4 us  [exchange(): return lax.ppermute(piece, axis, [(i, i ^ flip) for i in range(count)])]
    ppermute x0 -> x3, starting transfers between devices: none -> 3.52 us  [exchange_two(): lax.ppermute(piece, axis, [(i, i ^ flips[i % 2]) for i in range(count)])]
    ppermute x30 -> x26, waiting for transfers between devices: 13.9 us -> 12 us  [exchange(): return lax.ppermute(piece, axis, [(i, i ^ flip) for i in range(count)])]
  transfers between devices with their start and end apart: 30 -> 29, of which waited for: 14 -> 13; matrix products, arithmetic and copies ran while one was open for 0% -> 0% of each run, Pallas kernels for 29% -> 31%
where the time goes in v3:
time: 72.8 us; the launch traced here: 72.7 us
  starting transfers between devices  29.9 us (41%)
  Pallas kernels  27.8 us (38%)
  waiting for transfers between devices  12 us (16%)
  local copies, waits for them, and re-layouts  2.14 us (3%)
  between operations  0.85 us (1%)
    ppermute x26, starting transfers between devices, exchange(): return lax.ppermute(piece, axis, [(i, i ^ flip) for i in range(count)])  26.4 us
    ppermute x26, waiting for transfers between devices, exchange(): return lax.ppermute(piece, axis, [(i, i ^ flip) for i in range(count)])  12 us
    pallas_call x1, Pallas kernels, slope_step(): pl.pallas_call(functools.partial(slope_kernel, blocks=blocks), out_shape=...  8.25 us
    pallas_call x1, Pallas kernels, finish(): pl.pallas_call(functools.partial(finish_kernel, blocks=blocks, group=grou...  4.4 us
    pallas_call x1, Pallas kernels, pointwise_back(): pl.pallas_call(pointwise_back_kernel, out_shape=jax.ShapeDtypeStruct((2 *...  3.52 us
    ppermute x3, starting transfers between devices, exchange_two(): lax.ppermute(piece, axis, [(i, i ^ flips[i % 2]) for i in range(count)])  3.52 us
    pallas_call x1, Pallas kernels, pointwise_map(): pl.pallas_call(pointwise_kernel, out_shape=jax.ShapeDtypeStruct(values.sh...  2.45 us
    unnamed x8, local copies, waits for them, and re-layouts  2.14 us
  transfers between devices with their start and end apart: 29, of which 13 were waited for; matrix products, arithmetic and copies ran while one was open for 0% of the time, Pallas kernels for 31%

profile of v3, /device:TPU:0, one launch (start us, length us, event | category | flops | bytes accessed | tf_op | source)
XLA Modules:
  0.0 72.7 jit_solution(17700686401104701884)
XLA Ops:
  0.6 1.8 %pack.1 = (f32[32,640]{1,0:T(8,128)}, f32[32,1152]{1,0:T(8,128)}) custom-call(s32[4,8]{1,0:T(4,128)} %refs_0_.1, f32[512,32]{1,0:T(8,128)} %bitcast.14, s32[32]{0:T(128)} %refs_2_.1, s32[32]{0:T(128)} %refs_3_.1, f32[32]{0:T(128)} %refs_4_.1, bf16[32,32]{1,0:T(8,128)(2,1)} %refs_5_.1), custom_call_target="tpu_custom_call" | custom-call | tf_op jit(solution)/shard_map/pack/pallas_call | solution.py:362
  2.5 3.0 %collective-permute-start = (f32[32,640]{1,0:T(8,128)}, f32[32,640]{1,0:T(8,128)S(1)}, u32[]{:S(2)}, u32[]{:S(2)}) collective-permute-start(f32[32,640]{1,0:T(8,128)} %get-tuple-element.74), channel_id=1, source_target_pairs={{0,2},{1,3},{2,0},{3,1},{4,6},{5,7},{6,4},{7,5},{8,10},{9,11},{10,... | collective-permute-start | bytes 245768 | tf_op jit(solution)/shard_map/ppermute | solution.py:893
  5.5 1.5 %collective-permute-start.1 = (f32[32,640]{1,0:T(8,128)}, f32[32,640]{1,0:T(8,128)S(1)}, u32[]{:S(2)}, u32[]{:S(2)}) collective-permute-start(f32[32,640]{1,0:T(8,128)} %get-tuple-element.74), channel_id=1, source_target_pairs={{0,4},{1,5},{2,6},{3,7},{4,0},{5,1},{6,2},{7,3},{8,12},{9,13},{10,... | collective-permute-start | bytes 245768 | tf_op jit(solution)/shard_map/ppermute | solution.py:893
  7.0 0.0 collective-permute-start.2
  7.0 0.0 collective-permute-start.3
  7.0 1.2 %copy-done.2 = f32[64,2,32,32]{0,3,2,1:T(8,128)S(1)} copy-done((f32[64,2,32,32]{0,3,2,1:T(8,128)S(1)}, f32[64,2,32,32]{0,3,2,1:T(8,128)}, u32[]{:S(2)}) %copy-start.2) | copy-done | bytes 524312
  8.3 0.9 %copy-done.3 = f32[32,1152]{1,0:T(8,128)S(1)} copy-done((f32[32,1152]{1,0:T(8,128)S(1)}, f32[32,1152]{1,0:T(8,128)}, u32[]{:S(2)}) %copy-start.3) | copy-done | bytes 147480
  9.2 0.2 unpack.1
  9.4 0.0 collective-permute-done.refs_2_
  9.4 1.6 %collective-permute-done.1.refs_4_ = f32[32,640]{1,0:T(8,128)S(1)} collective-permute-done((f32[32,640]{1,0:T(8,128)}, f32[32,640]{1,0:T(8,128)S(1)}, u32[]{:S(2)}, u32[]{:S(2)}) %collective-permute-start.1) | collective-permute-done | bytes 81952 | tf_op jit(solution)/shard_map/ppermute | solution.py:893
  11.0 1.5 %collective-permute-done.2.refs_6_ = f32[32,640]{1,0:T(8,128)S(1)} collective-permute-done((f32[32,640]{1,0:T(8,128)}, f32[32,640]{1,0:T(8,128)S(1)}, u32[]{:S(2)}, u32[]{:S(2)}) %collective-permute-start.2) | collective-permute-done | bytes 81952 | tf_op jit(solution)/shard_map/ppermute | solution.py:893
  12.6 0.0 collective-permute-done.3.refs_1_
  12.6 0.0 collective-permute-start.4
  12.6 0.5 collective-permute-start.5
  13.1 0.0 collective-permute-start.6
  13.1 0.5 collective-permute-start.11
  13.6 0.3 collective-permute-done.4.refs_3_
  13.8 0.2 collective-permute-done.5.refs_5_
  14.0 0.4 collective-permute-done.6.refs_7_
  14.3 1.8 %mix.1 = (f32[512,128]{1,0:T(8,128)S(1)}, f32[256,128]{1,0:T(8,128)S(1)}, f32[4,32,128]{2,1,0:T(8,128)S(1)}, f32[4,32,128]{2,1,0:T(8,128)S(1)}) custom-call(f32[1024,128]{1,0:T(8,128)S(1)} %get-tuple-element.97.packed_ref.refs_4_, f32[32,640]{1,0:T(8,128)S(1)} %get-tuple-element.76.refs_0_, f32[32,640]{1,0:T(8,128)S(1)} %collective-permute-done.3.refs_1_, ...), custom_call_target="tpu_custom_call" | custom-call | flops 3000000000 | bytes 1048576 | tf_op jit(solution)/shard_map/mix/pallas_call | solution.py:420
  16.2 0.2 collective-permute-start.7
  16.4 0.8 %tables.1 = (bf16[2,256,512]{2,1,0:T(8,128)(2,1)S(1)}, bf16[128,512]{1,0:T(8,128)(2,1)S(1)}, bf16[384,512]{1,0:T(8,128)(2,1)S(1)}, bf16[512,256]{1,0:T(8,128)(2,...) custom-call(f32[32,512]{1,0:T(8,128)S(1)} %get-tuple-element.88.small_ref), custom_call_target="tpu_custom_call" | custom-call | flops 1000000000 | bytes 1048576 | tf_op jit(solution)/shard_map/tables/pallas_call | solution.py:312
  17.2 0.3 collective-permute-done.7.other_ref
  17.5 0.6 collective-permute-start.8
  18.1 0.6 collective-permute-start.9
  18.7 2.3 %collective-permute-start.10 = (f32[2,32,128]{2,1,0:T(8,128)S(1)}, f32[2,32,128]{2,1,0:T(8,128)S(1)}, u32[]{:S(2)}, u32[]{:S(2)}) collective-permute-start(f32[2,32,128]{2,1,0:T(8,128)S(1)} %get-tuple-element.86), channel_id=1, source_target_pairs={{0,6},{1,7},{2,4},{3,5},{4,2},{5,3},{6,0},{7,1},{8,14},{9,15},{10,... | collective-permute-start | bytes 98312 | tf_op jit(solution)/shard_map/ppermute | solution.py:893
  21.1 0.2 select.1.chosen_ref
  21.3 0.2 collective-permute-done.8.refs_1_
  21.5 0.9 %collective-permute-done.9.refs_2_ = f32[2,32,128]{2,1,0:T(8,128)S(1)} collective-permute-done((f32[2,32,128]{2,1,0:T(8,128)S(1)}, f32[2,32,128]{2,1,0:T(8,128)S(1)}, u32[]{:S(2)}, u32[]{:S(2)}) %collective-permute-start.9) | collective-permute-done | bytes 32800 | tf_op jit(solution)/shard_map/ppermute | solution.py:893
  22.4 1.2 %collective-permute-done.10.refs_3_ = f32[2,32,128]{2,1,0:T(8,128)S(1)} collective-permute-done((f32[2,32,128]{2,1,0:T(8,128)S(1)}, f32[2,32,128]{2,1,0:T(8,128)S(1)}, u32[]{:S(2)}, u32[]{:S(2)}) %collective-permute-start.10) | collective-permute-done | bytes 32800 | tf_op jit(solution)/shard_map/ppermute | solution.py:893
  23.6 1.4 %collective-permute-start.15 = (f32[1024,128]{1,0:T(8,128)S(1)}, f32[1024,128]{1,0:T(8,128)S(1)}, u32[]{:S(2)}, u32[]{:S(2)}) collective-permute-start(f32[1024,128]{1,0:T(8,128)S(1)} %get-tuple-element.97.packed_ref.refs_4_), channel_id=1, source_target_pairs={{0,4},{1,3},{2,6},{3,1},{4,0},{5,7},{6,2},{7,5},{8,12},{9,11},{10,... | collective-permute-start | bytes 1572872 | tf_op jit(solution)/shard_map/ppermute | solution.py:897
  24.9 0.5 to_modes.1.refs_0_
  25.5 1.6 %collective-permute-start.12 = (f32[128,128]{1,0:T(8,128)S(1)}, f32[128,128]{1,0:T(8,128)S(1)}, u32[]{:S(2)}, u32[]{:S(2)}) collective-permute-start(f32[128,128]{1,0:T(8,128)S(1)} %to_modes.1.refs_0_), channel_id=1, source_target_pairs={{0,8},{8,0},{16,24},{24,16},{1,9},{9,1},{17,25},{25,17},{2,10},{10... | collective-permute-start | bytes 196616 | tf_op jit(solution)/shard_map/ppermute | solution.py:893
  27.1 2.6 %collective-permute-start.13 = (f32[128,128]{1,0:T(8,128)S(1)}, f32[128,128]{1,0:T(8,128)S(1)}, u32[]{:S(2)}, u32[]{:S(2)}) collective-permute-start(f32[128,128]{1,0:T(8,128)S(1)} %to_modes.1.refs_0_), channel_id=1, source_target_pairs={{0,16},{8,24},{16,0},{24,8},{1,17},{9,25},{17,1},{25,9},{2,18},{10... | collective-permute-start | bytes 196616 | tf_op jit(solution)/shard_map/ppermute | solution.py:893
  29.7 0.2 collective-permute-start.14
  29.9 0.6 collective-permute-start.17
  30.6 2.4 %pointwise_map.1.refs_8_ = f32[32,128,512]{2,1,0:T(8,128)S(1)} custom-call(bf16[256,256]{1,0:T(8,128)(2,1)S(1)} %get-tuple-element.95.full_ref, f32[256,128]{1,0:T(8,128)S(1)} %get-tuple-element.96.shift_ref, bf16[32,128,512]{2,1,0:T(8,128)(2,1)S(1)} %bitcast.10), custom_call_target="tpu_custom_call" | custom-call | flops 3000000000 | bytes 1048576 | tf_op jit(solution)/shard_map/pointwise_map/pallas_call | solution.py:696
  33.0 0.0 collective-permute-done.12.refs_1_
  33.0 0.6 collective-permute-done.13.refs_2_
  33.7 2.1 %collective-permute-done.14.refs_3_ = f32[128,128]{1,0:T(8,128)S(1)} collective-permute-done((f32[128,128]{1,0:T(8,128)S(1)}, f32[128,128]{1,0:T(8,128)S(1)}, u32[]{:S(2)}, u32[]{:S(2)}) %collective-permute-start.14) | collective-permute-done | bytes 65568 | tf_op jit(solution)/shard_map/ppermute | solution.py:893
  35.8 0.0 collective-permute-done.15.refs_0_
  35.8 1.5 %collective-permute-start.16 = (f32[1024,128]{1,0:T(8,128)S(1)}, f32[1024,128]{1,0:T(8,128)S(1)}, u32[]{:S(2)}, u32[]{:S(2)}) collective-permute-start(f32[1024,128]{1,0:T(8,128)S(1)} %collective-permute-done.15.refs_0_), channel_id=1, source_target_pairs={{0,2},{1,5},{2,0},{3,7},{4,6},{5,1},{6,4},{7,3},{8,10},{9,13},{10,... | collective-permute-start | bytes 1572872 | tf_op jit(solution)/shard_map/ppermute | solution.py:897
  37.3 8.3 %slope_step.1 = (bf16[8,2,128,512]{3,2,1,0:T(8,128)(2,1)S(1)}, bf16[8,2,128,512]{3,2,1,0:T(8,128)(2,1)S(1)}, bf16[8,2,128,512]{3,2,1,0:T(8,128)(2,1)S(1)}, bf16[...) custom-call(f32[128,128]{1,0:T(8,128)S(1)} %to_modes.1.refs_0_, ...), custom_call_target="tpu_custom_call" | custom-call | flops 8000000000 | bytes 1048576 | tf_op jit(solution)/shard_map/slope_step/pallas_call | solution.py:825
  45.5 0.0 collective-permute-done.16.refs_2_
  45.5 0.1 join.1.refs_6_
  45.7 0.1 collective-permute-start.21
  45.7 0.1 collective-permute-start.18
  45.8 3.0 %collective-permute-start.19 = (f32[128,128]{1,0:T(8,128)S(1)}, f32[128,128]{1,0:T(8,128)S(1)}, u32[]{:S(2)}, u32[]{:S(2)}) collective-permute-start(f32[128,128]{1,0:T(8,128)S(1)} %get-tuple-element.119), channel_id=1, source_target_pairs={{0,16},{8,24},{16,0},{24,8},{1,17},{9,25},{17,1},{25,9},{2,18},{10... | collective-permute-start | bytes 196616 | tf_op jit(solution)/shard_map/ppermute | solution.py:893
  48.8 1.4 %collective-permute-start.20 = (f32[128,128]{1,0:T(8,128)S(1)}, f32[128,128]{1,0:T(8,128)S(1)}, u32[]{:S(2)}, u32[]{:S(2)}) collective-permute-start(f32[128,128]{1,0:T(8,128)S(1)} %get-tuple-element.120), channel_id=1, source_target_pairs={{0,24},{8,16},{16,8},{24,0},{1,25},{9,17},{17,9},{25,1},{2,26},{10... | collective-permute-start | bytes 196616 | tf_op jit(solution)/shard_map/ppermute | solution.py:893
  50.2 3.5 %pointwise_back.1.refs_6_ = f32[32,128,512]{2,1,0:T(8,128)S(1)} custom-call(bf16[256,256]{1,0:T(8,128)(2,1)S(1)} %get-tuple-element.121.full_ref, bf16[8,2,128,512]{3,2,1,0:T(8,128)(2,1)S(1)} %get-tuple-element.122.refs_0_, bf16[8,2,128,512]{3,2,1,0:T(8,128)(2,1)S(1)} %get-tuple-element.123.refs_1_, bf16[8,2,128,512]{3,2,1,0:T(8,128)(2,1)S(1)} %get-tuple-element.124.refs_2_, ...), custom_call_target="tpu_custom_call" | custom-call | flops 4000000000 | bytes 1048576 | tf_op jit(solution)/shard_map/pointwise_back/pallas_call | solution.py:731
  53.7 0.0 collective-permute-done.18.refs_1_
  53.7 0.0 collective-permute-done.19.refs_2_
  53.7 1.1 %collective-permute-done.20.refs_3_ = f32[128,128]{1,0:T(8,128)S(1)} collective-permute-done((f32[128,128]{1,0:T(8,128)S(1)}, f32[128,128]{1,0:T(8,128)S(1)}, u32[]{:S(2)}, u32[]{:S(2)}) %collective-permute-start.20) | collective-permute-done | bytes 65568 | tf_op jit(solution)/shard_map/ppermute | solution.py:893
  54.9 1.5 %adjoint.1 = (f32[4,32,128]{2,1,0:T(8,128)S(1)}, f32[4,32,128]{2,1,0:T(8,128)S(1)}, f32[128,128]{1,0:T(8,128)S(1)}) custom-call(bf16[512,1024]{1,0:T(8,128)(2,1)S(1)} %select.1.chosen_ref, f32[128,128]{1,0:T(8,128)S(1)} %get-tuple-element.128.refs_0_, f32[128,128]{1,0:T(8,128)S(1)} %collective-permute-done.18.refs_1_, ...), custom_call_target="tpu_custom_call" | custom-call | flops 2000000000 | bytes 1048576 | tf_op jit(solution)/shard_map/adjoint/pallas_call | solution.py:615
  56.4 0.1 collective-permute-start.25
  56.5 1.2 %collective-permute-start.22 = (f32[128,128]{1,0:T(8,128)S(1)}, f32[128,128]{1,0:T(8,128)S(1)}, u32[]{:S(2)}, u32[]{:S(2)}) collective-permute-start(f32[128,128]{1,0:T(8,128)S(1)} %get-tuple-element.133.refs_0_), channel_id=1, source_target_pairs={{0,8},{8,0},{16,24},{24,16},{1,9},{9,1},{17,25},{25,17},{2,10},{10... | collective-permute-start | bytes 196616 | tf_op jit(solution)/shard_map/ppermute | solution.py:893
  57.7 1.5 %collective-permute-start.23 = (f32[128,128]{1,0:T(8,128)S(1)}, f32[128,128]{1,0:T(8,128)S(1)}, u32[]{:S(2)}, u32[]{:S(2)}) collective-permute-start(f32[128,128]{1,0:T(8,128)S(1)} %get-tuple-element.133.refs_0_), channel_id=1, source_target_pairs={{0,16},{8,24},{16,0},{24,8},{1,17},{9,25},{17,1},{25,9},{2,18},{10... | collective-permute-start | bytes 196616 | tf_op jit(solution)/shard_map/ppermute | solution.py:893
  59.1 1.8 %collective-permute-start.24 = (f32[128,128]{1,0:T(8,128)S(1)}, f32[128,128]{1,0:T(8,128)S(1)}, u32[]{:S(2)}, u32[]{:S(2)}) collective-permute-start(f32[128,128]{1,0:T(8,128)S(1)} %get-tuple-element.133.refs_0_), channel_id=1, source_target_pairs={{0,24},{8,16},{16,8},{24,0},{1,25},{9,17},{17,9},{25,1},{2,26},{10... | collective-permute-start | bytes 196616 | tf_op jit(solution)/shard_map/ppermute | solution.py:893
  61.0 1.4 %collective-permute-start.26 = (f32[2,32,128]{2,1,0:T(8,128)S(1)}, f32[2,32,128]{2,1,0:T(8,128)S(1)}, u32[]{:S(2)}, u32[]{:S(2)}) collective-permute-start(f32[2,32,128]{2,1,0:T(8,128)S(1)} %get-tuple-element.139), channel_id=1, source_target_pairs={{0,2},{1,3},{2,0},{3,1},{4,6},{5,7},{6,4},{7,5},{8,10},{9,11},{10,... | collective-permute-start | bytes 98312 | tf_op jit(solution)/shard_map/ppermute | solution.py:893
  62.4 0.9 %collective-permute-start.27 = (f32[2,32,128]{2,1,0:T(8,128)S(1)}, f32[2,32,128]{2,1,0:T(8,128)S(1)}, u32[]{:S(2)}, u32[]{:S(2)}) collective-permute-start(f32[2,32,128]{2,1,0:T(8,128)S(1)} %get-tuple-element.140), channel_id=1, source_target_pairs={{0,4},{1,5},{2,6},{3,7},{4,0},{5,1},{6,2},{7,3},{8,12},{9,13},{10,... | collective-permute-start | bytes 98312 | tf_op jit(solution)/shard_map/ppermute | solution.py:893
  63.3 1.2 %collective-permute-start.28 = (f32[2,32,128]{2,1,0:T(8,128)S(1)}, f32[2,32,128]{2,1,0:T(8,128)S(1)}, u32[]{:S(2)}, u32[]{:S(2)}) collective-permute-start(f32[2,32,128]{2,1,0:T(8,128)S(1)} %get-tuple-element.141), channel_id=1, source_target_pairs={{0,6},{1,7},{2,4},{3,5},{4,2},{5,3},{6,0},{7,1},{8,14},{9,15},{10,... | collective-permute-start | bytes 98312 | tf_op jit(solution)/shard_map/ppermute | solution.py:893
  64.5 1.6 %collective-permute-done.23.refs_2_ = f32[128,128]{1,0:T(8,128)S(1)} collective-permute-done((f32[128,128]{1,0:T(8,128)S(1)}, f32[128,128]{1,0:T(8,128)S(1)}, u32[]{:S(2)}, u32[]{:S(2)}) %collective-permute-start.23) | collective-permute-done | bytes 65568 | tf_op jit(solution)/shard_map/ppermute | solution.py:893
  66.1 4.4 %finish.1 = f32[32,128,512]{2,1,0:T(8,128)} custom-call(f32[128,128]{1,0:T(8,128)S(1)} %get-tuple-element.133.refs_0_, f32[128,128]{1,0:T(8,128)S(1)} %collective-permute-done.22.refs_1_, f32[128,128]{1,0:T(8,128)S(1)} %collective-permute-done.23.refs_2_, f32[128,128]{1,0:T(8,128)S(1)} %collective-permute-done.24.refs_3_, ...), custom_call_target="tpu_custom_call" | custom-call | flops 4000000000 | bytes 1048576 | tf_op jit(solution)/shard_map/finish/pallas_call | solution.py:876
  70.5 2.1 %weight_grad.1 = f32[2,32,32,64]{3,2,1,0:T(8,128)} custom-call(f32[512,128]{1,0:T(8,128)S(1)} %get-tuple-element.135.kept_ref, f32[2,32,128]{2,1,0:T(8,128)S(1)} %get-tuple-element.138.refs_0_, f32[2,32,128]{2,1,0:T(8,128)S(1)} %collective-permute-done.26.refs_1_, f32[2,32,128]{2,1,0:T(8,128)S(1)} %collective-permute-done.27.refs_2_, ...), custom_call_target="tpu_custom_call" | custom-call | flops 2000000000 | bytes 1048576 | tf_op jit(solution)/shard_map/weight_grad/pallas_call | solution.py:483
  (17 shorter events, 0.1 us)
Async XLA Ops:
  2.5 6.9 %collective-permute-start = (f32[32,640]{1,0:T(8,128)}, f32[32,640]{1,0:T(8,128)S(1)}, u32[]{:S(2)}, u32[]{:S(2)}) collective-permute-start(f32[32,640]{1,0:T(8,128)} %get-tuple-element.74), channel_id=1, source_target_pairs={{0,2},{1,3},{2,0},{3,1},{4,6},{5,7},{6,4},{7,5},{8,10},{9,11},{10,... | collective-permute-start | bytes 245768 | tf_op jit(solution)/shard_map/ppermute | solution.py:893
  5.5 5.5 %collective-permute-start.1 = (f32[32,640]{1,0:T(8,128)}, f32[32,640]{1,0:T(8,128)S(1)}, u32[]{:S(2)}, u32[]{:S(2)}) collective-permute-start(f32[32,640]{1,0:T(8,128)} %get-tuple-element.74), channel_id=1, source_target_pairs={{0,4},{1,5},{2,6},{3,7},{4,0},{5,1},{6,2},{7,3},{8,12},{9,13},{10,... | collective-permute-start | bytes 245768 | tf_op jit(solution)/shard_map/ppermute | solution.py:893
  7.0 5.6 %collective-permute-start.2 = (f32[32,640]{1,0:T(8,128)}, f32[32,640]{1,0:T(8,128)S(1)}, u32[]{:S(2)}, u32[]{:S(2)}) collective-permute-start(f32[32,640]{1,0:T(8,128)} %get-tuple-element.74), channel_id=1, source_target_pairs={{0,6},{1,7},{2,4},{3,5},{4,2},{5,3},{6,0},{7,1},{8,14},{9,15},{10,... | collective-permute-start | bytes 245768 | tf_op jit(solution)/shard_map/ppermute | solution.py:893
  7.0 5.5 %collective-permute-start.3 = (f32[32,640]{1,0:T(8,128)}, f32[32,640]{1,0:T(8,128)S(1)}, u32[]{:S(2)}, u32[]{:S(2)}) collective-permute-start(f32[32,640]{1,0:T(8,128)} %get-tuple-element.74), channel_id=1, source_target_pairs={{0,1},{1,0},{2,3},{3,2},{4,5},{5,4},{6,7},{7,6},{8,9},{9,8},{10,11... | collective-permute-start | bytes 245768 | tf_op jit(solution)/shard_map/ppermute | solution.py:893
  7.0 1.2 %copy-start.2 = (f32[64,2,32,32]{0,3,2,1:T(8,128)S(1)}, f32[64,2,32,32]{0,3,2,1:T(8,128)}, u32[]{:S(2)}) copy-start(f32[64,2,32,32]{0,3,2,1:T(8,128)} %param.12) | copy-start | bytes 1572868
  8.2 0.9 %copy-start.3 = (f32[32,1152]{1,0:T(8,128)S(1)}, f32[32,1152]{1,0:T(8,128)}, u32[]{:S(2)}) copy-start(f32[32,1152]{1,0:T(8,128)} %get-tuple-element.72.all_ref) | copy-start | bytes 442372
  12.6 1.3 %collective-permute-start.4 = (f32[32,640]{1,0:T(8,128)S(1)}, f32[32,640]{1,0:T(8,128)S(1)}, u32[]{:S(2)}, u32[]{:S(2)}) collective-permute-start(f32[32,640]{1,0:T(8,128)S(1)} %collective-permute-done.refs_2_), channel_id=1, source_target_pairs={{0,1},{1,0},{2,3},{3,2},{4,5},{5,4},{6,7},{7,6},{8,9},{9,8},{10,11... | collective-permute-start | bytes 245768 | tf_op jit(solution)/shard_map/ppermute | solution.py:893
  12.6 1.4 %collective-permute-start.5 = (f32[32,640]{1,0:T(8,128)S(1)}, f32[32,640]{1,0:T(8,128)S(1)}, u32[]{:S(2)}, u32[]{:S(2)}) collective-permute-start(f32[32,640]{1,0:T(8,128)S(1)} %collective-permute-done.1.refs_4_), channel_id=1, source_target_pairs={{0,1},{1,0},{2,3},{3,2},{4,5},{5,4},{6,7},{7,6},{8,9},{9,8},{10,11... | collective-permute-start | bytes 245768 | tf_op jit(solution)/shard_map/ppermute | solution.py:893
  13.1 1.3 %collective-permute-start.6 = (f32[32,640]{1,0:T(8,128)S(1)}, f32[32,640]{1,0:T(8,128)S(1)}, u32[]{:S(2)}, u32[]{:S(2)}) collective-permute-start(f32[32,640]{1,0:T(8,128)S(1)} %collective-permute-done.2.refs_6_), channel_id=1, source_target_pairs={{0,1},{1,0},{2,3},{3,2},{4,5},{5,4},{6,7},{7,6},{8,9},{9,8},{10,11... | collective-permute-start | bytes 245768 | tf_op jit(solution)/shard_map/ppermute | solution.py:893
  13.1 10.5 %collective-permute-start.11 = (f32[1024,128]{1,0:T(8,128)S(1)}, f32[1024,128]{1,0:T(8,128)S(1)}, u32[]{:S(2)}, u32[]{:S(2)}) collective-permute-start(f32[1024,128]{1,0:T(8,128)S(1)} %get-tuple-element.97.packed_ref.refs_4_), channel_id=1, source_target_pairs={{0,1},{1,0},{2,3},{3,2},{4,5},{5,4},{6,7},{7,6},{8,9},{9,8},{10,11... | collective-permute-start | bytes 1572872 | tf_op jit(solution)/shard_map/ppermute | solution.py:893
  16.2 1.3 %collective-permute-start.7 = (f32[4,32,128]{2,1,0:T(8,128)S(1)}, f32[4,32,128]{2,1,0:T(8,128)S(1)}, u32[]{:S(2)}, u32[]{:S(2)}) collective-permute-start(f32[4,32,128]{2,1,0:T(8,128)S(1)} %get-tuple-element.82), channel_id=1, source_target_pairs={{0,1},{1,0},{2,3},{3,2},{4,5},{5,4},{6,7},{7,6},{8,9},{9,8},{10,11... | collective-permute-start | bytes 196616 | tf_op jit(solution)/shard_map/ppermute | solution.py:893
  17.5 4.0 %collective-permute-start.8 = (f32[2,32,128]{2,1,0:T(8,128)S(1)}, f32[2,32,128]{2,1,0:T(8,128)S(1)}, u32[]{:S(2)}, u32[]{:S(2)}) collective-permute-start(f32[2,32,128]{2,1,0:T(8,128)S(1)} %get-tuple-element.84), channel_id=1, source_target_pairs={{0,2},{1,3},{2,0},{3,1},{4,6},{5,7},{6,4},{7,5},{8,10},{9,11},{10,... | collective-permute-start | bytes 98312 | tf_op jit(solution)/shard_map/ppermute | solution.py:893
  18.1 4.3 %collective-permute-start.9 = (f32[2,32,128]{2,1,0:T(8,128)S(1)}, f32[2,32,128]{2,1,0:T(8,128)S(1)}, u32[]{:S(2)}, u32[]{:S(2)}) collective-permute-start(f32[2,32,128]{2,1,0:T(8,128)S(1)} %get-tuple-element.85), channel_id=1, source_target_pairs={{0,4},{1,5},{2,6},{3,7},{4,0},{5,1},{6,2},{7,3},{8,12},{9,13},{10,... | collective-permute-start | bytes 98312 | tf_op jit(solution)/shard_map/ppermute | solution.py:893
  18.7 4.8 %collective-permute-start.10 = (f32[2,32,128]{2,1,0:T(8,128)S(1)}, f32[2,32,128]{2,1,0:T(8,128)S(1)}, u32[]{:S(2)}, u32[]{:S(2)}) collective-permute-start(f32[2,32,128]{2,1,0:T(8,128)S(1)} %get-tuple-element.86), channel_id=1, source_target_pairs={{0,6},{1,7},{2,4},{3,5},{4,2},{5,3},{6,0},{7,1},{8,14},{9,15},{10,... | collective-permute-start | bytes 98312 | tf_op jit(solution)/shard_map/ppermute | solution.py:893
  21.1 9.5 %copy-start = (bf16[32,1,128,512]{3,2,1,0:T(8,128)(2,1)S(1)}, bf16[32,1,128,512]{3,2,1,0:T(8,128)(2,1)}, u32[]{:S(2)}) copy-start(bf16[32,1,128,512]{3,2,1,0:T(8,128)(2,1)} %param.9) | copy-start | bytes 12582916
  23.6 12.2 %collective-permute-start.15 = (f32[1024,128]{1,0:T(8,128)S(1)}, f32[1024,128]{1,0:T(8,128)S(1)}, u32[]{:S(2)}, u32[]{:S(2)}) collective-permute-start(f32[1024,128]{1,0:T(8,128)S(1)} %get-tuple-element.97.packed_ref.refs_4_), channel_id=1, source_target_pairs={{0,4},{1,3},{2,6},{3,1},{4,0},{5,7},{6,2},{7,5},{8,12},{9,11},{10,... | collective-permute-start | bytes 1572872 | tf_op jit(solution)/shard_map/ppermute | solution.py:897
  25.5 7.6 %collective-permute-start.12 = (f32[128,128]{1,0:T(8,128)S(1)}, f32[128,128]{1,0:T(8,128)S(1)}, u32[]{:S(2)}, u32[]{:S(2)}) collective-permute-start(f32[128,128]{1,0:T(8,128)S(1)} %to_modes.1.refs_0_), channel_id=1, source_target_pairs={{0,8},{8,0},{16,24},{24,16},{1,9},{9,1},{17,25},{25,17},{2,10},{10... | collective-permute-start | bytes 196616 | tf_op jit(solution)/shard_map/ppermute | solution.py:893
  27.1 6.6 %collective-permute-start.13 = (f32[128,128]{1,0:T(8,128)S(1)}, f32[128,128]{1,0:T(8,128)S(1)}, u32[]{:S(2)}, u32[]{:S(2)}) collective-permute-start(f32[128,128]{1,0:T(8,128)S(1)} %to_modes.1.refs_0_), channel_id=1, source_target_pairs={{0,16},{8,24},{16,0},{24,8},{1,17},{9,25},{17,1},{25,9},{2,18},{10... | collective-permute-start | bytes 196616 | tf_op jit(solution)/shard_map/ppermute | solution.py:893
  29.7 6.1 %collective-permute-start.14 = (f32[128,128]{1,0:T(8,128)S(1)}, f32[128,128]{1,0:T(8,128)S(1)}, u32[]{:S(2)}, u32[]{:S(2)}) collective-permute-start(f32[128,128]{1,0:T(8,128)S(1)} %to_modes.1.refs_0_), channel_id=1, source_target_pairs={{0,24},{8,16},{16,8},{24,0},{1,25},{9,17},{17,9},{25,1},{2,26},{10... | collective-permute-start | bytes 196616 | tf_op jit(solution)/shard_map/ppermute | solution.py:893
  29.9 15.6 %collective-permute-start.17 = (f32[1024,128]{1,0:T(8,128)S(1)}, f32[1024,128]{1,0:T(8,128)S(1)}, u32[]{:S(2)}, u32[]{:S(2)}) collective-permute-start(f32[1024,128]{1,0:T(8,128)S(1)} %collective-permute-done.11.refs_5_), channel_id=1, source_target_pairs={{0,4},{1,3},{2,6},{3,1},{4,0},{5,7},{6,2},{7,5},{8,12},{9,11},{10,... | collective-permute-start | bytes 1572872 | tf_op jit(solution)/shard_map/ppermute | solution.py:897
  30.6 6.7 %copy-start.1 = (bf16[32,1,128,512]{3,2,1,0:T(8,128)(2,1)S(1)}, bf16[32,1,128,512]{3,2,1,0:T(8,128)(2,1)}, u32[]{:S(2)}) copy-start(bf16[32,1,128,512]{3,2,1,0:T(8,128)(2,1)} %param.10) | copy-start | bytes 12582916
  35.8 9.8 %collective-permute-start.16 = (f32[1024,128]{1,0:T(8,128)S(1)}, f32[1024,128]{1,0:T(8,128)S(1)}, u32[]{:S(2)}, u32[]{:S(2)}) collective-permute-start(f32[1024,128]{1,0:T(8,128)S(1)} %collective-permute-done.15.refs_0_), channel_id=1, source_target_pairs={{0,2},{1,5},{2,0},{3,7},{4,6},{5,1},{6,4},{7,3},{8,10},{9,13},{10,... | collective-permute-start | bytes 1572872 | tf_op jit(solution)/shard_map/ppermute | solution.py:897
  45.7 9.2 %collective-permute-start.21 = (f32[3072,128]{1,0:T(8,128)S(1)}, f32[3072,128]{1,0:T(8,128)S(1)}, u32[]{:S(2)}, u32[]{:S(2)}) collective-permute-start(f32[3072,128]{1,0:T(8,128)S(1)} %join.1.refs_6_), channel_id=1, source_target_pairs={{0,1},{1,0},{2,3},{3,2},{4,5},{5,4},{6,7},{7,6},{8,9},{9,8},{10,11... | collective-permute-start | bytes 4718600 | tf_op jit(solution)/shard_map/ppermute | solution.py:893
  45.7 8.0 %collective-permute-start.18 = (f32[128,128]{1,0:T(8,128)S(1)}, f32[128,128]{1,0:T(8,128)S(1)}, u32[]{:S(2)}, u32[]{:S(2)}) collective-permute-start(f32[128,128]{1,0:T(8,128)S(1)} %get-tuple-element.118), channel_id=1, source_target_pairs={{0,8},{8,0},{16,24},{24,16},{1,9},{9,1},{17,25},{25,17},{2,10},{10... | collective-permute-start | bytes 196616 | tf_op jit(solution)/shard_map/ppermute | solution.py:893
  45.8 7.9 %collective-permute-start.19 = (f32[128,128]{1,0:T(8,128)S(1)}, f32[128,128]{1,0:T(8,128)S(1)}, u32[]{:S(2)}, u32[]{:S(2)}) collective-permute-start(f32[128,128]{1,0:T(8,128)S(1)} %get-tuple-element.119), channel_id=1, source_target_pairs={{0,16},{8,24},{16,0},{24,8},{1,17},{9,25},{17,1},{25,9},{2,18},{10... | collective-permute-start | bytes 196616 | tf_op jit(solution)/shard_map/ppermute | solution.py:893
  48.8 6.1 %collective-permute-start.20 = (f32[128,128]{1,0:T(8,128)S(1)}, f32[128,128]{1,0:T(8,128)S(1)}, u32[]{:S(2)}, u32[]{:S(2)}) collective-permute-start(f32[128,128]{1,0:T(8,128)S(1)} %get-tuple-element.120), channel_id=1, source_target_pairs={{0,24},{8,16},{16,8},{24,0},{1,25},{9,17},{17,9},{25,1},{2,26},{10... | collective-permute-start | bytes 196616 | tf_op jit(solution)/shard_map/ppermute | solution.py:893
  56.4 4.5 %collective-permute-start.25 = (f32[4,32,128]{2,1,0:T(8,128)S(1)}, f32[4,32,128]{2,1,0:T(8,128)S(1)}, u32[]{:S(2)}, u32[]{:S(2)}) collective-permute-start(f32[4,32,128]{2,1,0:T(8,128)S(1)} %get-tuple-element.137), channel_id=1, source_target_pairs={{0,1},{1,0},{2,3},{3,2},{4,5},{5,4},{6,7},{7,6},{8,9},{9,8},{10,11... | collective-permute-start | bytes 196616 | tf_op jit(solution)/shard_map/ppermute | solution.py:893
  56.5 6.8 %collective-permute-start.22 = (f32[128,128]{1,0:T(8,128)S(1)}, f32[128,128]{1,0:T(8,128)S(1)}, u32[]{:S(2)}, u32[]{:S(2)}) collective-permute-start(f32[128,128]{1,0:T(8,128)S(1)} %get-tuple-element.133.refs_0_), channel_id=1, source_target_pairs={{0,8},{8,0},{16,24},{24,16},{1,9},{9,1},{17,25},{25,17},{2,10},{10... | collective-permute-start | bytes 196616 | tf_op jit(solution)/shard_map/ppermute | solution.py:893
  57.7 8.4 %collective-permute-start.23 = (f32[128,128]{1,0:T(8,128)S(1)}, f32[128,128]{1,0:T(8,128)S(1)}, u32[]{:S(2)}, u32[]{:S(2)}) collective-permute-start(f32[128,128]{1,0:T(8,128)S(1)} %get-tuple-element.133.refs_0_), channel_id=1, source_target_pairs={{0,16},{8,24},{16,0},{24,8},{1,17},{9,25},{17,1},{25,9},{2,18},{10... | collective-permute-start | bytes 196616 | tf_op jit(solution)/shard_map/ppermute | solution.py:893
  59.1 7.0 %collective-permute-start.24 = (f32[128,128]{1,0:T(8,128)S(1)}, f32[128,128]{1,0:T(8,128)S(1)}, u32[]{:S(2)}, u32[]{:S(2)}) collective-permute-start(f32[128,128]{1,0:T(8,128)S(1)} %get-tuple-element.133.refs_0_), channel_id=1, source_target_pairs={{0,24},{8,16},{16,8},{24,0},{1,25},{9,17},{17,9},{25,1},{2,26},{10... | collective-permute-start | bytes 196616 | tf_op jit(solution)/shard_map/ppermute | solution.py:893
  61.0 9.5 %collective-permute-start.26 = (f32[2,32,128]{2,1,0:T(8,128)S(1)}, f32[2,32,128]{2,1,0:T(8,128)S(1)}, u32[]{:S(2)}, u32[]{:S(2)}) collective-permute-start(f32[2,32,128]{2,1,0:T(8,128)S(1)} %get-tuple-element.139), channel_id=1, source_target_pairs={{0,2},{1,3},{2,0},{3,1},{4,6},{5,7},{6,4},{7,5},{8,10},{9,11},{10,... | collective-permute-start | bytes 98312 | tf_op jit(solution)/shard_map/ppermute | solution.py:893
  62.4 8.1 %collective-permute-start.27 = (f32[2,32,128]{2,1,0:T(8,128)S(1)}, f32[2,32,128]{2,1,0:T(8,128)S(1)}, u32[]{:S(2)}, u32[]{:S(2)}) collective-permute-start(f32[2,32,128]{2,1,0:T(8,128)S(1)} %get-tuple-element.140), channel_id=1, source_target_pairs={{0,4},{1,5},{2,6},{3,7},{4,0},{5,1},{6,2},{7,3},{8,12},{9,13},{10,... | collective-permute-start | bytes 98312 | tf_op jit(solution)/shard_map/ppermute | solution.py:893
  63.3 7.2 %collective-permute-start.28 = (f32[2,32,128]{2,1,0:T(8,128)S(1)}, f32[2,32,128]{2,1,0:T(8,128)S(1)}, u32[]{:S(2)}, u32[]{:S(2)}) collective-permute-start(f32[2,32,128]{2,1,0:T(8,128)S(1)} %get-tuple-element.141), channel_id=1, source_target_pairs={{0,6},{1,7},{2,4},{3,5},{4,2},{5,3},{6,0},{7,1},{8,14},{9,15},{10,... | collective-permute-start | bytes 98312 | tf_op jit(solution)/shard_map/ppermute | solution.py:893

commit v4 on v3

--- a/solution.py
+++ b/solution.py
@@ -163,6 +163,15 @@
 
 def place_of():
     return lax.axis_index("px"), lax.axis_index("py")
+
+
+TURN = (0, 2, 1, 3)
+
+
+def flip_at(step):
+    chip, other = step // 2, step % 2
+    core = lax.axis_index("py") % 2
+    return jnp.where(core == 1, 2 * chip + other, 2 * TURN[chip] + other)
 
 
 def split(values):
@@ -347,7 +356,7 @@
     out_ref[...] = piece
     modes_y, modes_x, channels = ky_ref.shape[0], kx_ref.shape[0], bias_ref.shape[0]
     ky = column_of(ky_ref, lambda i: (place_x ^ (i // local_y)) * local_y + i % local_y, modes_y)
-    kx = column_of(kx_ref, lambda i: (place_y ^ (i // local_x)) * local_x + i % local_x, modes_x)
+    kx = column_of(kx_ref, lambda i: (place_y ^ flip_at(i // local_x)) * local_x + i % local_x, modes_x)
     bias = column_of(bias_ref, lambda i: i, channels)
     weight = weight_ref[...].astype(jnp.float32)
     weight = jnp.concatenate([weight, jnp.zeros((channels, lanes - channels), jnp.float32)], 1)
@@ -411,7 +420,7 @@
 
     lax.fori_loop(0, channels, step, 0, unroll=4)
     for step in range(planes):
-        (other_ref if step % 2 else same_ref)[step // 2] = out_ref[place ^ step]
+        (other_ref if step % 2 else same_ref)[step // 2] = out_ref[place ^ flip_at(step)]
 
 
 def mix(packed, pieces, planes, local_x):
@@ -449,7 +458,7 @@
     for index, grad in enumerate(grads):
         swapped = swap_halves(grad[...])
         gs_ref[index] = jnp.where(lanes_of(swapped.shape) < capacity, swapped, -swapped)
-        starts.append((place_of()[1] ^ index) * 2 * channels)
+        starts.append((place_of()[1] ^ flip_at(index)) * 2 * channels)
     chunks = sems.shape[0]
     size = channels // chunks
 
@@ -507,7 +516,7 @@
     for mode in range(slots_ref.shape[0] // modes_x):
         numbers = slots_ref[pl.ds(mode * modes_x, modes_x)]
         for owner in range(chosen_ref.shape[1] // lanes):
-            wanted = ((owner ^ place) * capacity + lane % capacity).astype(jnp.float32)
+            wanted = ((place ^ flip_at(owner)) * capacity + lane % capacity).astype(jnp.float32)
             hit = jnp.where(numbers == wanted, 1.0, 0.0)
             both = jnp.concatenate([jnp.where(first, hit, zero), jnp.where(first, zero, hit)], 0)
             chosen_ref[pl.ds(mode * 2 * modes_x, 2 * modes_x), pl.ds(owner * lanes, lanes)] = both.astype(jnp.bfloat16)
@@ -582,7 +591,6 @@
     high, low = split(jnp.concatenate(columns, 1))
     found = dot(jnp.concatenate([high, low], 0), chosen_ref[...])
     found = found[:channels] + found[channels:]
-    core = place_of()[1] % 2
     size = channels * channels
     here, beside, others, over = stores
 
@@ -590,15 +598,9 @@
         chip, other = owner // 2, owner % 2
         if chip == 0:
             return lambda channel: (beside if other else here)[pl.ds(channel * channels, channels)]
-        if chip == 3:
-            return lambda channel: (over if other else others)[pl.ds(2 * size + channel * channels, channels)]
-
-        def block(channel):
-            own = others[pl.ds(other * size + channel * channels, channels)]
-            came = over[pl.ds((1 - other) * size + channel * channels, channels)]
-            return jnp.where(core == 2 - chip, own, came)
-
-        return block
+        start = (2 if chip == 3 else abs(chip - 1 - other)) * size
+        source = over if chip == 2 or chip == 3 and other else others
+        return lambda channel: source[pl.ds(start + channel * channels, channels)]
 
     mixed = []
     for owner in range(2 * steps):
@@ -628,7 +630,7 @@
 def pair_kernel(same_ref, other_ref, *outs):
     for index, out in enumerate(outs):
         out[0] = same_ref[index]
-        out[1] = other_ref[index]
+        out[1] = other_ref[TURN[index]]
 
 
 def pair(same, other):
@@ -867,7 +869,7 @@
     lax.fori_loop(0, steps, settle, 0)
 
 
-def finish(pieces, tables, part, group=2):
+def finish(pieces, tables, part, group=4):
     ti, _, xi, _ = tables
     blocks = len(pieces)
     channels, rows_x, _ = part.shape
@@ -897,18 +899,26 @@
     return lax.ppermute(piece, axis, [(i, i ^ flips[i % 2]) for i in range(count)])
 
 
+def around(pieces, count):
+    return [
+        pieces[0],
+        exchange_two(pieces[1], "py", count, 4, 2),
+        exchange_two(pieces[2], "py", count, 2, 4),
+        exchange(pieces[3], "py", count, 6),
+    ]
+
+
 def to_owners(same, other, count):
-    pairs = list(pair(same, exchange(other, "py", count, 1)))
-    return pairs[:1] + [exchange(pairs[i], "py", count, 2 * i) for i in range(1, len(pairs))]
+    return around(pair(same, exchange(other, "py", count, 1)), count)
 
 
 def between_chips(piece, count):
-    return [piece] + [exchange(piece, "py", count, step) for step in range(2, count, 2)]
+    return around([piece] * 4, count)
 
 
 def between_cores(pieces, count, beside):
     other = [beside] + [exchange(piece, "py", count, 1) for piece in pieces[1:]]
-    return [each for pair in zip(pieces, other) for each in pair]
+    return [each for i, piece in enumerate(pieces) for each in (piece, other[TURN[i]])]
 
 
 def from_all(piece, axis, count):

time: 72.8 us -> 72.7 us (level)
    ppermute x26 -> x20, starting transfers between devices: 26.4 us -> 18.2 us  [exchange(): return lax.ppermute(piece, axis, [(i, i ^ flip) for i in range(count)])]
    ppermute x3 -> x9, starting transfers between devices: 3.52 us -> 11.7 us  [exchange_two(): lax.ppermute(piece, axis, [(i, i ^ flips[i % 2]) for i in range(count)])]
    ppermute x3 -> x9, waiting for transfers between devices: 0.01 us -> 2.4 us  [exchange_two(): lax.ppermute(piece, axis, [(i, i ^ flips[i % 2]) for i in range(count)])]
    ppermute x26 -> x20, waiting for transfers between devices: 12 us -> 9.72 us  [exchange(): return lax.ppermute(piece, axis, [(i, i ^ flip) for i in range(count)])]
  transfers between devices with their start and end apart: 29 -> 29, of which waited for: 13 -> 13; matrix products, arithmetic and copies ran while one was open for 0% -> 0% of each run, Pallas kernels for 31% -> 30%
where the time goes in v4:
time: 72.7 us; the launch traced here: 72.5 us
  starting transfers between devices  29.9 us (41%)
  Pallas kernels  27.6 us (38%)
  waiting for transfers between devices  12.1 us (17%)
  local copies, waits for them, and re-layouts  2.14 us (3%)
  between operations  0.84 us (1%)
    ppermute x20, starting transfers between devices, exchange(): return lax.ppermute(piece, axis, [(i, i ^ flip) for i in range(count)])  18.2 us
    ppermute x9, starting transfers between devices, exchange_two(): lax.ppermute(piece, axis, [(i, i ^ flips[i % 2]) for i in range(count)])  11.7 us
    ppermute x20, waiting for transfers between devices, exchange(): return lax.ppermute(piece, axis, [(i, i ^ flip) for i in range(count)])  9.72 us
    pallas_call x1, Pallas kernels, slope_step(): pl.pallas_call(functools.partial(slope_kernel, blocks=blocks), out_shape=...  8.26 us
    pallas_call x1, Pallas kernels, finish(): pl.pallas_call(functools.partial(finish_kernel, blocks=blocks, group=grou...  4.28 us
    pallas_call x1, Pallas kernels, pointwise_back(): pl.pallas_call(pointwise_back_kernel, out_shape=jax.ShapeDtypeStruct((2 *...  3.52 us
    pallas_call x1, Pallas kernels, pointwise_map(): pl.pallas_call(pointwise_kernel, out_shape=jax.ShapeDtypeStruct(values.sh...  2.45 us
    ppermute x9, waiting for transfers between devices, exchange_two(): lax.ppermute(piece, axis, [(i, i ^ flips[i % 2]) for i in range(count)])  2.4 us
  transfers between devices with their start and end apart: 29, of which 13 were waited for; matrix products, arithmetic and copies ran while one was open for 0% of the time, Pallas kernels for 30%

profile of v4, /device:TPU:0, one launch (start us, length us, event | category | flops | bytes accessed | tf_op | source)
XLA Modules:
  0.0 72.5 jit_solution(12637201218848390073)
XLA Ops:
  0.6 1.8 %pack.1 = (f32[32,640]{1,0:T(8,128)}, f32[32,1152]{1,0:T(8,128)}) custom-call(s32[4,8]{1,0:T(4,128)} %refs_0_.1, f32[512,32]{1,0:T(8,128)} %bitcast.14, s32[32]{0:T(128)} %refs_2_.1, s32[32]{0:T(128)} %refs_3_.1, f32[32]{0:T(128)} %refs_4_.1, bf16[32,32]{1,0:T(8,128)(2,1)} %refs_5_.1), custom_call_target="tpu_custom_call" | custom-call | tf_op jit(solution)/shard_map/pack/pallas_call | solution.py:371
  2.5 3.0 %collective-permute-start = (f32[32,640]{1,0:T(8,128)}, f32[32,640]{1,0:T(8,128)S(1)}, u32[]{:S(2)}, u32[]{:S(2)}) collective-permute-start(f32[32,640]{1,0:T(8,128)} %get-tuple-element.74), channel_id=1, source_target_pairs={{0,4},{1,3},{2,6},{3,1},{4,0},{5,7},{6,2},{7,5},{8,12},{9,11},{10,... | collective-permute-start | bytes 245768 | tf_op jit(solution)/shard_map/ppermute | solution.py:899
  5.5 1.5 %collective-permute-start.1 = (f32[32,640]{1,0:T(8,128)}, f32[32,640]{1,0:T(8,128)S(1)}, u32[]{:S(2)}, u32[]{:S(2)}) collective-permute-start(f32[32,640]{1,0:T(8,128)} %get-tuple-element.74), channel_id=1, source_target_pairs={{0,2},{1,5},{2,0},{3,7},{4,6},{5,1},{6,4},{7,3},{8,10},{9,13},{10,... | collective-permute-start | bytes 245768 | tf_op jit(solution)/shard_map/ppermute | solution.py:899
  7.0 0.0 collective-permute-start.2
  7.0 0.0 collective-permute-start.3
  7.1 1.2 %copy-done.2 = f32[64,2,32,32]{0,3,2,1:T(8,128)S(1)} copy-done((f32[64,2,32,32]{0,3,2,1:T(8,128)S(1)}, f32[64,2,32,32]{0,3,2,1:T(8,128)}, u32[]{:S(2)}) %copy-start.2) | copy-done | bytes 524312
  8.3 0.9 %copy-done.3 = f32[32,1152]{1,0:T(8,128)S(1)} copy-done((f32[32,1152]{1,0:T(8,128)S(1)}, f32[32,1152]{1,0:T(8,128)}, u32[]{:S(2)}) %copy-start.3) | copy-done | bytes 147480
  9.2 0.2 unpack.1
  9.4 0.0 collective-permute-done.refs_2_
  9.4 1.4 %collective-permute-done.1.refs_4_ = f32[32,640]{1,0:T(8,128)S(1)} collective-permute-done((f32[32,640]{1,0:T(8,128)}, f32[32,640]{1,0:T(8,128)S(1)}, u32[]{:S(2)}, u32[]{:S(2)}) %collective-permute-start.1) | collective-permute-done | bytes 81952 | tf_op jit(solution)/shard_map/ppermute | solution.py:899
  10.8 1.8 %collective-permute-done.2.refs_6_ = f32[32,640]{1,0:T(8,128)S(1)} collective-permute-done((f32[32,640]{1,0:T(8,128)}, f32[32,640]{1,0:T(8,128)S(1)}, u32[]{:S(2)}, u32[]{:S(2)}) %collective-permute-start.2) | collective-permute-done | bytes 81952 | tf_op jit(solution)/shard_map/ppermute | solution.py:895
  12.6 0.5 collective-permute-start.5
  13.1 0.0 collective-permute-start.6
  13.1 0.5 collective-permute-start.11
  13.6 0.3 collective-permute-done.4.refs_3_
  13.8 0.2 collective-permute-done.5.refs_5_
  14.0 0.4 collective-permute-done.6.refs_7_
  14.3 1.8 %mix.1 = (f32[512,128]{1,0:T(8,128)S(1)}, f32[256,128]{1,0:T(8,128)S(1)}, f32[4,32,128]{2,1,0:T(8,128)S(1)}, f32[4,32,128]{2,1,0:T(8,128)S(1)}) custom-call(f32[1024,128]{1,0:T(8,128)S(1)} %get-tuple-element.97.packed_ref.refs_4_, f32[32,640]{1,0:T(8,128)S(1)} %get-tuple-element.76.refs_0_, f32[32,640]{1,0:T(8,128)S(1)} %collective-permute-done.3.refs_1_, ...), custom_call_target="tpu_custom_call" | custom-call | flops 3000000000 | bytes 1048576 | tf_op jit(solution)/shard_map/mix/pallas_call | solution.py:429
  16.2 0.2 collective-permute-start.7
  16.4 0.8 %tables.1 = (bf16[2,256,512]{2,1,0:T(8,128)(2,1)S(1)}, bf16[128,512]{1,0:T(8,128)(2,1)S(1)}, bf16[384,512]{1,0:T(8,128)(2,1)S(1)}, bf16[512,256]{1,0:T(8,128)(2,...) custom-call(f32[32,512]{1,0:T(8,128)S(1)} %get-tuple-element.88.small_ref), custom_call_target="tpu_custom_call" | custom-call | flops 1000000000 | bytes 1048576 | tf_op jit(solution)/shard_map/tables/pallas_call | solution.py:321
  17.2 0.3 collective-permute-done.7.other_ref
  17.5 0.6 collective-permute-start.8
  18.1 0.9 %collective-permute-start.9 = (f32[2,32,128]{2,1,0:T(8,128)S(1)}, f32[2,32,128]{2,1,0:T(8,128)S(1)}, u32[]{:S(2)}, u32[]{:S(2)}) collective-permute-start(f32[2,32,128]{2,1,0:T(8,128)S(1)} %get-tuple-element.85), channel_id=1, source_target_pairs={{0,2},{1,5},{2,0},{3,7},{4,6},{5,1},{6,4},{7,3},{8,10},{9,13},{10,... | collective-permute-start | bytes 98312 | tf_op jit(solution)/shard_map/ppermute | solution.py:899
  19.0 2.0 %collective-permute-start.10 = (f32[2,32,128]{2,1,0:T(8,128)S(1)}, f32[2,32,128]{2,1,0:T(8,128)S(1)}, u32[]{:S(2)}, u32[]{:S(2)}) collective-permute-start(f32[2,32,128]{2,1,0:T(8,128)S(1)} %get-tuple-element.86), channel_id=1, source_target_pairs={{0,6},{1,7},{2,4},{3,5},{4,2},{5,3},{6,0},{7,1},{8,14},{9,15},{10,... | collective-permute-start | bytes 98312 | tf_op jit(solution)/shard_map/ppermute | solution.py:895
  21.1 0.2 select.1.chosen_ref
  21.3 0.2 collective-permute-done.8.refs_1_
  21.5 0.8 %collective-permute-done.9.refs_2_ = f32[2,32,128]{2,1,0:T(8,128)S(1)} collective-permute-done((f32[2,32,128]{2,1,0:T(8,128)S(1)}, f32[2,32,128]{2,1,0:T(8,128)S(1)}, u32[]{:S(2)}, u32[]{:S(2)}) %collective-permute-start.9) | collective-permute-done | bytes 32800 | tf_op jit(solution)/shard_map/ppermute | solution.py:899
  22.3 1.5 %collective-permute-done.10.refs_3_ = f32[2,32,128]{2,1,0:T(8,128)S(1)} collective-permute-done((f32[2,32,128]{2,1,0:T(8,128)S(1)}, f32[2,32,128]{2,1,0:T(8,128)S(1)}, u32[]{:S(2)}, u32[]{:S(2)}) %collective-permute-start.10) | collective-permute-done | bytes 32800 | tf_op jit(solution)/shard_map/ppermute | solution.py:895
  23.8 0.0 collective-permute-done.11.refs_5_
  23.8 1.2 %collective-permute-start.15 = (f32[1024,128]{1,0:T(8,128)S(1)}, f32[1024,128]{1,0:T(8,128)S(1)}, u32[]{:S(2)}, u32[]{:S(2)}) collective-permute-start(f32[1024,128]{1,0:T(8,128)S(1)} %get-tuple-element.97.packed_ref.refs_4_), channel_id=1, source_target_pairs={{0,4},{1,3},{2,6},{3,1},{4,0},{5,7},{6,2},{7,5},{8,12},{9,11},{10,... | collective-permute-start | bytes 1572872 | tf_op jit(solution)/shard_map/ppermute | solution.py:899
  25.0 0.5 to_modes.1.refs_0_
  25.5 1.6 %collective-permute-start.12 = (f32[128,128]{1,0:T(8,128)S(1)}, f32[128,128]{1,0:T(8,128)S(1)}, u32[]{:S(2)}, u32[]{:S(2)}) collective-permute-start(f32[128,128]{1,0:T(8,128)S(1)} %to_modes.1.refs_0_), channel_id=1, source_target_pairs={{0,8},{8,0},{16,24},{24,16},{1,9},{9,1},{17,25},{25,17},{2,10},{10... | collective-permute-start | bytes 196616 | tf_op jit(solution)/shard_map/ppermute | solution.py:895
  27.2 2.6 %collective-permute-start.13 = (f32[128,128]{1,0:T(8,128)S(1)}, f32[128,128]{1,0:T(8,128)S(1)}, u32[]{:S(2)}, u32[]{:S(2)}) collective-permute-start(f32[128,128]{1,0:T(8,128)S(1)} %to_modes.1.refs_0_), channel_id=1, source_target_pairs={{0,16},{8,24},{16,0},{24,8},{1,17},{9,25},{17,1},{25,9},{2,18},{10... | collective-permute-start | bytes 196616 | tf_op jit(solution)/shard_map/ppermute | solution.py:895
  29.8 0.2 collective-permute-start.14
  30.0 0.8 %collective-permute-start.17 = (f32[1024,128]{1,0:T(8,128)S(1)}, f32[1024,128]{1,0:T(8,128)S(1)}, u32[]{:S(2)}, u32[]{:S(2)}) collective-permute-start(f32[1024,128]{1,0:T(8,128)S(1)} %collective-permute-done.11.refs_5_), channel_id=1, source_target_pairs={{0,4},{1,3},{2,6},{3,1},{4,0},{5,7},{6,2},{7,5},{8,12},{9,11},{10,... | collective-permute-start | bytes 1572872 | tf_op jit(solution)/shard_map/ppermute | solution.py:899
  30.8 2.4 %pointwise_map.1.refs_8_ = f32[32,128,512]{2,1,0:T(8,128)S(1)} custom-call(bf16[256,256]{1,0:T(8,128)(2,1)S(1)} %get-tuple-element.95.full_ref, f32[256,128]{1,0:T(8,128)S(1)} %get-tuple-element.96.shift_ref, bf16[32,128,512]{2,1,0:T(8,128)(2,1)S(1)} %bitcast.10), custom_call_target="tpu_custom_call" | custom-call | flops 3000000000 | bytes 1048576 | tf_op jit(solution)/shard_map/pointwise_map/pallas_call | solution.py:698
  33.3 0.4 collective-permute-done.13.refs_2_
  33.8 2.1 %collective-permute-done.14.refs_3_ = f32[128,128]{1,0:T(8,128)S(1)} collective-permute-done((f32[128,128]{1,0:T(8,128)S(1)}, f32[128,128]{1,0:T(8,128)S(1)}, u32[]{:S(2)}, u32[]{:S(2)}) %collective-permute-start.14) | collective-permute-done | bytes 65568 | tf_op jit(solution)/shard_map/ppermute | solution.py:895
  35.8 0.0 collective-permute-done.15.refs_0_
  35.8 1.4 %collective-permute-start.16 = (f32[1024,128]{1,0:T(8,128)S(1)}, f32[1024,128]{1,0:T(8,128)S(1)}, u32[]{:S(2)}, u32[]{:S(2)}) collective-permute-start(f32[1024,128]{1,0:T(8,128)S(1)} %collective-permute-done.15.refs_0_), channel_id=1, source_target_pairs={{0,2},{1,5},{2,0},{3,7},{4,6},{5,1},{6,4},{7,3},{8,10},{9,13},{10,... | collective-permute-start | bytes 1572872 | tf_op jit(solution)/shard_map/ppermute | solution.py:899
  37.3 8.3 %slope_step.1 = (bf16[8,2,128,512]{3,2,1,0:T(8,128)(2,1)S(1)}, bf16[8,2,128,512]{3,2,1,0:T(8,128)(2,1)S(1)}, bf16[8,2,128,512]{3,2,1,0:T(8,128)(2,1)S(1)}, bf16[...) custom-call(f32[128,128]{1,0:T(8,128)S(1)} %to_modes.1.refs_0_, ...), custom_call_target="tpu_custom_call" | custom-call | flops 8000000000 | bytes 1048576 | tf_op jit(solution)/shard_map/slope_step/pallas_call | solution.py:827
  45.5 0.0 collective-permute-done.16.refs_2_
  45.6 0.1 join.1.refs_6_
  45.7 0.1 collective-permute-start.21
  45.7 0.1 collective-permute-start.18
  45.9 3.0 %collective-permute-start.19 = (f32[128,128]{1,0:T(8,128)S(1)}, f32[128,128]{1,0:T(8,128)S(1)}, u32[]{:S(2)}, u32[]{:S(2)}) collective-permute-start(f32[128,128]{1,0:T(8,128)S(1)} %get-tuple-element.119), channel_id=1, source_target_pairs={{0,16},{8,24},{16,0},{24,8},{1,17},{9,25},{17,1},{25,9},{2,18},{10... | collective-permute-start | bytes 196616 | tf_op jit(solution)/shard_map/ppermute | solution.py:895
  48.9 1.3 %collective-permute-start.20 = (f32[128,128]{1,0:T(8,128)S(1)}, f32[128,128]{1,0:T(8,128)S(1)}, u32[]{:S(2)}, u32[]{:S(2)}) collective-permute-start(f32[128,128]{1,0:T(8,128)S(1)} %get-tuple-element.120), channel_id=1, source_target_pairs={{0,24},{8,16},{16,8},{24,0},{1,25},{9,17},{17,9},{25,1},{2,26},{10... | collective-permute-start | bytes 196616 | tf_op jit(solution)/shard_map/ppermute | solution.py:895
  50.2 3.5 %pointwise_back.1.refs_6_ = f32[32,128,512]{2,1,0:T(8,128)S(1)} custom-call(bf16[256,256]{1,0:T(8,128)(2,1)S(1)} %get-tuple-element.121.full_ref, bf16[8,2,128,512]{3,2,1,0:T(8,128)(2,1)S(1)} %get-tuple-element.122.refs_0_, bf16[8,2,128,512]{3,2,1,0:T(8,128)(2,1)S(1)} %get-tuple-element.123.refs_1_, bf16[8,2,128,512]{3,2,1,0:T(8,128)(2,1)S(1)} %get-tuple-element.124.refs_2_, ...), custom_call_target="tpu_custom_call" | custom-call | flops 4000000000 | bytes 1048576 | tf_op jit(solution)/shard_map/pointwise_back/pallas_call | solution.py:733
  53.7 0.0 collective-permute-done.19.refs_2_
  53.8 1.3 %collective-permute-done.20.refs_3_ = f32[128,128]{1,0:T(8,128)S(1)} collective-permute-done((f32[128,128]{1,0:T(8,128)S(1)}, f32[128,128]{1,0:T(8,128)S(1)}, u32[]{:S(2)}, u32[]{:S(2)}) %collective-permute-start.20) | collective-permute-done | bytes 65568 | tf_op jit(solution)/shard_map/ppermute | solution.py:895
  55.0 0.0 collective-permute-done.21.refs_7_
  55.0 1.4 %adjoint.1 = (f32[4,32,128]{2,1,0:T(8,128)S(1)}, f32[4,32,128]{2,1,0:T(8,128)S(1)}, f32[128,128]{1,0:T(8,128)S(1)}) custom-call(bf16[512,1024]{1,0:T(8,128)(2,1)S(1)} %select.1.chosen_ref, f32[128,128]{1,0:T(8,128)S(1)} %get-tuple-element.128.refs_0_, f32[128,128]{1,0:T(8,128)S(1)} %collective-permute-done.18.refs_1_, ...), custom_call_target="tpu_custom_call" | custom-call | flops 2000000000 | bytes 1048576 | tf_op jit(solution)/shard_map/adjoint/pallas_call | solution.py:617
  56.4 0.1 collective-permute-start.25
  56.5 1.2 %collective-permute-start.22 = (f32[128,128]{1,0:T(8,128)S(1)}, f32[128,128]{1,0:T(8,128)S(1)}, u32[]{:S(2)}, u32[]{:S(2)}) collective-permute-start(f32[128,128]{1,0:T(8,128)S(1)} %get-tuple-element.133.refs_0_), channel_id=1, source_target_pairs={{0,8},{8,0},{16,24},{24,16},{1,9},{9,1},{17,25},{25,17},{2,10},{10... | collective-permute-start | bytes 196616 | tf_op jit(solution)/shard_map/ppermute | solution.py:895
  57.7 1.5 %collective-permute-start.23 = (f32[128,128]{1,0:T(8,128)S(1)}, f32[128,128]{1,0:T(8,128)S(1)}, u32[]{:S(2)}, u32[]{:S(2)}) collective-permute-start(f32[128,128]{1,0:T(8,128)S(1)} %get-tuple-element.133.refs_0_), channel_id=1, source_target_pairs={{0,16},{8,24},{16,0},{24,8},{1,17},{9,25},{17,1},{25,9},{2,18},{10... | collective-permute-start | bytes 196616 | tf_op jit(solution)/shard_map/ppermute | solution.py:895
  59.1 1.8 %collective-permute-start.24 = (f32[128,128]{1,0:T(8,128)S(1)}, f32[128,128]{1,0:T(8,128)S(1)}, u32[]{:S(2)}, u32[]{:S(2)}) collective-permute-start(f32[128,128]{1,0:T(8,128)S(1)} %get-tuple-element.133.refs_0_), channel_id=1, source_target_pairs={{0,24},{8,16},{16,8},{24,0},{1,25},{9,17},{17,9},{25,1},{2,26},{10... | collective-permute-start | bytes 196616 | tf_op jit(solution)/shard_map/ppermute | solution.py:895
  60.9 0.0 collective-permute-done.25.other_ref
  61.0 1.1 %collective-permute-start.26 = (f32[2,32,128]{2,1,0:T(8,128)S(1)}, f32[2,32,128]{2,1,0:T(8,128)S(1)}, u32[]{:S(2)}, u32[]{:S(2)}) collective-permute-start(f32[2,32,128]{2,1,0:T(8,128)S(1)} %get-tuple-element.139), channel_id=1, source_target_pairs={{0,4},{1,3},{2,6},{3,1},{4,0},{5,7},{6,2},{7,5},{8,12},{9,11},{10,... | collective-permute-start | bytes 98312 | tf_op jit(solution)/shard_map/ppermute | solution.py:899
  62.0 1.2 %collective-permute-start.27 = (f32[2,32,128]{2,1,0:T(8,128)S(1)}, f32[2,32,128]{2,1,0:T(8,128)S(1)}, u32[]{:S(2)}, u32[]{:S(2)}) collective-permute-start(f32[2,32,128]{2,1,0:T(8,128)S(1)} %get-tuple-element.140), channel_id=1, source_target_pairs={{0,2},{1,5},{2,0},{3,7},{4,6},{5,1},{6,4},{7,3},{8,10},{9,13},{10,... | collective-permute-start | bytes 98312 | tf_op jit(solution)/shard_map/ppermute | solution.py:899
  63.2 1.3 %collective-permute-start.28 = (f32[2,32,128]{2,1,0:T(8,128)S(1)}, f32[2,32,128]{2,1,0:T(8,128)S(1)}, u32[]{:S(2)}, u32[]{:S(2)}) collective-permute-start(f32[2,32,128]{2,1,0:T(8,128)S(1)} %get-tuple-element.141), channel_id=1, source_target_pairs={{0,6},{1,7},{2,4},{3,5},{4,2},{5,3},{6,0},{7,1},{8,14},{9,15},{10,... | collective-permute-start | bytes 98312 | tf_op jit(solution)/shard_map/ppermute | solution.py:895
  64.5 1.6 %collective-permute-done.23.refs_2_ = f32[128,128]{1,0:T(8,128)S(1)} collective-permute-done((f32[128,128]{1,0:T(8,128)S(1)}, f32[128,128]{1,0:T(8,128)S(1)}, u32[]{:S(2)}, u32[]{:S(2)}) %collective-permute-start.23) | collective-permute-done | bytes 65568 | tf_op jit(solution)/shard_map/ppermute | solution.py:895
  66.1 4.3 %finish.1 = f32[32,128,512]{2,1,0:T(8,128)} custom-call(f32[128,128]{1,0:T(8,128)S(1)} %get-tuple-element.133.refs_0_, f32[128,128]{1,0:T(8,128)S(1)} %collective-permute-done.22.refs_1_, f32[128,128]{1,0:T(8,128)S(1)} %collective-permute-done.23.refs_2_, f32[128,128]{1,0:T(8,128)S(1)} %collective-permute-done.24.refs_3_, ...), custom_call_target="tpu_custom_call" | custom-call | flops 4000000000 | bytes 1048576 | tf_op jit(solution)/shard_map/finish/pallas_call | solution.py:878
  70.4 0.0 collective-permute-done.26.refs_1_
  70.4 2.1 %weight_grad.1 = f32[2,32,32,64]{3,2,1,0:T(8,128)} custom-call(f32[512,128]{1,0:T(8,128)S(1)} %get-tuple-element.135.kept_ref, f32[2,32,128]{2,1,0:T(8,128)S(1)} %get-tuple-element.138.refs_0_, f32[2,32,128]{2,1,0:T(8,128)S(1)} %collective-permute-done.26.refs_1_, f32[2,32,128]{2,1,0:T(8,128)S(1)} %collective-permute-done.27.refs_2_, ...), custom_call_target="tpu_custom_call" | custom-call | flops 2000000000 | bytes 1048576 | tf_op jit(solution)/shard_map/weight_grad/pallas_call | solution.py:492
  (17 shorter events, 0.1 us)
Async XLA Ops:
  2.5 6.9 %collective-permute-start = (f32[32,640]{1,0:T(8,128)}, f32[32,640]{1,0:T(8,128)S(1)}, u32[]{:S(2)}, u32[]{:S(2)}) collective-permute-start(f32[32,640]{1,0:T(8,128)} %get-tuple-element.74), channel_id=1, source_target_pairs={{0,4},{1,3},{2,6},{3,1},{4,0},{5,7},{6,2},{7,5},{8,12},{9,11},{10,... | collective-permute-start | bytes 245768 | tf_op jit(solution)/shard_map/ppermute | solution.py:899
  5.5 5.3 %collective-permute-start.1 = (f32[32,640]{1,0:T(8,128)}, f32[32,640]{1,0:T(8,128)S(1)}, u32[]{:S(2)}, u32[]{:S(2)}) collective-permute-start(f32[32,640]{1,0:T(8,128)} %get-tuple-element.74), channel_id=1, source_target_pairs={{0,2},{1,5},{2,0},{3,7},{4,6},{5,1},{6,4},{7,3},{8,10},{9,13},{10,... | collective-permute-start | bytes 245768 | tf_op jit(solution)/shard_map/ppermute | solution.py:899
  7.0 5.6 %collective-permute-start.2 = (f32[32,640]{1,0:T(8,128)}, f32[32,640]{1,0:T(8,128)S(1)}, u32[]{:S(2)}, u32[]{:S(2)}) collective-permute-start(f32[32,640]{1,0:T(8,128)} %get-tuple-element.74), channel_id=1, source_target_pairs={{0,6},{1,7},{2,4},{3,5},{4,2},{5,3},{6,0},{7,1},{8,14},{9,15},{10,... | collective-permute-start | bytes 245768 | tf_op jit(solution)/shard_map/ppermute | solution.py:895
  7.0 5.5 %collective-permute-start.3 = (f32[32,640]{1,0:T(8,128)}, f32[32,640]{1,0:T(8,128)S(1)}, u32[]{:S(2)}, u32[]{:S(2)}) collective-permute-start(f32[32,640]{1,0:T(8,128)} %get-tuple-element.74), channel_id=1, source_target_pairs={{0,1},{1,0},{2,3},{3,2},{4,5},{5,4},{6,7},{7,6},{8,9},{9,8},{10,11... | collective-permute-start | bytes 245768 | tf_op jit(solution)/shard_map/ppermute | solution.py:895
  7.1 1.2 %copy-start.2 = (f32[64,2,32,32]{0,3,2,1:T(8,128)S(1)}, f32[64,2,32,32]{0,3,2,1:T(8,128)}, u32[]{:S(2)}) copy-start(f32[64,2,32,32]{0,3,2,1:T(8,128)} %param.12) | copy-start | bytes 1572868
  8.3 0.9 %copy-start.3 = (f32[32,1152]{1,0:T(8,128)S(1)}, f32[32,1152]{1,0:T(8,128)}, u32[]{:S(2)}) copy-start(f32[32,1152]{1,0:T(8,128)} %get-tuple-element.72.all_ref) | copy-start | bytes 442372
  12.6 1.3 %collective-permute-start.4 = (f32[32,640]{1,0:T(8,128)S(1)}, f32[32,640]{1,0:T(8,128)S(1)}, u32[]{:S(2)}, u32[]{:S(2)}) collective-permute-start(f32[32,640]{1,0:T(8,128)S(1)} %collective-permute-done.1.refs_4_), channel_id=1, source_target_pairs={{0,1},{1,0},{2,3},{3,2},{4,5},{5,4},{6,7},{7,6},{8,9},{9,8},{10,11... | collective-permute-start | bytes 245768 | tf_op jit(solution)/shard_map/ppermute | solution.py:895
  12.6 1.4 %collective-permute-start.5 = (f32[32,640]{1,0:T(8,128)S(1)}, f32[32,640]{1,0:T(8,128)S(1)}, u32[]{:S(2)}, u32[]{:S(2)}) collective-permute-start(f32[32,640]{1,0:T(8,128)S(1)} %collective-permute-done.refs_2_), channel_id=1, source_target_pairs={{0,1},{1,0},{2,3},{3,2},{4,5},{5,4},{6,7},{7,6},{8,9},{9,8},{10,11... | collective-permute-start | bytes 245768 | tf_op jit(solution)/shard_map/ppermute | solution.py:895
  13.1 1.3 %collective-permute-start.6 = (f32[32,640]{1,0:T(8,128)S(1)}, f32[32,640]{1,0:T(8,128)S(1)}, u32[]{:S(2)}, u32[]{:S(2)}) collective-permute-start(f32[32,640]{1,0:T(8,128)S(1)} %collective-permute-done.2.refs_6_), channel_id=1, source_target_pairs={{0,1},{1,0},{2,3},{3,2},{4,5},{5,4},{6,7},{7,6},{8,9},{9,8},{10,11... | collective-permute-start | bytes 245768 | tf_op jit(solution)/shard_map/ppermute | solution.py:895
  13.1 10.8 %collective-permute-start.11 = (f32[1024,128]{1,0:T(8,128)S(1)}, f32[1024,128]{1,0:T(8,128)S(1)}, u32[]{:S(2)}, u32[]{:S(2)}) collective-permute-start(f32[1024,128]{1,0:T(8,128)S(1)} %get-tuple-element.97.packed_ref.refs_4_), channel_id=1, source_target_pairs={{0,1},{1,0},{2,3},{3,2},{4,5},{5,4},{6,7},{7,6},{8,9},{9,8},{10,11... | collective-permute-start | bytes 1572872 | tf_op jit(solution)/shard_map/ppermute | solution.py:895
  16.2 1.3 %collective-permute-start.7 = (f32[4,32,128]{2,1,0:T(8,128)S(1)}, f32[4,32,128]{2,1,0:T(8,128)S(1)}, u32[]{:S(2)}, u32[]{:S(2)}) collective-permute-start(f32[4,32,128]{2,1,0:T(8,128)S(1)} %get-tuple-element.82), channel_id=1, source_target_pairs={{0,1},{1,0},{2,3},{3,2},{4,5},{5,4},{6,7},{7,6},{8,9},{9,8},{10,11... | collective-permute-start | bytes 196616 | tf_op jit(solution)/shard_map/ppermute | solution.py:895
  17.5 4.0 %collective-permute-start.8 = (f32[2,32,128]{2,1,0:T(8,128)S(1)}, f32[2,32,128]{2,1,0:T(8,128)S(1)}, u32[]{:S(2)}, u32[]{:S(2)}) collective-permute-start(f32[2,32,128]{2,1,0:T(8,128)S(1)} %get-tuple-element.84), channel_id=1, source_target_pairs={{0,4},{1,3},{2,6},{3,1},{4,0},{5,7},{6,2},{7,5},{8,12},{9,11},{10,... | collective-permute-start | bytes 98312 | tf_op jit(solution)/shard_map/ppermute | solution.py:899
  18.1 4.1 %collective-permute-start.9 = (f32[2,32,128]{2,1,0:T(8,128)S(1)}, f32[2,32,128]{2,1,0:T(8,128)S(1)}, u32[]{:S(2)}, u32[]{:S(2)}) collective-permute-start(f32[2,32,128]{2,1,0:T(8,128)S(1)} %get-tuple-element.85), channel_id=1, source_target_pairs={{0,2},{1,5},{2,0},{3,7},{4,6},{5,1},{6,4},{7,3},{8,10},{9,13},{10,... | collective-permute-start | bytes 98312 | tf_op jit(solution)/shard_map/ppermute | solution.py:899
  19.0 4.8 %collective-permute-start.10 = (f32[2,32,128]{2,1,0:T(8,128)S(1)}, f32[2,32,128]{2,1,0:T(8,128)S(1)}, u32[]{:S(2)}, u32[]{:S(2)}) collective-permute-start(f32[2,32,128]{2,1,0:T(8,128)S(1)} %get-tuple-element.86), channel_id=1, source_target_pairs={{0,6},{1,7},{2,4},{3,5},{4,2},{5,3},{6,0},{7,1},{8,14},{9,15},{10,... | collective-permute-start | bytes 98312 | tf_op jit(solution)/shard_map/ppermute | solution.py:895
  21.1 9.8 %copy-start = (bf16[32,1,128,512]{3,2,1,0:T(8,128)(2,1)S(1)}, bf16[32,1,128,512]{3,2,1,0:T(8,128)(2,1)}, u32[]{:S(2)}) copy-start(bf16[32,1,128,512]{3,2,1,0:T(8,128)(2,1)} %param.9) | copy-start | bytes 12582916
  23.8 12.0 %collective-permute-start.15 = (f32[1024,128]{1,0:T(8,128)S(1)}, f32[1024,128]{1,0:T(8,128)S(1)}, u32[]{:S(2)}, u32[]{:S(2)}) collective-permute-start(f32[1024,128]{1,0:T(8,128)S(1)} %get-tuple-element.97.packed_ref.refs_4_), channel_id=1, source_target_pairs={{0,4},{1,3},{2,6},{3,1},{4,0},{5,7},{6,2},{7,5},{8,12},{9,11},{10,... | collective-permute-start | bytes 1572872 | tf_op jit(solution)/shard_map/ppermute | solution.py:899
  25.5 7.8 %collective-permute-start.12 = (f32[128,128]{1,0:T(8,128)S(1)}, f32[128,128]{1,0:T(8,128)S(1)}, u32[]{:S(2)}, u32[]{:S(2)}) collective-permute-start(f32[128,128]{1,0:T(8,128)S(1)} %to_modes.1.refs_0_), channel_id=1, source_target_pairs={{0,8},{8,0},{16,24},{24,16},{1,9},{9,1},{17,25},{25,17},{2,10},{10... | collective-permute-start | bytes 196616 | tf_op jit(solution)/shard_map/ppermute | solution.py:895
  27.2 6.6 %collective-permute-start.13 = (f32[128,128]{1,0:T(8,128)S(1)}, f32[128,128]{1,0:T(8,128)S(1)}, u32[]{:S(2)}, u32[]{:S(2)}) collective-permute-start(f32[128,128]{1,0:T(8,128)S(1)} %to_modes.1.refs_0_), channel_id=1, source_target_pairs={{0,16},{8,24},{16,0},{24,8},{1,17},{9,25},{17,1},{25,9},{2,18},{10... | collective-permute-start | bytes 196616 | tf_op jit(solution)/shard_map/ppermute | solution.py:895
  29.8 6.1 %collective-permute-start.14 = (f32[128,128]{1,0:T(8,128)S(1)}, f32[128,128]{1,0:T(8,128)S(1)}, u32[]{:S(2)}, u32[]{:S(2)}) collective-permute-start(f32[128,128]{1,0:T(8,128)S(1)} %to_modes.1.refs_0_), channel_id=1, source_target_pairs={{0,24},{8,16},{16,8},{24,0},{1,25},{9,17},{17,9},{25,1},{2,26},{10... | collective-permute-start | bytes 196616 | tf_op jit(solution)/shard_map/ppermute | solution.py:895
  30.0 15.5 %collective-permute-start.17 = (f32[1024,128]{1,0:T(8,128)S(1)}, f32[1024,128]{1,0:T(8,128)S(1)}, u32[]{:S(2)}, u32[]{:S(2)}) collective-permute-start(f32[1024,128]{1,0:T(8,128)S(1)} %collective-permute-done.11.refs_5_), channel_id=1, source_target_pairs={{0,4},{1,3},{2,6},{3,1},{4,0},{5,7},{6,2},{7,5},{8,12},{9,11},{10,... | collective-permute-start | bytes 1572872 | tf_op jit(solution)/shard_map/ppermute | solution.py:899
  30.8 6.4 %copy-start.1 = (bf16[32,1,128,512]{3,2,1,0:T(8,128)(2,1)S(1)}, bf16[32,1,128,512]{3,2,1,0:T(8,128)(2,1)}, u32[]{:S(2)}) copy-start(bf16[32,1,128,512]{3,2,1,0:T(8,128)(2,1)} %param.10) | copy-start | bytes 12582916
  35.8 9.7 %collective-permute-start.16 = (f32[1024,128]{1,0:T(8,128)S(1)}, f32[1024,128]{1,0:T(8,128)S(1)}, u32[]{:S(2)}, u32[]{:S(2)}) collective-permute-start(f32[1024,128]{1,0:T(8,128)S(1)} %collective-permute-done.15.refs_0_), channel_id=1, source_target_pairs={{0,2},{1,5},{2,0},{3,7},{4,6},{5,1},{6,4},{7,3},{8,10},{9,13},{10,... | collective-permute-start | bytes 1572872 | tf_op jit(solution)/shard_map/ppermute | solution.py:899
  45.7 9.3 %collective-permute-start.21 = (f32[3072,128]{1,0:T(8,128)S(1)}, f32[3072,128]{1,0:T(8,128)S(1)}, u32[]{:S(2)}, u32[]{:S(2)}) collective-permute-start(f32[3072,128]{1,0:T(8,128)S(1)} %join.1.refs_6_), channel_id=1, source_target_pairs={{0,1},{1,0},{2,3},{3,2},{4,5},{5,4},{6,7},{7,6},{8,9},{9,8},{10,11... | collective-permute-start | bytes 4718600 | tf_op jit(solution)/shard_map/ppermute | solution.py:895
  45.7 8.0 %collective-permute-start.18 = (f32[128,128]{1,0:T(8,128)S(1)}, f32[128,128]{1,0:T(8,128)S(1)}, u32[]{:S(2)}, u32[]{:S(2)}) collective-permute-start(f32[128,128]{1,0:T(8,128)S(1)} %get-tuple-element.118), channel_id=1, source_target_pairs={{0,8},{8,0},{16,24},{24,16},{1,9},{9,1},{17,25},{25,17},{2,10},{10... | collective-permute-start | bytes 196616 | tf_op jit(solution)/shard_map/ppermute | solution.py:895
  45.9 7.9 %collective-permute-start.19 = (f32[128,128]{1,0:T(8,128)S(1)}, f32[128,128]{1,0:T(8,128)S(1)}, u32[]{:S(2)}, u32[]{:S(2)}) collective-permute-start(f32[128,128]{1,0:T(8,128)S(1)} %get-tuple-element.119), channel_id=1, source_target_pairs={{0,16},{8,24},{16,0},{24,8},{1,17},{9,25},{17,1},{25,9},{2,18},{10... | collective-permute-start | bytes 196616 | tf_op jit(solution)/shard_map/ppermute | solution.py:895
  48.9 6.1 %collective-permute-start.20 = (f32[128,128]{1,0:T(8,128)S(1)}, f32[128,128]{1,0:T(8,128)S(1)}, u32[]{:S(2)}, u32[]{:S(2)}) collective-permute-start(f32[128,128]{1,0:T(8,128)S(1)} %get-tuple-element.120), channel_id=1, source_target_pairs={{0,24},{8,16},{16,8},{24,0},{1,25},{9,17},{17,9},{25,1},{2,26},{10... | collective-permute-start | bytes 196616 | tf_op jit(solution)/shard_map/ppermute | solution.py:895
  56.4 4.5 %collective-permute-start.25 = (f32[4,32,128]{2,1,0:T(8,128)S(1)}, f32[4,32,128]{2,1,0:T(8,128)S(1)}, u32[]{:S(2)}, u32[]{:S(2)}) collective-permute-start(f32[4,32,128]{2,1,0:T(8,128)S(1)} %get-tuple-element.137), channel_id=1, source_target_pairs={{0,1},{1,0},{2,3},{3,2},{4,5},{5,4},{6,7},{7,6},{8,9},{9,8},{10,11... | collective-permute-start | bytes 196616 | tf_op jit(solution)/shard_map/ppermute | solution.py:895
  56.5 6.7 %collective-permute-start.22 = (f32[128,128]{1,0:T(8,128)S(1)}, f32[128,128]{1,0:T(8,128)S(1)}, u32[]{:S(2)}, u32[]{:S(2)}) collective-permute-start(f32[128,128]{1,0:T(8,128)S(1)} %get-tuple-element.133.refs_0_), channel_id=1, source_target_pairs={{0,8},{8,0},{16,24},{24,16},{1,9},{9,1},{17,25},{25,17},{2,10},{10... | collective-permute-start | bytes 196616 | tf_op jit(solution)/shard_map/ppermute | solution.py:895
  57.7 8.4 %collective-permute-start.23 = (f32[128,128]{1,0:T(8,128)S(1)}, f32[128,128]{1,0:T(8,128)S(1)}, u32[]{:S(2)}, u32[]{:S(2)}) collective-permute-start(f32[128,128]{1,0:T(8,128)S(1)} %get-tuple-element.133.refs_0_), channel_id=1, source_target_pairs={{0,16},{8,24},{16,0},{24,8},{1,17},{9,25},{17,1},{25,9},{2,18},{10... | collective-permute-start | bytes 196616 | tf_op jit(solution)/shard_map/ppermute | solution.py:895
  59.1 7.0 %collective-permute-start.24 = (f32[128,128]{1,0:T(8,128)S(1)}, f32[128,128]{1,0:T(8,128)S(1)}, u32[]{:S(2)}, u32[]{:S(2)}) collective-permute-start(f32[128,128]{1,0:T(8,128)S(1)} %get-tuple-element.133.refs_0_), channel_id=1, source_target_pairs={{0,24},{8,16},{16,8},{24,0},{1,25},{9,17},{17,9},{25,1},{2,26},{10... | collective-permute-start | bytes 196616 | tf_op jit(solution)/shard_map/ppermute | solution.py:895
  61.0 9.4 %collective-permute-start.26 = (f32[2,32,128]{2,1,0:T(8,128)S(1)}, f32[2,32,128]{2,1,0:T(8,128)S(1)}, u32[]{:S(2)}, u32[]{:S(2)}) collective-permute-start(f32[2,32,128]{2,1,0:T(8,128)S(1)} %get-tuple-element.139), channel_id=1, source_target_pairs={{0,4},{1,3},{2,6},{3,1},{4,0},{5,7},{6,2},{7,5},{8,12},{9,11},{10,... | collective-permute-start | bytes 98312 | tf_op jit(solution)/shard_map/ppermute | solution.py:899
  62.0 8.4 %collective-permute-start.27 = (f32[2,32,128]{2,1,0:T(8,128)S(1)}, f32[2,32,128]{2,1,0:T(8,128)S(1)}, u32[]{:S(2)}, u32[]{:S(2)}) collective-permute-start(f32[2,32,128]{2,1,0:T(8,128)S(1)} %get-tuple-element.140), channel_id=1, source_target_pairs={{0,2},{1,5},{2,0},{3,7},{4,6},{5,1},{6,4},{7,3},{8,10},{9,13},{10,... | collective-permute-start | bytes 98312 | tf_op jit(solution)/shard_map/ppermute | solution.py:899
  63.2 7.2 %collective-permute-start.28 = (f32[2,32,128]{2,1,0:T(8,128)S(1)}, f32[2,32,128]{2,1,0:T(8,128)S(1)}, u32[]{:S(2)}, u32[]{:S(2)}) collective-permute-start(f32[2,32,128]{2,1,0:T(8,128)S(1)} %get-tuple-element.141), channel_id=1, source_target_pairs={{0,6},{1,7},{2,4},{3,5},{4,2},{5,3},{6,0},{7,1},{8,14},{9,15},{10,... | collective-permute-start | bytes 98312 | tf_op jit(solution)/shard_map/ppermute | solution.py:895
